TPU v7x, 32 devices: a whole 2x2x4 slice. The times are simulated.
32 devices in a mesh: seq: 4 (over x, core), expert: 8 (over z, y).
Axes of the slice: x: 2, y: 2, z: 4, core: 2. Of those that a mesh axis runs over, the one named last changes fastest.
Arguments:
- queries: bfloat16 [2, 1024, 2048], P(None, 'seq', 'expert'), may hold values from -6 to 6
- key_rows: bfloat16 [2, 1024, 2048], P(None, 'seq', 'expert'), may hold values from -6 to 6
- value_rows: bfloat16 [2, 1024, 2048], P(None, 'seq', 'expert'), may hold values from -6 to 6
- decay_rate: float32 [16], P('expert'), as said below
- norm_gain: float32 [2048], P('expert'), may hold values from 0.1 to 1.9
- attn_probe: bfloat16 [2, 1024, 2048], P(None, 'seq', 'expert'), may hold values from -6 to 6
- hidden_in: bfloat16 [2, 1024, 6144], P(None, ('seq', 'expert')), may hold values from -6 to 6
- moe_probe: bfloat16 [2, 1024, 6144], P(None, ('seq', 'expert')), may hold values from -6 to 6
- router_weight: bfloat16 [6144, 4], replicated, may hold values from -0.078125 to 0.078125
- routes: int32 [2, 1024, 2], P(None, ('seq', 'expert')), may hold values from 0 to 3, all different within a row; in each aligned block of 32 rows (0 to 31, 32 to 63, ..., all dimensions but the last counted through in order) at most 17 rows name the same one
- gate_weight: bfloat16 [8, 6144, 2304], P('expert', 'seq'), may hold values from -0.078125 to 0.078125
- up_weight: bfloat16 [8, 6144, 2304], P('expert', 'seq'), may hold values from -0.078125 to 0.078125
- down_weight: bfloat16 [8, 6144, 2304], P('expert', 'seq'), may hold values from -0.09375 to 0.09375
- rollout_logprob: float32 [2, 1024], P(None, 'seq'), may hold values from -1 to 0
- trainer_logprob: float32 [2, 1024], P(None, 'seq'), may hold values from -1 to 0
- advantage: float32 [2, 1024], P(None, 'seq'), may hold values from -4 to 4
- clip_low: float32 [1], replicated, may hold values from 0.4 to 0.95
- clip_high: float32 [1], replicated, may hold values from 1.05 to 2.5
Outputs:
- objective: float32 [2, 1024], P(None, 'seq')
- grad_queries: bfloat16 [2, 1024, 2048], P(None, 'seq', 'expert')
- grad_keys: bfloat16 [2, 1024, 2048], P(None, 'seq', 'expert')
- grad_values: bfloat16 [2, 1024, 2048], P(None, 'seq', 'expert')
- grad_hidden: bfloat16 [2, 1024, 6144], P(None, ('seq', 'expert'))
Inputs may be any that keep to these rules, and one draw needn't show every extreme that they name: `routes`: in each rollout, the 32 positions that one device holds in the expert block name no expert more than 17 times; the 2 experts of a token differ. `decay_rate`: positive rates.
All inputs are finite; a program needn't handle non-finite values.
Results may differ from a plain program's by a relative error of at most 0.0045.
The roundings to bfloat16 on the way count: a program that leaves them out, or rounds other values in their place, can miss the bound.
Values may be sent and summed in bfloat16 or wider, within the bound.
No kernel may reach another device: no remote copies, remote signals or barrier semaphores. Data moves between devices by JAX's collectives and lax.ppermute only.
A program may use at most 192 MiB of HBM per device.

v0:
```python
import jax
import jax.numpy as jnp
from jax import lax
from jax.sharding import PartitionSpec as P

highest = lax.Precision.HIGHEST
norm_epsilon = 1e-06


def entering(x, axis, combine, identity, reverse):
    length, here = (lax.axis_size(axis), lax.axis_index(axis))
    everything = jax.tree.map(lambda part: lax.all_gather(part, axis), x)
    start = jax.tree.map(
        lambda part, zero: jnp.broadcast_to(jnp.asarray(zero, part.dtype), part.shape), x, identity
    )

    def lap(k, before):
        at = length - 1 - k if reverse else k
        reached = at > here if reverse else at < here
        new = combine(before, jax.tree.map(lambda part: part[at], everything))
        return jax.tree.map(lambda a, b: jnp.where(reached, a, b), new, before)

    return lax.fori_loop(0, length, lap, start)


def carry_combine(earlier, later):
    return (earlier[0] * later[0], later[0] * earlier[1] + later[1])


def earlier_state(summary, block_decay):
    identity = (jnp.ones_like(block_decay), jnp.zeros_like(summary))
    result = entering((block_decay, summary), "seq", carry_combine, identity, False)
    return result[1]


def later_state(summary, block_decay):
    identity = (jnp.ones_like(block_decay), jnp.zeros_like(summary))
    result = entering((block_decay, summary), "seq", carry_combine, identity, True)
    return result[1]


def on_device(
    queries,
    key_rows,
    value_rows,
    decay_rate,
    norm_gain,
    attn_probe,
    hidden_in,
    moe_probe,
    router_weight,
    routes,
    gate_weight,
    up_weight,
    down_weight,
    rollout_logprob,
    trainer_logprob,
    advantage,
    clip_low,
    clip_high,
):
    rollouts, block_size, feature_width = queries.shape
    head_count = decay_rate.shape[0]
    head_size = feature_width // head_count
    importance = jnp.exp(trainer_logprob - rollout_logprob)
    clipped = jnp.minimum(jnp.maximum(importance, clip_low[0]), clip_high[0])
    coeff = -(clipped * advantage) / rollouts
    objective = coeff * trainer_logprob
    gate_block, up_block, down_block = (
        lax.all_gather(gate_weight, "seq", axis=1, tiled=True),
        lax.all_gather(up_weight, "seq", axis=1, tiled=True),
        lax.all_gather(down_weight, "seq", axis=1, tiled=True),
    )
    gate_mat = gate_block[0]
    up_mat = up_block[0]
    down_mat = down_block[0]
    shape_four = (rollouts, block_size, head_count, head_size)
    query_full = queries.reshape(shape_four).astype(jnp.float32)
    key_full = key_rows.reshape(shape_four).astype(jnp.float32)
    value_full = value_rows.reshape(shape_four).astype(jnp.float32)
    probe_full = attn_probe.reshape(shape_four).astype(jnp.float32)
    gain_full = norm_gain.reshape(head_count, head_size)
    offsets = jnp.arange(block_size, dtype=jnp.float32)
    rate_row = decay_rate[None, :]
    distance = offsets[:, None] - offsets[None, :]
    within = jnp.where(
        (distance >= 0)[None],
        jnp.exp(-decay_rate[:, None, None] * jnp.maximum(distance, 0.0)[None]),
        0.0,
    )
    lead_decay = jnp.exp(-rate_row * (offsets[:, None] + 1.0))[None, :, :, None]
    key_tail = jnp.exp(-rate_row * (block_size - 1.0 - offsets[:, None]))[None, :, :, None]
    query_tail = jnp.exp(-rate_row * offsets[:, None])[None, :, :, None]
    grad_tail = jnp.exp(-rate_row * (block_size - offsets[:, None]))[None, :, :, None]
    block_decay = jnp.exp(-decay_rate * block_size).reshape(1, head_count, 1, 1)
    forward_summary = jnp.einsum(
        "rjhk,rjhv->rhkv", key_full * key_tail, value_full, precision=highest
    )
    state_before = earlier_state(forward_summary, block_decay)
    scores = jnp.einsum("rihc,rjhc->rhij", query_full, key_full, precision=highest) * within[None]
    output = jnp.einsum("rhij,rjhv->rihv", scores, value_full, precision=highest)
    output = output + lead_decay * jnp.einsum(
        "rihk,rhkv->rihv", query_full, state_before, precision=highest
    )
    inverse = lax.rsqrt(jnp.mean(output * output, axis=-1, keepdims=True) + norm_epsilon)
    scaled = gain_full[None, None] * (coeff[:, :, None, None] * probe_full)
    grad_out = inverse * scaled - output * inverse**3 * jnp.mean(
        scaled * output, axis=-1, keepdims=True
    )
    backward_summary = jnp.einsum(
        "rihk,rihv->rhkv", query_full * query_tail, grad_out, precision=highest
    )
    state_after = later_state(backward_summary, block_decay)
    product = jnp.einsum("rihv,rjhv->rhij", grad_out, value_full, precision=highest) * within[None]
    grad_query = jnp.einsum("rhij,rjhk->rihk", product, key_full, precision=highest)
    grad_query = grad_query + lead_decay * jnp.einsum(
        "rihv,rhkv->rihk", grad_out, state_before, precision=highest
    )
    grad_key = jnp.einsum("rhij,rihk->rjhk", product, query_full, precision=highest)
    grad_key = grad_key + grad_tail * jnp.einsum(
        "rjhv,rhkv->rjhk", value_full, state_after, precision=highest
    )
    grad_value = jnp.einsum("rhij,rihv->rjhv", scores, grad_out, precision=highest)
    grad_value = grad_value + grad_tail * jnp.einsum(
        "rjhk,rhkv->rjhv", key_full, state_after, precision=highest
    )
    out_shape = (rollouts, block_size, feature_width)
    grad_queries = grad_query.reshape(out_shape).astype(jnp.bfloat16)
    grad_keys = grad_key.reshape(out_shape).astype(jnp.bfloat16)
    grad_values = grad_value.reshape(out_shape).astype(jnp.bfloat16)
    expert_count = lax.axis_size("expert")
    expert_index = lax.axis_index("expert")
    window_experts = router_weight.shape[1]
    slice_count = expert_count // window_experts
    positions = hidden_in.shape[1]
    top_count = routes.shape[2]
    model_width = hidden_in.shape[2]
    capacity = positions // 2 + 1
    local_coeff = lax.dynamic_slice_in_dim(coeff, expert_index * positions, positions, 1)
    grad_rows = (local_coeff[:, :, None] * moe_probe.astype(jnp.float32)).astype(jnp.bfloat16)
    onehot = (routes[..., None] == jnp.arange(window_experts, dtype=jnp.int32)).astype(jnp.float32)
    flat_hot = onehot.reshape(rollouts, positions * top_count, window_experts)
    earlier_count = jnp.cumsum(flat_hot, axis=1) - flat_hot
    slot_rank = jnp.sum(earlier_count * flat_hot, axis=-1)
    slot_hot = (slot_rank[..., None] == jnp.arange(capacity, dtype=jnp.float32)).astype(jnp.float32)
    select = (
        (flat_hot[..., None] * slot_hot[:, :, None, :])
        .reshape(rollouts, positions, top_count, window_experts, capacity)
        .sum(axis=2)
    )
    select_half = select.astype(jnp.bfloat16)
    token_buffer = jnp.einsum(
        "rpem,rpd->ermd", select_half, hidden_in, preferred_element_type=jnp.float32
    ).astype(jnp.bfloat16)
    grad_buffer = jnp.einsum(
        "rpem,rpd->ermd", select_half, grad_rows, preferred_element_type=jnp.float32
    ).astype(jnp.bfloat16)

    def spread(buffer):
        wide = jnp.broadcast_to(
            buffer[:, None], (window_experts, slice_count, rollouts, capacity, model_width)
        )
        return wide.reshape(window_experts * slice_count, rollouts * capacity, model_width)

    token_part = lax.all_to_all(
        spread(token_buffer), "expert", split_axis=0, concat_axis=0, tiled=True
    )
    grad_part = lax.all_to_all(
        spread(grad_buffer), "expert", split_axis=0, concat_axis=0, tiled=True
    )
    sources, item_count, feature_count = token_part.shape
    token_flat = token_part.reshape(sources * item_count, feature_count)
    grad_flat = grad_part.reshape(sources * item_count, feature_count)
    pre_gate = jnp.dot(token_flat, gate_mat, preferred_element_type=jnp.float32)
    pre_up = jnp.dot(token_flat, up_mat, preferred_element_type=jnp.float32)
    sigmoid_gate = jax.nn.sigmoid(pre_gate)
    activated = pre_gate * sigmoid_gate
    units = activated * pre_up
    unit_grad = jnp.dot(grad_flat, down_mat, preferred_element_type=jnp.float32)
    slice_score = jnp.sum(units * unit_grad, axis=-1).astype(jnp.bfloat16)
    up_grad = (unit_grad * activated).astype(jnp.bfloat16)
    gate_grad = (
        unit_grad * pre_up * sigmoid_gate * (1.0 + pre_gate * (1.0 - sigmoid_gate))
    ).astype(jnp.bfloat16)
    contract = (((1,), (1,)), ((), ()))
    slice_dx = lax.dot_general(gate_grad, gate_mat, contract, preferred_element_type=jnp.float32)
    slice_dx = slice_dx + lax.dot_general(
        up_grad, up_mat, contract, preferred_element_type=jnp.float32
    )
    slice_dx = slice_dx.astype(jnp.bfloat16).reshape(sources, item_count, feature_count)
    returned_dx = lax.all_to_all(slice_dx, "expert", split_axis=0, concat_axis=0, tiled=True)
    returned_score = lax.all_to_all(
        slice_score.reshape(sources, item_count), "expert", split_axis=0, concat_axis=0, tiled=True
    )
    part_dx = (
        returned_dx.astype(jnp.float32)
        .reshape(window_experts, slice_count, rollouts, capacity, model_width)
        .sum(axis=1)
    )
    part_score = (
        returned_score.astype(jnp.float32)
        .reshape(window_experts, slice_count, rollouts, capacity)
        .sum(axis=1)
    )
    row_dx = jnp.einsum("rpem,ermd->rped", select, part_dx, precision=highest)
    row_score = jnp.einsum("rpem,erm->rpe", select, part_score, precision=highest)
    logits = jnp.einsum("rpd,de->rpe", hidden_in, router_weight, preferred_element_type=jnp.float32)
    chosen = jnp.einsum("rpke,rpe->rpk", onehot, logits, precision=highest)
    exponent = jnp.exp(chosen)
    gates = exponent / jnp.sum(exponent, axis=-1, keepdims=True)
    gate_expert = jnp.einsum("rpk,rpke->rpe", gates, onehot, precision=highest)
    score_pick = jnp.einsum("rpke,rpe->rpk", onehot, row_score, precision=highest)
    score_mean = jnp.sum(gates * score_pick, axis=-1, keepdims=True)
    logit_grad = gates * (score_pick - score_mean)
    logit_expert = jnp.einsum("rpk,rpke->rpe", logit_grad, onehot, precision=highest)
    grad_hidden = jnp.einsum("rpe,rped->rpd", gate_expert, row_dx, precision=highest)
    grad_hidden = grad_hidden + jnp.einsum(
        "rpe,de->rpd", logit_expert, router_weight.astype(jnp.float32), precision=highest
    )
    return (objective, grad_queries, grad_keys, grad_values, grad_hidden.astype(jnp.bfloat16))


def solution(mesh):
    in_specs = (
        P(None, "seq", "expert"),
        P(None, "seq", "expert"),
        P(None, "seq", "expert"),
        P("expert"),
        P("expert"),
        P(None, "seq", "expert"),
        P(None, ("seq", "expert"), None),
        P(None, ("seq", "expert"), None),
        P(),
        P(None, ("seq", "expert"), None),
        P("expert", "seq", None),
        P("expert", "seq", None),
        P("expert", "seq", None),
        P(None, "seq"),
        P(None, "seq"),
        P(None, "seq"),
        P(),
        P(),
    )
    out_specs = (
        P(None, "seq"),
        P(None, "seq", "expert"),
        P(None, "seq", "expert"),
        P(None, "seq", "expert"),
        P(None, ("seq", "expert"), None),
    )
    return jax.shard_map(
        on_device, mesh=mesh, in_specs=in_specs, out_specs=out_specs, check_vma=False
    )
```

profile of v0, /device:TPU:0, one launch (start us, length us, event | category | flops | bytes accessed | tf_op | source)
XLA Modules:
  0.0 773.1 jit_solution(16652704851146988830)
XLA Ops:
  20.5 4.4 broadcast_in_dim.18
  24.9 7.7 reshape.272
  32.5 5.7 copy.206
  38.3 7.5 all-to-all-start
  47.9 4.5 broadcast_in_dim.19
  52.4 7.9 %reshape.274 = bf16[8,34,6144]{2,0,1:T(8,128)(2,1)} reshape(bf16[4,2,2,17,6144]{4,1,0,3,2:T(2,128)(2,1)} %broadcast_in_dim.19) | data formatting | bytes 6684672 | tf_op jit(solution)/shard_map/reshape | solution.py:163
  60.3 5.8 copy.209
  66.1 67.3 %all-to-all-done = bf16[8,34,6144]{2,1,0:T(8,128)(2,1)} async-done(((bf16[8,34,6144]{2,1,0:T(8,128)(2,1)}), bf16[8,34,6144]{2,1,0:T(8,128)(2,1)}, u32[]{:S(2)}, u32[]{:S(2)}) %all-to-all-start) | async-done | bytes 3342368 | tf_op jit(solution)/shard_map/all_to_all | solution.py:168
  133.4 4.5 all-to-all-start.1
  137.9 6.4 all-reduce
  146.2 4.4 while.30
  152.6 3.8 reshape.273
  156.5 68.4 %all-to-all-done.1 = bf16[8,34,6144]{2,1,0:T(8,128)(2,1)} async-done(((bf16[8,34,6144]{2,1,0:T(8,128)(2,1)}), bf16[8,34,6144]{2,1,0:T(8,128)(2,1)}, u32[]{:S(2)}, u32[]{:S(2)}) %all-to-all-start.1) | async-done | bytes 3342368 | tf_op jit(solution)/shard_map/all_to_all | solution.py:165
  224.9 5.1 reshape.275
  229.9 17.1 %fusion.4 = f32[272,2304]{1,0:T(8,128)} fusion(bf16[272,6144]{1,0:T(8,128)(2,1)} %reshape.275, bf16[1,6144,2304]{2,1,0:T(8,128)(2,1)} %all-gather.13.cloned.1.call-done), kind=kOutput, calls=%fused_computation.8 | convolution fusion | flops 7700742144 | bytes 34160640 | tf_op jit(solution)/shard_map/dot_general | solution.py:174
  247.0 133.6 %all-gather.11.cloned.1.call-done = bf16[1,6144,2304]{2,1,0:T(8,128)(2,1)} async-done(((bf16[1,1536,2304]{2,1,0:T(8,128)(2,1)}), bf16[1,6144,2304]{2,1,0:T(8,128)(2,1)}) %all-gather.11.cloned.1.call-update) | async-done | bytes 28311568 | tf_op jit(solution)/shard_map/all_gather | solution.py:71
  380.6 17.9 %fusion.8 = f32[272,2304]{1,0:T(8,128)} fusion(bf16[272,6144]{1,0:T(8,128)(2,1)} %reshape.275, bf16[1,6144,2304]{2,1,0:T(8,128)(2,1)} %all-gather.11.cloned.1.call-done), kind=kOutput, calls=%fused_computation.12 | convolution fusion | flops 7700742144 | bytes 34160640 | tf_op jit(solution)/shard_map/dot_general | solution.py:175
  398.5 155.8 %all-gather.9.cloned.1.call-done = bf16[1,6144,2304]{2,1,0:T(8,128)(2,1)} async-done(((bf16[1,1536,2304]{2,1,0:T(8,128)(2,1)}), bf16[1,6144,2304]{2,1,0:T(8,128)(2,1)}) %all-gather.9.cloned.1.call-update) | async-done | bytes 28311568 | tf_op jit(solution)/shard_map/all_gather | solution.py:72
  554.3 17.7 %multiply_reduce_fusion = (bf16[272]{0:T(512)(128)(2,1)S(1)}, f32[272,2304]{1,0:T(8,128)}) fusion(f32[272,2304]{1,0:T(8,128)} %fusion.8, f32[272,2304]{1,0:T(8,128)} %fusion.4, bf16[272,6144]{1,0:T(8,128)(2,1)} %reshape.273, bf16[1,6144,2304]{2,1,0:T(8,128)(2,1)} %all-gather.9.cloned.1.call-done), kind=kOutput, calls=%fused_computation.29 | convolution fusion | flops 7705128448 | bytes 39174688 | tf_op jit(solution)/shard_map/dot_general | solution.py:179
  572.7 5.5 all-to-all-start.3
  578.2 18.7 %fusion.2 = f32[272,6144]{1,0:T(8,128)} fusion(bf16[1,6144,2304]{2,1,0:T(8,128)(2,1)} %all-gather.13.cloned.1.call-done, f32[272,2304]{1,0:T(8,128)} %fusion.4, f32[272,2304]{1,0:T(8,128)} %get-tuple-element.399, f32[272,2304]{1,0:T(8,128)} %fusion.8), kind=kOutput, calls=%fused_computation.6 | convolution fusion | flops 7707009024 | bytes 42516480 | tf_op jit(solution)/shard_map/dot_general | solution.py:186
  596.9 17.7 %fusion.15 = bf16[272,6144]{1,0:T(8,128)(2,1)} fusion(f32[272,6144]{1,0:T(8,128)} %fusion.2, bf16[1,6144,2304]{2,1,0:T(8,128)(2,1)} %all-gather.11.cloned.1.call-done, f32[272,2304]{1,0:T(8,128)} %get-tuple-element.399, f32[272,2304]{1,0:T(8,128)} %fusion.4), kind=kOutput, calls=%fused_computation.18 | convolution fusion | flops 7707844608 | bytes 43352064 | tf_op jit(solution)/shard_map/dot_general | solution.py:187
  614.6 3.8 reshape.276
  618.5 6.1 all-to-all-start.2
  634.7 10.2 %all-gather.17.cloned.1.call-done = f32[8,2,128,128]{3,2,1,0:T(8,128)} async-done(((f32[2,2,128,128]{3,2,1,0:T(8,128)}), f32[8,2,128,128]{3,2,1,0:T(8,128)}) %all-gather.17.cloned.1.call-update) | async-done | bytes 1048592 | tf_op jit(solution)/shard_map/all_gather | solution.py:12
  644.9 6.8 while.31
  657.2 54.9 %all-to-all-done.2 = bf16[8,34,6144]{2,1,0:T(8,128)(2,1)} async-done(((bf16[8,34,6144]{2,1,0:T(8,128)(2,1)}), bf16[8,34,6144]{2,1,0:T(8,128)(2,1)}, u32[]{:S(2)}, u32[]{:S(2)}) %all-to-all-start.2) | async-done | bytes 3342368 | tf_op jit(solution)/shard_map/all_to_all | solution.py:191
  712.1 6.8 copy_convert_fusion
  718.9 8.5 %reshape.281 = f32[4,2,2,17,6144]{4,1,0,3,2:T(2,128)} reshape(f32[8,34,6144]{2,0,1:T(8,128)} %copy_convert_fusion) | data formatting | bytes 13369344 | tf_op jit(solution)/shard_map/reshape | solution.py:197
  727.4 12.3 %reduce_sum.86 = f32[4,2,17,6144]{3,0,2,1:T(4,128)} reduce(f32[4,2,2,17,6144]{4,1,0,3,2:T(2,128)} %reshape.281, f32[]{:T(128)} %constant.92.clone.1), dimensions={1}, to_apply=%region_10.11 | reduce | flops 835584 | bytes 10027012 | tf_op jit(solution)/shard_map/reduce_sum | solution.py:198
  739.6 9.9 %convolution_bitcast_fusion = f32[2,32,4,6144]{3,1,2,0:T(8,128)S(1)} fusion(f32[4,2,17,6144]{3,0,2,1:T(4,128)} %reduce_sum.86, f32[2,32,4,17]{1,2,3,0:T(4,128)S(1)} %multiply_reduce_fusion.3), kind=kOutput, calls=%fused_computation.16 | convolution fusion | flops 320864256 | bytes 9651200 | tf_op jit(solution)/shard_map/rpem,ermd->rped/dot_general | solution.py:205
  749.5 14.7 %fusion.21 = f32[2,32,1,6144]{3,2,1,0:T(1,128)S(1)} fusion(f32[2,32,4,1]{2,3,1,0:T(1,128)S(1)} %copy.236, f32[2,32,4,6144]{3,1,2,0:T(8,128)S(1)} %convolution_bitcast_fusion), kind=kOutput, calls=%fused_computation.25 | convolution fusion | flops 18874368 | bytes 7865344 | tf_op jit(solution)/shard_map/rpe,rped->rpd/dot_general | solution.py:216
  (130 shorter events, 46.3 us)
Async XLA Ops:
  7.2 38.6 %copy-start = (bf16[2,32,6144]{2,1,0:T(8,128)(2,1)S(1)}, bf16[2,32,6144]{2,1,0:T(8,128)(2,1)}, u32[]{:S(2)}) copy-start(bf16[2,32,6144]{2,1,0:T(8,128)(2,1)} %param.28) | copy-start | bytes 2359300
  7.2 139.0 %all-gather.15.cloned.1.call-start = ((), (), s32[]{:S(2)}) async-start(), calls=%async_computation.7 | async-start | bytes 1310720 | tf_op jit(solution)/shard_map/all_gather | solution.py:12
  8.4 5.6 copy-start.5
  13.3 216.7 %all-gather.13.cloned.1.call-start = ((), (), s32[]{:S(2)}) async-start(), calls=%async_computation.6 | async-start | bytes 35389440 | tf_op jit(solution)/shard_map/all_gather | solution.py:70
  14.0 366.6 %all-gather.11.cloned.1.call-start = ((), (), s32[]{:S(2)}) async-start(), calls=%async_computation.5 | async-start | bytes 35389440 | tf_op jit(solution)/shard_map/all_gather | solution.py:71
  14.8 1.9 copy-start.13
  14.8 2.8 copy-start.16
  14.8 2.8 copy-start.17
  14.8 2.8 copy-start.18
  14.8 3.5 copy-start.9
  14.8 539.5 %all-gather.9.cloned.1.call-start = ((), (), s32[]{:S(2)}) async-start(), calls=%async_computation.4 | async-start | bytes 35389440 | tf_op jit(solution)/shard_map/all_gather | solution.py:72
  38.3 95.1 %all-to-all-start = ((bf16[8,34,6144]{2,1,0:T(8,128)(2,1)}), bf16[8,34,6144]{2,1,0:T(8,128)(2,1)}, u32[]{:S(2)}, u32[]{:S(2)}) async-start(bf16[8,34,6144]{2,1,0:T(8,128)(2,1)} %copy.206), calls=%async_computation | async-start | bytes 7864320 | tf_op jit(solution)/shard_map/all_to_all | solution.py:168
  66.1 78.3 %copy-start.11 = (bf16[2,256,256]{2,1,0:T(8,128)(2,1)S(1)}, bf16[2,256,256]{2,1,0:T(8,128)(2,1)}, u32[]{:S(2)}) copy-start(bf16[2,256,256]{2,1,0:T(8,128)(2,1)} %param.22) | copy-start | bytes 786436
  66.1 78.5 %copy-start.10 = (bf16[2,256,256]{2,1,0:T(8,128)(2,1)S(1)}, bf16[2,256,256]{2,1,0:T(8,128)(2,1)}, u32[]{:S(2)}) copy-start(bf16[2,256,256]{2,1,0:T(8,128)(2,1)} %param.27) | copy-start | bytes 786436
  66.1 79.8 %copy-start.7 = (bf16[2,256,256]{2,1,0:T(8,128)(2,1)S(1)}, bf16[2,256,256]{2,1,0:T(8,128)(2,1)}, u32[]{:S(2)}) copy-start(bf16[2,256,256]{2,1,0:T(8,128)(2,1)} %param.23) | copy-start | bytes 786436
  133.4 91.5 %all-to-all-start.1 = ((bf16[8,34,6144]{2,1,0:T(8,128)(2,1)}), bf16[8,34,6144]{2,1,0:T(8,128)(2,1)}, u32[]{:S(2)}, u32[]{:S(2)}) async-start(bf16[8,34,6144]{2,1,0:T(8,128)(2,1)} %copy.209), calls=%async_computation.1 | async-start | bytes 7864320 | tf_op jit(solution)/shard_map/all_to_all | solution.py:165
  144.7 6.3 copy-start.2
  145.0 0.8 copy-start.3
  145.8 5.2 copy-start.4
  145.8 5.2 copy-start.14
  150.6 5.9 copy-start.15
  572.7 45.8 %all-to-all-start.3 = ((bf16[8,1,34]{2,1,0:T(2,128)(2,1)}), bf16[8,1,34]{2,1,0:T(2,128)(2,1)S(1)}, u32[]{:S(2)}, u32[]{:S(2)}) async-start(bf16[8,1,34]{2,1,0:T(2,128)(2,1)} %convert_element_type.138), calls=%async_computation.3 | async-start | bytes 8192 | tf_op jit(solution)/shard_map/all_to_all | solution.py:192
  618.5 9.1 %copy-start.12 = (bf16[6144,4]{0,1:T(4,128)(2,1)S(1)}, bf16[6144,4]{0,1:T(4,128)(2,1)}, u32[]{:S(2)}) copy-start(bf16[6144,4]{0,1:T(4,128)(2,1)} %param.30) | copy-start | bytes 147460
  618.5 93.6 %all-to-all-start.2 = ((bf16[8,34,6144]{2,1,0:T(8,128)(2,1)}), bf16[8,34,6144]{2,1,0:T(8,128)(2,1)}, u32[]{:S(2)}, u32[]{:S(2)}) async-start(bf16[8,34,6144]{2,1,0:T(8,128)(2,1)} %reshape.276), calls=%async_computation.2 | async-start | bytes 7864320 | tf_op jit(solution)/shard_map/all_to_all | solution.py:191
  624.6 20.3 %all-gather.17.cloned.1.call-start = ((), (), s32[]{:S(2)}) async-start(), calls=%async_computation.8 | async-start | bytes 1310720 | tf_op jit(solution)/shard_map/all_gather | solution.py:12
  627.6 3.9 copy-start.6
  630.5 1.0 copy-start.1
  631.5 20.2 %copy-start.8 = (bf16[2,256,256]{2,1,0:T(8,128)(2,1)S(1)}, bf16[2,256,256]{2,1,0:T(8,128)(2,1)}, u32[]{:S(2)}) copy-start(bf16[2,256,256]{2,1,0:T(8,128)(2,1)} %param.23) | copy-start | bytes 786436
Sparse Core Ops, SparseCore 0:
  13.4 19.4 all-gather.14
  34.4 172.3 all-gather.12
  208.4 172.1 all-gather.10
  382.1 172.1 all-gather.8
  627.7 17.1 all-gather.16
where the time goes:
time: 780 us; the launch traced here: 773 us
  waiting for transfers between devices  492 us (63%)
  matrix products  131 us (17%)
  local copies, waits for them, and re-layouts  71.8 us (9%)
  other arithmetic  31.1 us (4%)
  starting transfers between devices  24.1 us (3%)
  between operations  16.5 us (2%)
    all_gather x1, waiting for transfers between devices, on_device(): lax.all_gather(down_weight, 'seq', axis=1, tiled=True)  156 us
    all_gather x1, waiting for transfers between devices, on_device(): lax.all_gather(up_weight, 'seq', axis=1, tiled=True)  134 us
    all_to_all x1, waiting for transfers between devices, on_device(): lax.all_to_all(spread(token_buffer), 'expert', split_axis=0, concat_axis=...  68.4 us
    all_to_all x1, waiting for transfers between devices, on_device(): lax.all_to_all(spread(grad_buffer), 'expert', split_axis=0, concat_axis=0...  67.3 us
    all_to_all x1, waiting for transfers between devices, on_device(): lax.all_to_all(slice_dx, 'expert', split_axis=0, concat_axis=0, tiled=True)  54.9 us
    reshape x4, local copies, waits for them, and re-layouts, spread(): wide.reshape(window_experts * slice_count, rollouts * capacity, model_width)  27.1 us
    dot_general x1, matrix products, on_device(): lax.dot_general(gate_grad, gate_mat, contract, preferred_element_type=jnp...  18.7 us
    dot_general x1, matrix products, on_device(): pre_up = jnp.dot(token_flat, up_mat, preferred_element_type=jnp.float32)  17.9 us
  transfers between devices with their start and end apart: 9, of which 6 were waited for; matrix products, arithmetic and copies ran while one was open for 20% of the time, Pallas kernels for 0%

commit v1 on v0

v1 whole, which is shorter than its diff:
```python
import jax
import jax.numpy as jnp
from jax import lax
from jax.experimental import pallas as pl
from jax.experimental.pallas import tpu as pltpu
from jax.sharding import PartitionSpec as P

highest = lax.Precision.HIGHEST
norm_epsilon = 1e-06
f32 = jnp.float32
bf16 = jnp.bfloat16
vmem_limit = 48 * 2**20

in_scale = 32.0
out_scale = 4.0


class Layout:
    def __init__(self, window_experts):
        self.seq = lax.axis_size("seq")
        self.chips = self.seq // 2
        self.spread = lax.axis_size("expert")
        self.experts = window_experts
        self.slices = self.spread // window_experts
        here = lax.axis_index("seq")
        self.chip, self.core = here // 2, here % 2
        self.expert = lax.axis_index("expert") // self.slices

    def swap_core(self, v):
        return lax.ppermute(v, "seq", [(i, i ^ 1) for i in range(self.seq)])

    def turn_chip(self, v, p):
        n = self.chips
        return lax.ppermute(
            v, "seq", [(i, ((i // 2 + p) % n) * 2 + i % 2) for i in range(self.seq)]
        )

    def later_chip(self, v, p):
        pairs = [(i, i + 2 * p) for i in range(self.seq) if 0 <= i + 2 * p < self.seq]
        return lax.ppermute(v, "seq", pairs)

    def turn_expert(self, v, d):
        n, m = self.experts, self.slices
        return lax.ppermute(
            v, "expert", [(i, ((i // m + d) % n) * m + i % m) for i in range(self.spread)]
        )

    def turn_slice(self, v, k):
        m = self.slices
        return lax.ppermute(
            v, "expert", [(i, (i // m) * m + (i % m + k) % m) for i in range(self.spread)]
        )


def params(**kw):
    return pltpu.CompilerParams(vmem_limit_bytes=vmem_limit, **kw)


def cost(flops, moved):
    return pl.CostEstimate(flops=int(flops), bytes_accessed=int(moved), transcendentals=0)


def pick_rows(groups, rank, first, count, padded):
    experts = rank.shape[0]
    halves, tokens, width = groups[0].shape
    total = tokens * len(groups)

    def body(rank_ref, *refs):
        group_refs, out_refs = refs[: len(groups)], refs[len(groups) :]
        slot = lax.broadcasted_iota(jnp.int32, (padded, total), 0)
        wanted = jnp.where(slot < count, slot + first, -2)
        for h in range(halves):
            rows = jnp.concatenate([g[h] for g in group_refs], axis=0)
            for d in range(experts):
                pick = (rank_ref[d : d + 1, :] == wanted).astype(bf16)
                out_refs[d][h] = jnp.dot(pick, rows, preferred_element_type=f32).astype(bf16)

    shape = jax.ShapeDtypeStruct((halves, padded, width), bf16)
    return pl.pallas_call(
        body,
        out_shape=[shape] * experts,
        compiler_params=params(),
        cost_estimate=cost(
            2 * experts * halves * padded * total * width,
            2 * halves * width * (total + experts * padded),
        ),
        name="pick_rows",
    )(rank, *groups)


def project(blocks, rows, mats, chip, chips):
    halves, padded, width = blocks[0].shape
    count = len(blocks)
    total = rows * count
    part = total // chips
    per_part = count // chips
    units = mats[0].shape[1]
    tile = 256 if units % 256 == 0 else units

    def body(chip_ref, *refs):
        block_refs = refs[:count]
        own_ref, other_ref, keep_ref, send_ref, held = refs[count:]

        @pl.when(pl.program_id(0) == 0)
        def _():
            column = lax.broadcasted_iota(jnp.int32, (1, count * padded), 1)
            target = jnp.full((1, count * padded), -1, jnp.int32)
            for b in range(count):
                place = (b // per_part - chip_ref[0] + chips) % chips
                start = place * part + (b % per_part) * rows
                inside = (column >= b * padded) & (column < b * padded + rows)
                target = jnp.where(inside, column - b * padded + start, target)
            line = lax.broadcasted_iota(jnp.int32, (total, count * padded), 0)
            pick = (line == target).astype(bf16)
            for h in range(halves):
                every = jnp.concatenate([b[h] for b in block_refs], axis=0)
                held[h] = jnp.dot(pick, every, preferred_element_type=f32).astype(bf16)

        result = jnp.dot(held[0], own_ref[...], preferred_element_type=f32)
        result = result + jnp.dot(held[1], other_ref[...], preferred_element_type=f32)
        keep_ref[...] = result[:part]
        for p in range(1, chips):
            send_ref[p - 1] = result[p * part : (p + 1) * part]

    mat_spec = pl.BlockSpec((width, tile), lambda i: (0, i))
    return pl.pallas_call(
        body,
        grid=(units // tile,),
        in_specs=[pl.BlockSpec(memory_space=pltpu.SMEM)]
        + [pl.BlockSpec((halves, padded, width), lambda i: (0, 0, 0))] * count
        + [mat_spec, mat_spec],
        out_specs=[
            pl.BlockSpec((part, tile), lambda i: (0, i)),
            pl.BlockSpec((chips - 1, part, tile), lambda i: (0, 0, i)),
        ],
        out_shape=[
            jax.ShapeDtypeStruct((part, units), f32),
            jax.ShapeDtypeStruct((chips - 1, part, units), f32),
        ],
        scratch_shapes=[pltpu.VMEM((halves, total, width), bf16)],
        compiler_params=params(),
        cost_estimate=cost(
            2 * halves * total * width * units, 2 * halves * width * units + 4 * total * units
        ),
        name="project",
    )(chip, *blocks, *mats)


def project_back(gate_parts, up_parts, gate_mat, up_mat):
    chips = len(gate_parts)
    part, units = gate_parts[0].shape
    width = gate_mat.shape[0]
    tile = 256 if width % 256 == 0 else width
    total = part * chips

    def body(*refs):
        gate_refs, up_refs = refs[:chips], refs[chips : 2 * chips]
        gate_mat_ref, up_mat_ref, out_ref, gate_all, up_all = refs[2 * chips :]

        @pl.when(pl.program_id(0) == 0)
        def _():
            for r in range(chips):
                gate_all[r * part : (r + 1) * part] = gate_refs[r][...]
                up_all[r * part : (r + 1) * part] = up_refs[r][...]

        contract = (((1,), (1,)), ((), ()))
        result = lax.dot_general(
            gate_all[...], gate_mat_ref[...], contract, preferred_element_type=f32
        )
        result = result + lax.dot_general(
            up_all[...], up_mat_ref[...], contract, preferred_element_type=f32
        )
        for r in range(chips):
            out_ref[r] = result[r * part : (r + 1) * part].astype(bf16)

    part_spec = pl.BlockSpec((part, units), lambda i: (0, 0))
    mat_spec = pl.BlockSpec((tile, units), lambda i: (i, 0))
    return pl.pallas_call(
        body,
        grid=(width // tile,),
        in_specs=[part_spec] * (2 * chips) + [mat_spec, mat_spec],
        out_specs=pl.BlockSpec((chips, part, tile), lambda i: (0, 0, i)),
        out_shape=jax.ShapeDtypeStruct((chips, part, width), bf16),
        scratch_shapes=[pltpu.VMEM((total, units), bf16)] * 2,
        compiler_params=params(),
        cost_estimate=cost(4 * total * width * units, 4 * width * units + 2 * total * width),
        name="project_back",
    )(*gate_parts, *up_parts, gate_mat, up_mat)


def combine(returned, scores, rank, gates, router, firsts, groups):
    chunk_count, experts = len(returned), len(returned[0])
    width = returned[0][0].shape[1]
    total = rank.shape[0]
    tokens = total // groups
    flat = [v for chunk in returned for v in chunk]

    def body(*refs):
        flat_refs = refs[: len(flat)]
        score_ref, rank_ref, gate_ref, router_ref = refs[len(flat) : len(flat) + 4]
        out_refs = refs[len(flat) + 4 :]
        acc = jnp.zeros((total, width), f32)
        picked = []
        slots = lax.broadcasted_iota(jnp.int32, (total, score_ref.shape[1]), 1)
        for d in range(experts):
            hit = rank_ref[:, d : d + 1] == slots
            picked.append(
                jnp.sum(jnp.where(hit, score_ref[d : d + 1, :], 0.0), axis=1, keepdims=True)
            )
        mean = sum(gate_ref[:, d : d + 1] * picked[d] for d in range(experts))
        for d in range(experts):
            grad = gate_ref[:, d : d + 1] * (picked[d] - mean)
            acc = acc + grad * router_ref[d : d + 1, :]
        for c in range(chunk_count):
            for d in range(experts):
                value = flat_refs[c * experts + d][...]
                slot = lax.broadcasted_iota(jnp.int32, (total, value.shape[0]), 1) + firsts[c]
                weight = jnp.where(rank_ref[:, d : d + 1] == slot, gate_ref[:, d : d + 1], 0.0)
                high = weight.astype(bf16)
                low = (weight - high.astype(f32)).astype(bf16)
                acc = acc + jnp.dot(high, value, preferred_element_type=f32)
                acc = acc + jnp.dot(low, value, preferred_element_type=f32)
        for g in range(groups):
            out_refs[g][...] = acc[g * tokens : (g + 1) * tokens].astype(bf16)

    return pl.pallas_call(
        body,
        out_shape=[jax.ShapeDtypeStruct((tokens, width), bf16)] * groups,
        compiler_params=params(),
        cost_estimate=cost(
            4 * total * width * experts * 68, 2 * width * (total + experts * 68)
        ),
        name="combine",
    )(*flat, scores, rank, gates, router)


def attention(
    place, queries, key_rows, value_rows, decay_rate, norm_gain, attn_probe, coeff
):
    rollouts, block_size, feature_width = queries.shape
    head_count = decay_rate.shape[0]
    head_size = feature_width // head_count
    shape_four = (rollouts, block_size, head_count, head_size)
    query_full = queries.reshape(shape_four).astype(f32)
    key_full = key_rows.reshape(shape_four).astype(f32)
    value_full = value_rows.reshape(shape_four).astype(f32)
    probe_full = attn_probe.reshape(shape_four).astype(f32)
    gain_full = norm_gain.reshape(head_count, head_size)
    offsets = jnp.arange(block_size, dtype=f32)
    rate_row = decay_rate[None, :]
    distance = offsets[:, None] - offsets[None, :]
    within = jnp.where(
        (distance >= 0)[None],
        jnp.exp(-decay_rate[:, None, None] * jnp.maximum(distance, 0.0)[None]),
        0.0,
    )
    lead_decay = jnp.exp(-rate_row * (offsets[:, None] + 1.0))[None, :, :, None]
    key_tail = jnp.exp(-rate_row * (block_size - 1.0 - offsets[:, None]))[None, :, :, None]
    query_tail = jnp.exp(-rate_row * offsets[:, None])[None, :, :, None]
    grad_tail = jnp.exp(-rate_row * (block_size - offsets[:, None]))[None, :, :, None]

    def block_decay(blocks):
        return jnp.exp(-decay_rate * (block_size * blocks)).reshape(1, head_count, 1, 1)

    def carried(summary, direction):
        partner = place.swap_core(summary)
        first = (place.core == 0) if direction > 0 else (place.core == 1)
        one = block_decay(1)
        near = jnp.where(first, partner + one * summary, summary + one * partner)
        outside = jnp.zeros_like(summary)
        for p in range(1, place.chips):
            outside = outside + block_decay(2 * (p - 1)) * place.later_chip(near, direction * p)
        return jnp.where(first, outside, partner + one * outside)

    forward_summary = jnp.einsum(
        "rjhk,rjhv->rhkv", key_full * key_tail, value_full, precision=highest
    )
    state_before = carried(forward_summary, 1)
    scores = jnp.einsum("rihc,rjhc->rhij", query_full, key_full, precision=highest) * within[None]
    output = jnp.einsum("rhij,rjhv->rihv", scores, value_full, precision=highest)
    output = output + lead_decay * jnp.einsum(
        "rihk,rhkv->rihv", query_full, state_before, precision=highest
    )
    inverse = lax.rsqrt(jnp.mean(output * output, axis=-1, keepdims=True) + norm_epsilon)
    scaled = gain_full[None, None] * (coeff[:, :, None, None] * probe_full)
    grad_out = inverse * scaled - output * inverse**3 * jnp.mean(
        scaled * output, axis=-1, keepdims=True
    )
    backward_summary = jnp.einsum(
        "rihk,rihv->rhkv", query_full * query_tail, grad_out, precision=highest
    )
    state_after = carried(backward_summary, -1)
    product = jnp.einsum("rihv,rjhv->rhij", grad_out, value_full, precision=highest) * within[None]
    grad_query = jnp.einsum("rhij,rjhk->rihk", product, key_full, precision=highest)
    grad_query = grad_query + lead_decay * jnp.einsum(
        "rihv,rhkv->rihk", grad_out, state_before, precision=highest
    )
    grad_key = jnp.einsum("rhij,rihk->rjhk", product, query_full, precision=highest)
    grad_key = grad_key + grad_tail * jnp.einsum(
        "rjhv,rhkv->rjhk", value_full, state_after, precision=highest
    )
    grad_value = jnp.einsum("rhij,rihv->rjhv", scores, grad_out, precision=highest)
    grad_value = grad_value + grad_tail * jnp.einsum(
        "rjhk,rhkv->rjhv", key_full, state_after, precision=highest
    )
    out_shape = (rollouts, block_size, feature_width)
    return tuple(v.reshape(out_shape).astype(bf16) for v in (grad_query, grad_key, grad_value))


def expert_block(
    place, hidden_in, moe_probe, router_weight, routes, gate_weight, up_weight, down_weight, coeff
):
    rollouts, positions, model_width = hidden_in.shape
    chips, experts, slices = place.chips, place.experts, place.slices
    tokens = rollouts * positions
    width = gate_weight.shape[1]
    own_mats = (gate_weight[0], up_weight[0], down_weight[0])

    hidden = hidden_in.reshape(tokens, model_width)
    local_coeff = lax.dynamic_slice_in_dim(
        coeff, lax.axis_index("expert") * positions, positions, 1
    )
    grads = (local_coeff[:, :, None] * moe_probe.astype(f32)).astype(bf16)
    grads = grads.reshape(tokens, model_width)

    def halves_of(v, p):
        chip = (place.chip + p) % chips
        return jnp.stack(
            [
                lax.dynamic_slice_in_dim(v, (2 * chip + core) * width, width, 1)
                for core in (place.core, 1 - place.core)
            ]
        )

    far = (place.expert + jnp.arange(experts, dtype=jnp.int32)) % experts
    logits = jnp.dot(hidden, router_weight, preferred_element_type=f32)
    flat_routes = routes.reshape(tokens, -1)
    onehot = (flat_routes[:, :, None] == jnp.arange(experts, dtype=jnp.int32)).astype(f32)
    chosen = jnp.sum(onehot * logits[:, None, :], axis=-1)
    exponent = jnp.exp(chosen)
    gate = exponent / jnp.sum(exponent, axis=-1, keepdims=True)
    near_hot = (flat_routes[:, :, None] == far).astype(f32)
    facts = jnp.concatenate(
        [near_hot.sum(axis=1), jnp.sum(near_hot * gate[:, :, None], axis=1)], axis=1
    )
    all_facts = [facts] + [place.turn_chip(facts, p) for p in range(1, chips)]

    def across(v):
        return [halves_of(v, 0)] + [
            place.turn_chip(halves_of(v, p), p) for p in range(1, chips)
        ]

    hidden_groups = across(hidden)
    grad_groups = across(grads)
    pairs = [(m, place.swap_core(m)) for m in own_mats]

    fact_stack = jnp.stack(all_facts)
    member, gates = fact_stack[:, :, :experts], fact_stack[:, :, experts:]
    whose = (place.chip - jnp.arange(chips)) % chips
    earlier = (whose[None, :] < whose[:, None]).astype(f32)
    offset = jnp.sum(earlier[:, :, None] * member.sum(axis=1)[None], axis=1)
    step = jnp.arange(tokens)
    below = (step[:, None] > step[None, :]).astype(f32)
    rank = jnp.einsum("ts,gse->gte", below, member) + offset[:, None, :]
    rank = jnp.where(member > 0, rank, -1.0).astype(jnp.int32)
    rank = rank.reshape(chips * tokens, experts)
    gates = gates.reshape(chips * tokens, experts)
    rank_lanes = rank.T

    most = chips * rollouts * (positions // 2 + 1)
    small = max(16, most // 2 // 16 * 16)
    chunks = [(0, small), (small, most - small)]
    chip_here = place.chip.reshape(1).astype(jnp.int32)

    def dispatch(groups, first, count):
        padded = -(-count // 16) * 16
        picked = pick_rows(groups, rank_lanes, first, count, padded)
        mine = [picked[0]] + [place.turn_expert(picked[d], d) for d in range(1, experts)]
        blocks = list(mine)
        for k in range(1, slices):
            blocks += [place.turn_slice(v, k) for v in mine]
        return blocks

    def partial(blocks, count, pair, scale):
        keep, send = project(blocks, count, pair, chip_here, chips)
        ready = (send * scale).astype(jnp.float16)
        arrived = [place.turn_chip(ready[p - 1], p) for p in range(1, chips)]
        return keep, arrived

    def settle(part, scale):
        keep, arrived = part
        return keep + sum(v.astype(f32) for v in arrived) * (1.0 / scale)

    def ring(v):
        found = [v] + [None] * (chips - 1)
        for p in range(1, chips):
            found[chips - p] = place.turn_chip(v, p)
        return found

    def forward(first, count):
        blocks = dispatch(hidden_groups, first, count)
        gate_part = partial(blocks, count, pairs[0], in_scale)
        up_part = partial(blocks, count, pairs[1], in_scale)
        blocks = dispatch(grad_groups, first, count)
        down_part = partial(blocks, count, pairs[2], out_scale)
        return gate_part, up_part, down_part

    def middle(parts):
        pre_gate = settle(parts[0], in_scale)
        pre_up = settle(parts[1], in_scale)
        unit_grad = settle(parts[2], out_scale)
        sigmoid_gate = jax.nn.sigmoid(pre_gate)
        activated = pre_gate * sigmoid_gate
        units = activated * pre_up
        score = jnp.sum(units * unit_grad, axis=-1).astype(bf16)
        up_grad = (unit_grad * activated).astype(bf16)
        gate_grad = (
            unit_grad * pre_up * sigmoid_gate * (1.0 + pre_gate * (1.0 - sigmoid_gate))
        ).astype(bf16)
        return ring(gate_grad), ring(up_grad), ring(score)

    def rows_for(parts, k, count):
        per_part = slices // chips
        block = experts * count
        which = (k // per_part - place.chip + chips) % chips
        part = lax.dynamic_index_in_dim(parts, which, 0, keepdims=False)
        return lax.slice_in_dim(part, (k % per_part) * block, (k % per_part + 1) * block, axis=0)

    def home(parts, count):
        total = rows_for(parts, 0, count).astype(f32)
        for k in range(1, slices):
            total = total + place.turn_slice(rows_for(parts, k, count), -k).astype(f32)
        return total

    def homeward(v, count):
        blocks = [lax.slice_in_dim(v, d * count, (d + 1) * count, axis=0) for d in range(experts)]
        return [blocks[0]] + [place.turn_expert(blocks[d], -d) for d in range(1, experts)]

    def backward(gate_parts, up_parts, count):
        out = []
        for h in range(2):
            dx = project_back(gate_parts, up_parts, pairs[0][h], pairs[1][h])
            out.append(homeward(home(dx, count).astype(bf16), count))
        return out

    first_parts = forward(*chunks[0])
    second_parts = forward(*chunks[1])
    first_grads = middle(first_parts)
    first_back = backward(first_grads[0], first_grads[1], chunks[0][1])
    second_grads = middle(second_parts)
    second_back = backward(second_grads[0], second_grads[1], chunks[1][1])

    score_rows = [
        home(jnp.stack(g[2]), count).reshape(experts, count)
        for g, (_, count) in zip((first_grads, second_grads), chunks)
    ]
    score_rows = jnp.concatenate(score_rows, axis=1)
    score_home = jnp.concatenate(
        [score_rows[:1]]
        + [place.turn_expert(score_rows[d : d + 1], -d) for d in range(1, experts)],
        axis=0,
    )

    router_rows = halves_of(router_weight.T.astype(f32), 0)
    router_rows = jnp.take(router_rows, far, axis=1)
    firsts = [first for first, _ in chunks]
    result = jnp.zeros((tokens, model_width), bf16)
    for h in range(2):
        groups = combine(
            [first_back[h], second_back[h]],
            score_home,
            rank,
            gates,
            router_rows[h],
            firsts,
            chips,
        )
        core = place.core if h == 0 else 1 - place.core
        for g in range(chips):
            part = groups[g] if g == 0 else place.turn_chip(groups[g], -g)
            chip = (place.chip + g) % chips
            result = lax.dynamic_update_slice_in_dim(result, part, (2 * chip + core) * width, 1)
    return result.reshape(rollouts, positions, model_width)


def on_device(
    queries,
    key_rows,
    value_rows,
    decay_rate,
    norm_gain,
    attn_probe,
    hidden_in,
    moe_probe,
    router_weight,
    routes,
    gate_weight,
    up_weight,
    down_weight,
    rollout_logprob,
    trainer_logprob,
    advantage,
    clip_low,
    clip_high,
):
    place = Layout(router_weight.shape[1])
    importance = jnp.exp(trainer_logprob - rollout_logprob)
    clipped = jnp.minimum(jnp.maximum(importance, clip_low[0]), clip_high[0])
    coeff = -(clipped * advantage) / queries.shape[0]
    objective = coeff * trainer_logprob
    grad_hidden = expert_block(
        place,
        hidden_in,
        moe_probe,
        router_weight,
        routes,
        gate_weight,
        up_weight,
        down_weight,
        coeff,
    )
    attention_grads = attention(
        place, queries, key_rows, value_rows, decay_rate, norm_gain, attn_probe, coeff
    )
    return (objective, *attention_grads, grad_hidden)


def solution(mesh):
    in_specs = (
        P(None, "seq", "expert"),
        P(None, "seq", "expert"),
        P(None, "seq", "expert"),
        P("expert"),
        P("expert"),
        P(None, "seq", "expert"),
        P(None, ("seq", "expert"), None),
        P(None, ("seq", "expert"), None),
        P(),
        P(None, ("seq", "expert"), None),
        P("expert", "seq", None),
        P("expert", "seq", None),
        P("expert", "seq", None),
        P(None, "seq"),
        P(None, "seq"),
        P(None, "seq"),
        P(),
        P(),
    )
    out_specs = (
        P(None, "seq"),
        P(None, "seq", "expert"),
        P(None, "seq", "expert"),
        P(None, "seq", "expert"),
        P(None, ("seq", "expert"), None),
    )
    return jax.shard_map(
        on_device, mesh=mesh, in_specs=in_specs, out_specs=out_specs, check_vma=False
    )
```

time: 780 us -> 416 us (0.53)
  waiting for transfers between devices: 492 us -> 150 us
  matrix products: 131 us -> 15.7 us
  Pallas kernels: 0 us -> 109 us
  starting transfers between devices: 24.1 us -> 110 us
  local copies, waits for them, and re-layouts: 71.8 us -> 10.1 us
  other arithmetic: 31.1 us -> 15.4 us
  between operations: 16.5 us -> 3.19 us
    all_gather x5 -> x0, waiting for transfers between devices: 300 us -> none  [the longest x1 156 us: on_device(): lax.all_gather(down_weight, 'seq', axis=1, tiled=True)]
    all_to_all x4 -> x0, waiting for transfers between devices: 191 us -> none  [the longest x1 68.4 us: on_device(): lax.all_to_all(spread(token_buffer), 'expert', split_axis=0, concat_axis=...]
    ppermute x0 -> x73, waiting for transfers between devices: none -> 150 us  [the longest x17 66.3 us: turn_chip(): lax.ppermute(v, 'seq', [(i, (i // 2 + p) % n * 2 + i % 2) for i in range(...]
    dot_general x24 -> x14, matrix products: 131 us -> 15.7 us  [the longest x1 2.15 us: attention(): jnp.einsum('rjhk,rhkv->rjhv', key_full, state_after, precision=highest)]
    ppermute x0 -> x73, starting transfers between devices: none -> 110 us  [the longest x27 68.8 us: turn_expert(): lax.ppermute(v, 'expert', [(i, (i // m + d) % n * m + i % m) for i in ran...]
    pallas_call x0 -> x16, Pallas kernels: none -> 109 us  [the longest x6 66.3 us: project(): pl.pallas_call(body, grid=(units // tile,), in_specs=[pl.BlockSpec(memory...]
    reshape x10 -> x4, local copies, waits for them, and re-layouts: 49.5 us -> 0.43 us  [the longest x2 0.17 us: expert_block(): home(jnp.stack(g[2]), count).reshape(experts, count)]
    all_to_all x4 -> x0, starting transfers between devices: 23.7 us -> none  [the longest x1 7.52 us: on_device(): lax.all_to_all(spread(grad_buffer), 'expert', split_axis=0, concat_axis=0...]
  transfers between devices with their start and end apart: 9 -> 73, of which waited for: 6 -> 32; matrix products, arithmetic and copies ran while one was open for 20% -> 8% of each run, Pallas kernels for 0% -> 26%
where the time goes in v1:
time: 416 us; the launch traced here: 414 us
  waiting for transfers between devices  150 us (36%)
  starting transfers between devices  110 us (26%)
  Pallas kernels  109 us (26%)
  matrix products  15.7 us (4%)
  other arithmetic  15.4 us (4%)
  local copies, waits for them, and re-layouts  10.1 us (2%)
    ppermute x27, starting transfers between devices, turn_expert(): lax.ppermute(v, 'expert', [(i, (i // m + d) % n * m + i % m) for i in ran...  68.8 us
    pallas_call x6, Pallas kernels, project(): pl.pallas_call(body, grid=(units // tile,), in_specs=[pl.BlockSpec(memory...  66.3 us
    ppermute x17, waiting for transfers between devices, turn_chip(): lax.ppermute(v, 'seq', [(i, (i // 2 + p) % n * 2 + i % 2) for i in range(...  66.3 us
    ppermute x27, waiting for transfers between devices, turn_expert(): lax.ppermute(v, 'expert', [(i, (i // m + d) % n * m + i % m) for i in ran...  48.3 us
    pallas_call x4, Pallas kernels, project_back(): pl.pallas_call(body, grid=(width // tile,), in_specs=[part_spec] * (2 * c...  36.4 us
    ppermute x22, waiting for transfers between devices, turn_slice(): lax.ppermute(v, 'expert', [(i, i // m * m + (i % m + k) % m) for i in ran...  30.1 us
    ppermute x22, starting transfers between devices, turn_slice(): lax.ppermute(v, 'expert', [(i, i // m * m + (i % m + k) % m) for i in ran...  19.6 us
    ppermute x17, starting transfers between devices, turn_chip(): lax.ppermute(v, 'seq', [(i, (i // 2 + p) % n * 2 + i % 2) for i in range(...  15.8 us
  transfers between devices with their start and end apart: 73, of which 32 were waited for; matrix products, arithmetic and copies ran while one was open for 8% of the time, Pallas kernels for 26%

profile of v1, /device:TPU:0, one launch (start us, length us, event | category | flops | bytes accessed | tf_op | source)
XLA Modules:
  0.0 414.2 jit_solution(17496267727596044825)
XLA Ops:
  22.4 3.9 collective-permute-start.1
  47.8 12.6 %collective-permute-start.6 = (bf16[2,32,1536]{2,1,0:T(8,128)(2,1)S(1)}, bf16[2,32,1536]{2,1,0:T(8,128)(2,1)S(1)}, u32[]{:S(2)}, u32[]{:S(2)}) collective-permute-start(bf16[2,32,1536]{2,1,0:T(8,128)(2,1)S(1)} %get-tuple-element.38), channel_id=1, source_target_pairs={{0,2},{1,3},{2,4},{3,5},{4,6},{5,7},{6,0},{7,1},{8,10},{9,11},{10,... | collective-permute-start | bytes 589832 | tf_op jit(solution)/shard_map/ppermute | solution.py:44
  66.0 8.0 %collective-permute-done.7.refs_2_ = bf16[2,32,1536]{2,1,0:T(8,128)(2,1)S(1)} collective-permute-done((bf16[2,32,1536]{2,1,0:T(8,128)(2,1)S(1)}, bf16[2,32,1536]{2,1,0:T(8,128)(2,1)S(1)}, u32[]{:S(2)}, u32[]{:S(2)}) %collective-permute-start.7) | collective-permute-done | bytes 196640 | tf_op jit(solution)/shard_map/ppermute | solution.py:44
  77.8 4.1 collective-permute-start.43
  82.0 10.8 %collective-permute-done.42.refs_2_ = bf16[2,48,1536]{2,1,0:T(8,128)(2,1)S(1)} collective-permute-done((bf16[2,48,1536]{2,1,0:T(8,128)(2,1)S(1)}, bf16[2,48,1536]{2,1,0:T(8,128)(2,1)S(1)}, u32[]{:S(2)}, u32[]{:S(2)}) %collective-permute-start.42) | collective-permute-done | bytes 294944 | tf_op jit(solution)/shard_map/ppermute | solution.py:44
  94.3 5.5 %collective-permute-start.33 = (bf16[2,48,1536]{2,1,0:T(8,128)(2,1)S(1)}, bf16[2,48,1536]{2,1,0:T(8,128)(2,1)S(1)}, u32[]{:S(2)}, u32[]{:S(2)}) collective-permute-start(bf16[2,48,1536]{2,1,0:T(8,128)(2,1)S(1)} %get-tuple-element.52), channel_id=1, source_target_pairs={{0,2},{1,3},{2,4},{3,5},{4,6},{5,7},{6,0},{7,1},{8,10},{9,11},{10,... | collective-permute-start | bytes 884744 | tf_op jit(solution)/shard_map/ppermute | solution.py:44
  104.7 5.0 %collective-permute-done.33.refs_1_ = bf16[2,48,1536]{2,1,0:T(8,128)(2,1)S(1)} collective-permute-done((bf16[2,48,1536]{2,1,0:T(8,128)(2,1)S(1)}, bf16[2,48,1536]{2,1,0:T(8,128)(2,1)S(1)}, u32[]{:S(2)}, u32[]{:S(2)}) %collective-permute-start.33) | collective-permute-done | bytes 294944 | tf_op jit(solution)/shard_map/ppermute | solution.py:44
  114.2 8.1 %collective-permute-done.34.refs_2_ = bf16[2,48,1536]{2,1,0:T(8,128)(2,1)S(1)} collective-permute-done((bf16[2,48,1536]{2,1,0:T(8,128)(2,1)S(1)}, bf16[2,48,1536]{2,1,0:T(8,128)(2,1)S(1)}, u32[]{:S(2)}, u32[]{:S(2)}) %collective-permute-start.34) | collective-permute-done | bytes 294944 | tf_op jit(solution)/shard_map/ppermute | solution.py:44
  128.1 4.2 %collective-permute-done.36.refs_4_ = bf16[2,48,1536]{2,1,0:T(8,128)(2,1)} collective-permute-done((bf16[2,48,1536]{2,1,0:T(8,128)(2,1)S(1)}, bf16[2,48,1536]{2,1,0:T(8,128)(2,1)}, u32[]{:S(2)}, u32[]{:S(2)}) %collective-permute-start.36) | collective-permute-done | bytes 294944 | tf_op jit(solution)/shard_map/ppermute | solution.py:50
  147.9 5.8 %collective-permute-done.47.refs_7_ = bf16[2,48,1536]{2,1,0:T(8,128)(2,1)S(1)} collective-permute-done((bf16[2,48,1536]{2,1,0:T(8,128)(2,1)S(1)}, bf16[2,48,1536]{2,1,0:T(8,128)(2,1)S(1)}, u32[]{:S(2)}, u32[]{:S(2)}) %collective-permute-start.47) | collective-permute-done | bytes 294944 | tf_op jit(solution)/shard_map/ppermute | solution.py:50
  155.8 11.5 %project.11 = (f32[144,2304]{1,0:T(8,128)S(1)}, f32[1,144,2304]{2,1,0:T(8,128)S(1)}) custom-call(s32[1]{0:T(128)} %bitcast.15.chip_ref, bf16[2,48,1536]{2,1,0:T(8,128)(2,1)S(1)} %get-tuple-element.57.refs_0_, bf16[2,48,1536]{2,1,0:T(8,128)(2,1)S(1)} %collective-permute-done.41.refs_1_, bf16[2,48,1536]{2,1,0:T(8,128)(2,1)S(1)} %collective-permute-done.42.refs_2_, ...), custom_call_target="tpu_custom_call" | custom-call | flops 4076863488 | bytes 16809984 | tf_op jit(solution)/shard_map/project/pallas_call | solution.py:126
  171.0 10.6 %project.8 = (f32[128,2304]{1,0:T(8,128)S(1)}, f32[1,128,2304]{2,1,0:T(8,128)S(1)}) custom-call(s32[1]{0:T(128)} %bitcast.15.chip_ref, bf16[2,32,1536]{2,1,0:T(8,128)(2,1)S(1)} %get-tuple-element.43.refs_0_, bf16[2,32,1536]{2,1,0:T(8,128)(2,1)S(1)} %collective-permute-done.16.refs_1_, bf16[2,32,1536]{2,1,0:T(8,128)(2,1)S(1)} %collective-permute-done.17.refs_2_, ...), custom_call_target="tpu_custom_call" | custom-call | flops 3623878656 | bytes 16515072 | tf_op jit(solution)/shard_map/project/pallas_call | solution.py:126
  185.2 5.8 %collective-permute-done.39.refs_7_ = bf16[2,48,1536]{2,1,0:T(8,128)(2,1)S(1)} collective-permute-done((bf16[2,48,1536]{2,1,0:T(8,128)(2,1)S(1)}, bf16[2,48,1536]{2,1,0:T(8,128)(2,1)S(1)}, u32[]{:S(2)}, u32[]{:S(2)}) %collective-permute-start.39) | collective-permute-done | bytes 294944 | tf_op jit(solution)/shard_map/ppermute | solution.py:50
  193.1 11.5 %project.9 = (f32[144,2304]{1,0:T(8,128)S(1)}, f32[1,144,2304]{2,1,0:T(8,128)S(1)}) custom-call(s32[1]{0:T(128)} %bitcast.15.chip_ref, bf16[2,48,1536]{2,1,0:T(8,128)(2,1)S(1)} %copy-done.7, bf16[2,48,1536]{2,1,0:T(8,128)(2,1)S(1)} %copy-done.9, bf16[2,48,1536]{2,1,0:T(8,128)(2,1)S(1)} %copy-done.11, bf16[2,48,1536]{2,1,0:T(8,128)(2,1)S(1)} %copy-done.13, ...), custom_call_target="tpu_custom_call" | custom-call | flops 4076863488 | bytes 16809984 | tf_op jit(solution)/shard_map/project/pallas_call | solution.py:126
  209.0 10.6 %project.6 = (f32[128,2304]{1,0:T(8,128)S(1)}, f32[1,128,2304]{2,1,0:T(8,128)S(1)}) custom-call(s32[1]{0:T(128)} %bitcast.15.chip_ref, bf16[2,32,1536]{2,1,0:T(8,128)(2,1)S(1)} %copy-done.15, bf16[2,32,1536]{2,1,0:T(8,128)(2,1)S(1)} %copy-done.17, bf16[2,32,1536]{2,1,0:T(8,128)(2,1)S(1)} %copy-done.19, bf16[2,32,1536]{2,1,0:T(8,128)(2,1)S(1)} %copy-done.21, ...), custom_call_target="tpu_custom_call" | custom-call | flops 3623878656 | bytes 16515072 | tf_op jit(solution)/shard_map/project/pallas_call | solution.py:126
  221.7 10.6 %project.7 = (f32[128,2304]{1,0:T(8,128)S(1)}, f32[1,128,2304]{2,1,0:T(8,128)S(1)}) custom-call(s32[1]{0:T(128)} %bitcast.15.chip_ref, bf16[2,32,1536]{2,1,0:T(8,128)(2,1)S(1)} %get-tuple-element.43.refs_0_, bf16[2,32,1536]{2,1,0:T(8,128)(2,1)S(1)} %collective-permute-done.16.refs_1_, bf16[2,32,1536]{2,1,0:T(8,128)(2,1)S(1)} %collective-permute-done.17.refs_2_, ...), custom_call_target="tpu_custom_call" | custom-call | flops 3623878656 | bytes 16515072 | tf_op jit(solution)/shard_map/project/pallas_call | solution.py:126
  232.7 11.4 %project.10 = (f32[144,2304]{1,0:T(8,128)S(1)}, f32[1,144,2304]{2,1,0:T(8,128)S(1)}) custom-call(s32[1]{0:T(128)} %bitcast.15.chip_ref, bf16[2,48,1536]{2,1,0:T(8,128)(2,1)S(1)} %get-tuple-element.57.refs_0_, bf16[2,48,1536]{2,1,0:T(8,128)(2,1)S(1)} %collective-permute-done.41.refs_1_, bf16[2,48,1536]{2,1,0:T(8,128)(2,1)S(1)} %collective-permute-done.42.refs_2_, ...), custom_call_target="tpu_custom_call" | custom-call | flops 4076863488 | bytes 16809984 | tf_op jit(solution)/shard_map/project/pallas_call | solution.py:126
  244.2 7.5 %collective-permute-done.26 = f16[128,2304]{1,0:T(8,128)(2,1)S(1)} collective-permute-done((f16[128,2304]{1,0:T(8,128)(2,1)S(1)}, f16[128,2304]{1,0:T(8,128)(2,1)S(1)}, u32[]{:S(2)}, u32[]{:S(2)}) %collective-permute-start.26) | collective-permute-done | bytes 589856 | tf_op jit(solution)/shard_map/ppermute | solution.py:34
  251.8 12.6 %collective-permute-done.14 = f16[128,2304]{1,0:T(8,128)(2,1)S(1)} collective-permute-done((f16[128,2304]{1,0:T(8,128)(2,1)S(1)}, f16[128,2304]{1,0:T(8,128)(2,1)S(1)}, u32[]{:S(2)}, u32[]{:S(2)}) %collective-permute-start.14) | collective-permute-done | bytes 589856 | tf_op jit(solution)/shard_map/ppermute | solution.py:34
  264.4 12.6 %collective-permute-done.24 = f16[128,2304]{1,0:T(8,128)(2,1)S(1)} collective-permute-done((f16[128,2304]{1,0:T(8,128)(2,1)S(1)}, f16[128,2304]{1,0:T(8,128)(2,1)S(1)}, u32[]{:S(2)}, u32[]{:S(2)}) %collective-permute-start.24) | collective-permute-done | bytes 589856 | tf_op jit(solution)/shard_map/ppermute | solution.py:34
  281.9 9.5 %collective-permute-done.56 = bf16[128]{0:T(256)(128)(2,1)S(1)} collective-permute-done((bf16[128]{0:T(256)(128)(2,1)S(1)}, bf16[128]{0:T(256)(128)(2,1)S(1)}, u32[]{:S(2)}, u32[]{:S(2)}) %collective-permute-start.56) | collective-permute-done | bytes 288 | tf_op jit(solution)/shard_map/ppermute | solution.py:34
  297.7 15.7 %collective-permute-done.58 = bf16[144]{0:T(256)(128)(2,1)S(1)} collective-permute-done((bf16[144]{0:T(256)(128)(2,1)S(1)}, bf16[144]{0:T(256)(128)(2,1)S(1)}, u32[]{:S(2)}, u32[]{:S(2)}) %collective-permute-start.58) | collective-permute-done | bytes 320 | tf_op jit(solution)/shard_map/ppermute | solution.py:34
  317.2 6.9 %collective-permute-start.60 = (f32[1,68]{1,0:T(1,128)S(1)}, f32[1,68]{1,0:T(1,128)S(1)}, u32[]{:S(2)}, u32[]{:S(2)}) collective-permute-start(f32[1,68]{1,0:T(1,128)S(1)} %get-tuple-element.133), channel_id=1, source_target_pairs={{0,6},{1,7},{2,0},{3,1},{4,2},{5,3},{6,4},{7,5},{8,14},{9,15},{10,... | collective-permute-start | bytes 824 | tf_op jit(solution)/shard_map/ppermute | solution.py:44
  324.7 9.0 %project_back.6 = bf16[2,128,1536]{2,1,0:T(8,128)(2,1)S(1)} custom-call(bf16[128,2304]{1,0:T(8,128)(2,1)S(1)} %get-tuple-element.93.refs_0_, bf16[128,2304]{1,0:T(8,128)(2,1)} %collective-permute-done.27.refs_1_, bf16[128,2304]{1,0:T(8,128)(2,1)S(1)} %get-tuple-element.95.refs_2_, bf16[128,2304]{1,0:T(8,128)(2,1)} %collective-permute-done.28.refs_3_, ...), custom_call_target="tpu_custom_call" | custom-call | flops 3623878656 | bytes 14942208 | tf_op jit(solution)/shard_map/project_back/pallas_call | solution.py:178
  333.8 9.0 %project_back.4 = bf16[2,128,1536]{2,1,0:T(8,128)(2,1)S(1)} custom-call(bf16[128,2304]{1,0:T(8,128)(2,1)S(1)} %get-tuple-element.93.refs_0_, bf16[128,2304]{1,0:T(8,128)(2,1)} %collective-permute-done.27.refs_1_, bf16[128,2304]{1,0:T(8,128)(2,1)S(1)} %get-tuple-element.95.refs_2_, bf16[128,2304]{1,0:T(8,128)(2,1)} %collective-permute-done.28.refs_3_, ...), custom_call_target="tpu_custom_call" | custom-call | flops 3623878656 | bytes 14942208 | tf_op jit(solution)/shard_map/project_back/pallas_call | solution.py:178
  345.0 9.2 %project_back.7 = bf16[2,144,1536]{2,1,0:T(8,128)(2,1)S(1)} custom-call(bf16[144,2304]{1,0:T(8,128)(2,1)S(1)} %get-tuple-element.91.refs_0_, bf16[144,2304]{1,0:T(8,128)(2,1)S(1)} %collective-permute-done.50.refs_1_, bf16[144,2304]{1,0:T(8,128)(2,1)S(1)} %get-tuple-element.94.refs_2_, bf16[144,2304]{1,0:T(8,128)(2,1)} %collective-permute-done.51.refs_3_, ...), custom_call_target="tpu_custom_call" | custom-call | flops 4076863488 | bytes 15040512 | tf_op jit(solution)/shard_map/project_back/pallas_call | solution.py:178
  354.1 9.2 %project_back.5 = bf16[2,144,1536]{2,1,0:T(8,128)(2,1)S(1)} custom-call(bf16[144,2304]{1,0:T(8,128)(2,1)S(1)} %get-tuple-element.91.refs_0_, bf16[144,2304]{1,0:T(8,128)(2,1)S(1)} %collective-permute-done.50.refs_1_, bf16[144,2304]{1,0:T(8,128)(2,1)S(1)} %get-tuple-element.94.refs_2_, bf16[144,2304]{1,0:T(8,128)(2,1)} %collective-permute-done.51.refs_3_, ...), custom_call_target="tpu_custom_call" | custom-call | flops 4076863488 | bytes 15040512 | tf_op jit(solution)/shard_map/project_back/pallas_call | solution.py:178
  365.9 5.9 %collective-permute-done.68 = bf16[144,1536]{1,0:T(8,128)(2,1)S(1)} collective-permute-done((bf16[144,1536]{1,0:T(8,128)(2,1)S(1)}, bf16[144,1536]{1,0:T(8,128)(2,1)S(1)}, u32[]{:S(2)}, u32[]{:S(2)}) %collective-permute-start.68) | collective-permute-done | bytes 442400 | tf_op jit(solution)/shard_map/ppermute | solution.py:50
  388.6 5.2 %collective-permute-done.31.refs_2_ = bf16[32,1536]{1,0:T(8,128)(2,1)S(1)} collective-permute-done((bf16[32,1536]{1,0:T(8,128)(2,1)S(1)}, bf16[32,1536]{1,0:T(8,128)(2,1)S(1)}, u32[]{:S(2)}, u32[]{:S(2)}) %collective-permute-start.31) | collective-permute-done | bytes 98336 | tf_op jit(solution)/shard_map/ppermute | solution.py:44
  393.8 3.8 collective-permute-start.69
  401.7 4.0 collective-permute-done.70.refs_6_
  407.9 5.3 %collective-permute-done.72 = bf16[64,1536]{1,0:T(8,128)(2,1)S(1)} collective-permute-done((bf16[64,1536]{1,0:T(8,128)(2,1)S(1)}, bf16[64,1536]{1,0:T(8,128)(2,1)S(1)}, u32[]{:S(2)}, u32[]{:S(2)}) %collective-permute-start.72) | collective-permute-done | bytes 196640 | tf_op jit(solution)/shard_map/ppermute | solution.py:34
  (331 shorter events, 145.4 us)
Async XLA Ops:
  6.6 20.1 %collective-permute-start.15 = (bf16[2,64,1536]{2,1,0:T(8,128)(2,1)}, bf16[2,64,1536]{2,1,0:T(8,128)(2,1)S(1)}, u32[]{:S(2)}, u32[]{:S(2)}) collective-permute-start(bf16[2,64,1536]{2,1,0:T(8,128)(2,1)} %pad_maximum_fusion.3), channel_id=1, source_target_pairs={{0,16},{8,24},{16,0},{24,8},{1,17},{9,25},{17,1},{25,9},{2,18},{10... | collective-permute-start | bytes 1179656 | tf_op jit(solution)/shard_map/ppermute | solution.py:34
  10.2 144.1 %collective-permute-start.25 = (bf16[1536,2304]{1,0:T(8,128)(2,1)}, bf16[1536,2304]{1,0:T(8,128)(2,1)}, u32[]{:S(2)}, u32[]{:S(2)}) collective-permute-start(bf16[1536,2304]{1,0:T(8,128)(2,1)} %bitcast.209), channel_id=1, source_target_pairs={{0,8},{8,0},{16,24},{24,16},{1,9},{9,1},{17,25},{25,17},{2,10},{10... | collective-permute-start | bytes 21233672 | tf_op jit(solution)/shard_map/ppermute | solution.py:30
  10.2 181.3 %collective-permute-start.13 = (bf16[1536,2304]{1,0:T(8,128)(2,1)}, bf16[1536,2304]{1,0:T(8,128)(2,1)}, u32[]{:S(2)}, u32[]{:S(2)}) collective-permute-start(bf16[1536,2304]{1,0:T(8,128)(2,1)} %bitcast.214), channel_id=1, source_target_pairs={{0,8},{8,0},{16,24},{24,16},{1,9},{9,1},{17,25},{25,17},{2,10},{10... | collective-permute-start | bytes 21233672 | tf_op jit(solution)/shard_map/ppermute | solution.py:30
  41.1 36.6 %collective-permute-start.41 = (bf16[2,48,1536]{2,1,0:T(8,128)(2,1)S(1)}, bf16[2,48,1536]{2,1,0:T(8,128)(2,1)S(1)}, u32[]{:S(2)}, u32[]{:S(2)}) collective-permute-start(bf16[2,48,1536]{2,1,0:T(8,128)(2,1)S(1)} %get-tuple-element.58), channel_id=1, source_target_pairs={{0,2},{1,3},{2,4},{3,5},{4,6},{5,7},{6,0},{7,1},{8,10},{9,11},{10,... | collective-permute-start | bytes 884744 | tf_op jit(solution)/shard_map/ppermute | solution.py:44
  46.2 16.2 %collective-permute-start.19 = (bf16[2,32,1536]{2,1,0:T(8,128)(2,1)S(1)}, bf16[2,32,1536]{2,1,0:T(8,128)(2,1)S(1)}, u32[]{:S(2)}, u32[]{:S(2)}) collective-permute-start(bf16[2,32,1536]{2,1,0:T(8,128)(2,1)S(1)} %get-tuple-element.43.refs_0_), channel_id=1, source_target_pairs={{0,1},{1,0},{2,3},{3,2},{4,5},{5,4},{6,7},{7,6},{8,9},{9,8},{10,11... | collective-permute-start | bytes 589832 | tf_op jit(solution)/shard_map/ppermute | solution.py:50
  47.8 17.9 %collective-permute-start.6 = (bf16[2,32,1536]{2,1,0:T(8,128)(2,1)S(1)}, bf16[2,32,1536]{2,1,0:T(8,128)(2,1)S(1)}, u32[]{:S(2)}, u32[]{:S(2)}) collective-permute-start(bf16[2,32,1536]{2,1,0:T(8,128)(2,1)S(1)} %get-tuple-element.38), channel_id=1, source_target_pairs={{0,2},{1,3},{2,4},{3,5},{4,6},{5,7},{6,0},{7,1},{8,10},{9,11},{10,... | collective-permute-start | bytes 589832 | tf_op jit(solution)/shard_map/ppermute | solution.py:44
  74.1 147.6 %collective-permute-start.23 = (bf16[1536,2304]{1,0:T(8,128)(2,1)}, bf16[1536,2304]{1,0:T(8,128)(2,1)}, u32[]{:S(2)}, u32[]{:S(2)}) collective-permute-start(bf16[1536,2304]{1,0:T(8,128)(2,1)} %bitcast.204), channel_id=1, source_target_pairs={{0,8},{8,0},{16,24},{24,16},{1,9},{9,1},{17,25},{25,17},{2,10},{10... | collective-permute-start | bytes 21233672 | tf_op jit(solution)/shard_map/ppermute | solution.py:30
  75.6 17.2 %collective-permute-start.42 = (bf16[2,48,1536]{2,1,0:T(8,128)(2,1)S(1)}, bf16[2,48,1536]{2,1,0:T(8,128)(2,1)S(1)}, u32[]{:S(2)}, u32[]{:S(2)}) collective-permute-start(bf16[2,48,1536]{2,1,0:T(8,128)(2,1)S(1)} %get-tuple-element.59), channel_id=1, source_target_pairs={{0,4},{1,5},{2,6},{3,7},{4,0},{5,1},{6,2},{7,3},{8,12},{9,13},{10,... | collective-permute-start | bytes 884744 | tf_op jit(solution)/shard_map/ppermute | solution.py:44
  77.8 16.6 %collective-permute-start.43 = (bf16[2,48,1536]{2,1,0:T(8,128)(2,1)S(1)}, bf16[2,48,1536]{2,1,0:T(8,128)(2,1)S(1)}, u32[]{:S(2)}, u32[]{:S(2)}) collective-permute-start(bf16[2,48,1536]{2,1,0:T(8,128)(2,1)S(1)} %get-tuple-element.60), channel_id=1, source_target_pairs={{0,6},{1,7},{2,0},{3,1},{4,2},{5,3},{6,4},{7,5},{8,14},{9,15},{10,... | collective-permute-start | bytes 884744 | tf_op jit(solution)/shard_map/ppermute | solution.py:44
  101.2 21.1 %collective-permute-start.34 = (bf16[2,48,1536]{2,1,0:T(8,128)(2,1)S(1)}, bf16[2,48,1536]{2,1,0:T(8,128)(2,1)S(1)}, u32[]{:S(2)}, u32[]{:S(2)}) collective-permute-start(bf16[2,48,1536]{2,1,0:T(8,128)(2,1)S(1)} %get-tuple-element.53), channel_id=1, source_target_pairs={{0,4},{1,5},{2,6},{3,7},{4,0},{5,1},{6,2},{7,3},{8,12},{9,13},{10,... | collective-permute-start | bytes 884744 | tf_op jit(solution)/shard_map/ppermute | solution.py:44
  147.4 20.9 %collective-permute-start.20 = (bf16[2,32,1536]{2,1,0:T(8,128)(2,1)S(1)}, bf16[2,32,1536]{2,1,0:T(8,128)(2,1)S(1)}, u32[]{:S(2)}, u32[]{:S(2)}) collective-permute-start(bf16[2,32,1536]{2,1,0:T(8,128)(2,1)S(1)} %collective-permute-done.16.refs_1_), channel_id=1, source_target_pairs={{0,1},{1,0},{2,3},{3,2},{4,5},{5,4},{6,7},{7,6},{8,9},{9,8},{10,11... | collective-permute-start | bytes 589832 | tf_op jit(solution)/shard_map/ppermute | solution.py:50
  170.5 20.5 %collective-permute-start.39 = (bf16[2,48,1536]{2,1,0:T(8,128)(2,1)S(1)}, bf16[2,48,1536]{2,1,0:T(8,128)(2,1)S(1)}, u32[]{:S(2)}, u32[]{:S(2)}) collective-permute-start(bf16[2,48,1536]{2,1,0:T(8,128)(2,1)S(1)} %copy-done.13), channel_id=1, source_target_pairs={{0,1},{1,0},{2,3},{3,2},{4,5},{5,4},{6,7},{7,6},{8,9},{9,8},{10,11... | collective-permute-start | bytes 884744 | tf_op jit(solution)/shard_map/ppermute | solution.py:50
  181.7 25.1 %collective-permute-start.9 = (bf16[2,32,1536]{2,1,0:T(8,128)(2,1)S(1)}, bf16[2,32,1536]{2,1,0:T(8,128)(2,1)S(1)}, u32[]{:S(2)}, u32[]{:S(2)}) collective-permute-start(bf16[2,32,1536]{2,1,0:T(8,128)(2,1)S(1)} %copy-done.15), channel_id=1, source_target_pairs={{0,1},{1,0},{2,3},{3,2},{4,5},{5,4},{6,7},{7,6},{8,9},{9,8},{10,11... | collective-permute-start | bytes 589832 | tf_op jit(solution)/shard_map/ppermute | solution.py:50
  184.7 22.1 %collective-permute-start.10 = (bf16[2,32,1536]{2,1,0:T(8,128)(2,1)S(1)}, bf16[2,32,1536]{2,1,0:T(8,128)(2,1)S(1)}, u32[]{:S(2)}, u32[]{:S(2)}) collective-permute-start(bf16[2,32,1536]{2,1,0:T(8,128)(2,1)S(1)} %copy-done.17), channel_id=1, source_target_pairs={{0,1},{1,0},{2,3},{3,2},{4,5},{5,4},{6,7},{7,6},{8,9},{9,8},{10,11... | collective-permute-start | bytes 589832 | tf_op jit(solution)/shard_map/ppermute | solution.py:50
  191.0 17.8 %collective-permute-start.11 = (bf16[2,32,1536]{2,1,0:T(8,128)(2,1)S(1)}, bf16[2,32,1536]{2,1,0:T(8,128)(2,1)S(1)}, u32[]{:S(2)}, u32[]{:S(2)}) collective-permute-start(bf16[2,32,1536]{2,1,0:T(8,128)(2,1)S(1)} %copy-done.19), channel_id=1, source_target_pairs={{0,1},{1,0},{2,3},{3,2},{4,5},{5,4},{6,7},{7,6},{8,9},{9,8},{10,11... | collective-permute-start | bytes 589832 | tf_op jit(solution)/shard_map/ppermute | solution.py:50
  191.6 17.4 %collective-permute-start.12 = (bf16[2,32,1536]{2,1,0:T(8,128)(2,1)S(1)}, bf16[2,32,1536]{2,1,0:T(8,128)(2,1)S(1)}, u32[]{:S(2)}, u32[]{:S(2)}) collective-permute-start(bf16[2,32,1536]{2,1,0:T(8,128)(2,1)S(1)} %copy-done.21), channel_id=1, source_target_pairs={{0,1},{1,0},{2,3},{3,2},{4,5},{5,4},{6,7},{7,6},{8,9},{9,8},{10,11... | collective-permute-start | bytes 589832 | tf_op jit(solution)/shard_map/ppermute | solution.py:50
  206.8 84.6 %collective-permute-start.49 = (f16[144,2304]{1,0:T(8,128)(2,1)}, f16[144,2304]{1,0:T(8,128)(2,1)}, u32[]{:S(2)}, u32[]{:S(2)}) collective-permute-start(f16[144,2304]{1,0:T(8,128)(2,1)} %fusion.20), channel_id=1, source_target_pairs={{0,16},{8,24},{16,0},{24,8},{1,17},{9,25},{17,1},{25,9},{2,18},{10... | collective-permute-start | bytes 1990664 | tf_op jit(solution)/shard_map/ppermute | solution.py:34
  206.9 85.1 %collective-permute-start.40 = (f16[144,2304]{1,0:T(8,128)(2,1)}, f16[144,2304]{1,0:T(8,128)(2,1)}, u32[]{:S(2)}, u32[]{:S(2)}) collective-permute-start(f16[144,2304]{1,0:T(8,128)(2,1)} %fusion.18), channel_id=1, source_target_pairs={{0,16},{8,24},{16,0},{24,8},{1,17},{9,25},{17,1},{25,9},{2,18},{10... | collective-permute-start | bytes 1990664 | tf_op jit(solution)/shard_map/ppermute | solution.py:34
  208.9 42.9 %collective-permute-start.26 = (f16[128,2304]{1,0:T(8,128)(2,1)S(1)}, f16[128,2304]{1,0:T(8,128)(2,1)S(1)}, u32[]{:S(2)}, u32[]{:S(2)}) collective-permute-start(f16[128,2304]{1,0:T(8,128)(2,1)S(1)} %fusion.23), channel_id=1, source_target_pairs={{0,16},{8,24},{16,0},{24,8},{1,17},{9,25},{17,1},{25,9},{2,18},{10... | collective-permute-start | bytes 1769480 | tf_op jit(solution)/shard_map/ppermute | solution.py:34
  219.7 44.7 %collective-permute-start.14 = (f16[128,2304]{1,0:T(8,128)(2,1)S(1)}, f16[128,2304]{1,0:T(8,128)(2,1)S(1)}, u32[]{:S(2)}, u32[]{:S(2)}) collective-permute-start(f16[128,2304]{1,0:T(8,128)(2,1)S(1)} %fusion.21), channel_id=1, source_target_pairs={{0,16},{8,24},{16,0},{24,8},{1,17},{9,25},{17,1},{25,9},{2,18},{10... | collective-permute-start | bytes 1769480 | tf_op jit(solution)/shard_map/ppermute | solution.py:34
  232.5 44.5 %collective-permute-start.24 = (f16[128,2304]{1,0:T(8,128)(2,1)S(1)}, f16[128,2304]{1,0:T(8,128)(2,1)S(1)}, u32[]{:S(2)}, u32[]{:S(2)}) collective-permute-start(f16[128,2304]{1,0:T(8,128)(2,1)S(1)} %fusion.22), channel_id=1, source_target_pairs={{0,16},{8,24},{16,0},{24,8},{1,17},{9,25},{17,1},{25,9},{2,18},{10... | collective-permute-start | bytes 1769480 | tf_op jit(solution)/shard_map/ppermute | solution.py:34
  251.8 40.2 %collective-permute-start.48 = (f16[144,2304]{1,0:T(8,128)(2,1)S(1)}, f16[144,2304]{1,0:T(8,128)(2,1)S(1)}, u32[]{:S(2)}, u32[]{:S(2)}) collective-permute-start(f16[144,2304]{1,0:T(8,128)(2,1)S(1)} %fusion.19), channel_id=1, source_target_pairs={{0,16},{8,24},{16,0},{24,8},{1,17},{9,25},{17,1},{25,9},{2,18},{10... | collective-permute-start | bytes 1990664 | tf_op jit(solution)/shard_map/ppermute | solution.py:34
  279.9 44.2 %collective-permute-start.27 = (bf16[128,2304]{1,0:T(8,128)(2,1)S(1)}, bf16[128,2304]{1,0:T(8,128)(2,1)}, u32[]{:S(2)}, u32[]{:S(2)}) collective-permute-start(bf16[128,2304]{1,0:T(8,128)(2,1)S(1)} %get-tuple-element.93.refs_0_), channel_id=1, source_target_pairs={{0,16},{8,24},{16,0},{24,8},{1,17},{9,25},{17,1},{25,9},{2,18},{10... | collective-permute-start | bytes 1769480 | tf_op jit(solution)/shard_map/ppermute | solution.py:34
  291.3 32.8 %collective-permute-start.28 = (bf16[128,2304]{1,0:T(8,128)(2,1)S(1)}, bf16[128,2304]{1,0:T(8,128)(2,1)}, u32[]{:S(2)}, u32[]{:S(2)}) collective-permute-start(bf16[128,2304]{1,0:T(8,128)(2,1)S(1)} %get-tuple-element.95.refs_2_), channel_id=1, source_target_pairs={{0,16},{8,24},{16,0},{24,8},{1,17},{9,25},{17,1},{25,9},{2,18},{10... | collective-permute-start | bytes 1769480 | tf_op jit(solution)/shard_map/ppermute | solution.py:34
  295.6 17.8 %collective-permute-start.58 = (bf16[144]{0:T(256)(128)(2,1)S(1)}, bf16[144]{0:T(256)(128)(2,1)S(1)}, u32[]{:S(2)}, u32[]{:S(2)}) collective-permute-start(bf16[144]{0:T(256)(128)(2,1)S(1)} %get-tuple-element.90), channel_id=1, source_target_pairs={{0,16},{8,24},{16,0},{24,8},{1,17},{9,25},{17,1},{25,9},{2,18},{10... | collective-permute-start | bytes 872 | tf_op jit(solution)/shard_map/ppermute | solution.py:34
  313.6 29.3 %collective-permute-start.50 = (bf16[144,2304]{1,0:T(8,128)(2,1)S(1)}, bf16[144,2304]{1,0:T(8,128)(2,1)S(1)}, u32[]{:S(2)}, u32[]{:S(2)}) collective-permute-start(bf16[144,2304]{1,0:T(8,128)(2,1)S(1)} %get-tuple-element.91.refs_0_), channel_id=1, source_target_pairs={{0,16},{8,24},{16,0},{24,8},{1,17},{9,25},{17,1},{25,9},{2,18},{10... | collective-permute-start | bytes 1990664 | tf_op jit(solution)/shard_map/ppermute | solution.py:34
  313.6 30.0 %collective-permute-start.51 = (bf16[144,2304]{1,0:T(8,128)(2,1)S(1)}, bf16[144,2304]{1,0:T(8,128)(2,1)}, u32[]{:S(2)}, u32[]{:S(2)}) collective-permute-start(bf16[144,2304]{1,0:T(8,128)(2,1)S(1)} %get-tuple-element.94.refs_2_), channel_id=1, source_target_pairs={{0,16},{8,24},{16,0},{24,8},{1,17},{9,25},{17,1},{25,9},{2,18},{10... | collective-permute-start | bytes 1990664 | tf_op jit(solution)/shard_map/ppermute | solution.py:34
  317.2 62.8 %collective-permute-start.60 = (f32[1,68]{1,0:T(1,128)S(1)}, f32[1,68]{1,0:T(1,128)S(1)}, u32[]{:S(2)}, u32[]{:S(2)}) collective-permute-start(f32[1,68]{1,0:T(1,128)S(1)} %get-tuple-element.133), channel_id=1, source_target_pairs={{0,6},{1,7},{2,0},{3,1},{4,2},{5,3},{6,4},{7,5},{8,14},{9,15},{10,... | collective-permute-start | bytes 824 | tf_op jit(solution)/shard_map/ppermute | solution.py:44
  324.1 57.1 %collective-permute-start.61 = (f32[1,68]{1,0:T(1,128)S(1)}, f32[1,68]{1,0:T(1,128)S(1)}, u32[]{:S(2)}, u32[]{:S(2)}) collective-permute-start(f32[1,68]{1,0:T(1,128)S(1)} %get-tuple-element.132), channel_id=1, source_target_pairs={{0,4},{1,5},{2,6},{3,7},{4,0},{5,1},{6,2},{7,3},{8,12},{9,13},{10,... | collective-permute-start | bytes 824 | tf_op jit(solution)/shard_map/ppermute | solution.py:44
  324.1 57.3 %collective-permute-start.62 = (f32[1,68]{1,0:T(1,128)S(1)}, f32[1,68]{1,0:T(1,128)S(1)}, u32[]{:S(2)}, u32[]{:S(2)}) collective-permute-start(f32[1,68]{1,0:T(1,128)S(1)} %get-tuple-element.131), channel_id=1, source_target_pairs={{0,2},{1,3},{2,4},{3,5},{4,6},{5,7},{6,0},{7,1},{8,10},{9,11},{10,... | collective-permute-start | bytes 824 | tf_op jit(solution)/shard_map/ppermute | solution.py:44
  342.9 20.5 %collective-permute-start.64 = (bf16[128,1536]{1,0:T(8,128)(2,1)S(1)}, bf16[128,1536]{1,0:T(8,128)(2,1)S(1)}, u32[]{:S(2)}, u32[]{:S(2)}) collective-permute-start(bf16[128,1536]{1,0:T(8,128)(2,1)S(1)} %dynamic-slice_bitcast_fusion.2), channel_id=1, source_target_pairs={{0,1},{1,0},{2,3},{3,2},{4,5},{5,4},{6,7},{7,6},{8,9},{9,8},{10,11... | collective-permute-start | bytes 1179656 | tf_op jit(solution)/shard_map/ppermute | solution.py:50
  343.6 20.7 %collective-permute-start.29 = (bf16[128,1536]{1,0:T(8,128)(2,1)S(1)}, bf16[128,1536]{1,0:T(8,128)(2,1)S(1)}, u32[]{:S(2)}, u32[]{:S(2)}) collective-permute-start(bf16[128,1536]{1,0:T(8,128)(2,1)S(1)} %dynamic-slice_bitcast_fusion.3), channel_id=1, source_target_pairs={{0,1},{1,0},{2,3},{3,2},{4,5},{5,4},{6,7},{7,6},{8,9},{9,8},{10,11... | collective-permute-start | bytes 1179656 | tf_op jit(solution)/shard_map/ppermute | solution.py:50
  (90 other events, 1068.4 us)

commit v2 on v1

v2 whole, which is shorter than its diff:
```python
import jax
import jax.numpy as jnp
from jax import lax
from jax.experimental import pallas as pl
from jax.experimental.pallas import tpu as pltpu
from jax.sharding import PartitionSpec as P

highest = lax.Precision.HIGHEST
norm_epsilon = 1e-06
f32 = jnp.float32
bf16 = jnp.bfloat16
vmem_limit = 48 * 2**20

in_scale = 32.0
out_scale = 4.0


class Layout:
    def __init__(self, window_experts):
        self.seq = lax.axis_size("seq")
        self.chips = self.seq // 2
        self.spread = lax.axis_size("expert")
        self.experts = window_experts
        self.slices = self.spread // window_experts
        here = lax.axis_index("seq")
        self.chip, self.core = here // 2, here % 2
        self.expert = lax.axis_index("expert") // self.slices

    def swap_core(self, v):
        return lax.ppermute(v, "seq", [(i, i ^ 1) for i in range(self.seq)])

    def turn_chip(self, v, p):
        n = self.chips
        return lax.ppermute(
            v, "seq", [(i, ((i // 2 + p) % n) * 2 + i % 2) for i in range(self.seq)]
        )

    def later_chip(self, v, p):
        pairs = [(i, i + 2 * p) for i in range(self.seq) if 0 <= i + 2 * p < self.seq]
        return lax.ppermute(v, "seq", pairs)

    def between_experts(self, v):
        n, m = self.experts, self.slices
        groups = [[q * m + j for q in range(n)] for j in range(m)]
        return lax.all_to_all(v, "expert", 0, 0, axis_index_groups=groups, tiled=True)

    def turn_expert(self, v, d):
        n, m = self.experts, self.slices
        return lax.ppermute(
            v, "expert", [(i, ((i // m + d) % n) * m + i % m) for i in range(self.spread)]
        )

    def turn_slice(self, v, k):
        m = self.slices
        return lax.ppermute(
            v, "expert", [(i, (i // m) * m + (i % m + k) % m) for i in range(self.spread)]
        )


def params(**kw):
    return pltpu.CompilerParams(vmem_limit_bytes=vmem_limit, **kw)


short = pl.CostEstimate(flops=1000, bytes_accessed=1000, transcendentals=0)


def tile_of(size):
    return 768 if size % 768 == 0 else size


def any_spec():
    return pl.BlockSpec(memory_space=pl.ANY)


def pick_rows(groups, rank, first, count, padded, after):
    experts = rank.shape[0]
    halves, tokens, width = groups[0].shape
    total = tokens * len(groups)

    def body(rank_ref, *refs):
        group_refs, out_ref = refs[: len(groups)], refs[-1]
        slot = lax.broadcasted_iota(jnp.int32, (padded, total), 0)
        wanted = jnp.where(slot < count, slot + first, -2)
        for h in range(halves):
            rows = jnp.concatenate([g[h] for g in group_refs], axis=0)
            for d in range(experts):
                pick = (rank_ref[d : d + 1, :] == wanted).astype(bf16)
                out_ref[d, h] = jnp.dot(pick, rows, preferred_element_type=f32).astype(bf16)

    vmem = pl.BlockSpec(memory_space=pltpu.VMEM)
    return pl.pallas_call(
        body,
        in_specs=[vmem] * (1 + len(groups)) + [any_spec()] * len(after),
        out_specs=vmem,
        out_shape=jax.ShapeDtypeStruct((experts, halves, padded, width), bf16),
        compiler_params=params(),
        cost_estimate=short,
        name="pick_rows",
    )(rank, *groups, *after)


def project(jobs, rows, chip, chips, after):
    experts, halves, padded, width = jobs[0][0][0].shape
    arrays_each = len(jobs[0][0])
    count = arrays_each * experts
    part = rows * count // chips
    per_part = count // chips
    units = jobs[0][1][0][0].shape[1]
    tile = tile_of(units)
    arrays = [v for job in jobs for v in job[0]]
    mats = [half for job in jobs for pair in job[1] for half in pair]
    owner = [j for j, job in enumerate(jobs) for _ in job[1]]
    mat_count = len(owner)

    def body(chip_ref, *refs):
        array_refs = refs[: len(arrays)]
        mat_refs = refs[len(arrays) : len(arrays) + len(mats)]
        keep_ref, send_ref, held = refs[-3:]

        def left(job, h):
            found = [
                r[:, h].reshape(experts * padded, width)
                for r in array_refs[job * arrays_each : (job + 1) * arrays_each]
            ]
            return found[0] if len(found) == 1 else jnp.concatenate(found, axis=0)

        for m in range(mat_count):
            result = jnp.dot(
                left(owner[m], 0), mat_refs[2 * m][...], preferred_element_type=f32
            )
            result = result + jnp.dot(
                left(owner[m], 1), mat_refs[2 * m + 1][...], preferred_element_type=f32
            )
            held[...] = result.reshape(chips, per_part * padded, tile)
            for p in range(chips):
                value = held[(chip_ref[0] + p) % chips]
                for b in range(per_part):
                    piece = value[b * padded : b * padded + rows]
                    if p == 0:
                        keep_ref[m, b * rows : (b + 1) * rows] = piece
                    else:
                        send_ref[p - 1, m, b * rows : (b + 1) * rows] = piece

    mat_spec = pl.BlockSpec((width, tile), lambda i: (0, i))
    return pl.pallas_call(
        body,
        grid=(units // tile,),
        in_specs=[pl.BlockSpec(memory_space=pltpu.SMEM)]
        + [pl.BlockSpec(arrays[0].shape, lambda i: (0, 0, 0, 0))] * len(arrays)
        + [mat_spec] * len(mats)
        + [any_spec()] * len(after),
        out_specs=[
            pl.BlockSpec((mat_count, part, tile), lambda i: (0, 0, i)),
            pl.BlockSpec((chips - 1, mat_count, part, tile), lambda i: (0, 0, 0, i)),
        ],
        out_shape=[
            jax.ShapeDtypeStruct((mat_count, part, units), f32),
            jax.ShapeDtypeStruct((chips - 1, mat_count, part, units), f32),
        ],
        scratch_shapes=[pltpu.VMEM((chips, per_part * padded, tile), f32)],
        compiler_params=params(),
        cost_estimate=short,
        name="project",
    )(chip, *arrays, *mats, *after)


def project_back(groups, mats, chip, rows, after):
    chips = len(groups[0])
    units = groups[0][0].shape[2]
    width = mats[0][0].shape[0]
    halves = len(mats)
    tile = tile_of(width)
    steps = width // tile
    parts = [v for group in groups for v in group]
    sizes = [group[0].shape[1] for group in groups]
    rooms = [-(-size // 16) * 16 for size in sizes]
    bases = [chips * sum(rooms[:g]) for g in range(len(groups))]
    total = chips * sum(rooms)
    counts = [size * chips // rows for size in sizes]

    def body(chip_ref, *refs):
        part_refs = refs[: len(parts)]
        mat_refs = refs[len(parts) : len(parts) + 2 * halves]
        out_refs = refs[-2 - len(groups) : -2]
        gate_all, up_all = refs[-2:]
        step = pl.program_id(0)

        @pl.when(step == 0)
        def _():
            for g, size in enumerate(sizes):
                for r in range(chips):
                    place = (chip_ref[0] + r) % chips
                    start = pl.multiple_of(bases[g] + place * rooms[g], 16)
                    gate_all[pl.ds(start, size)] = part_refs[g * chips + r][0]
                    up_all[pl.ds(start, size)] = part_refs[g * chips + r][1]

        def multiply(gate_mat_ref, up_mat_ref):
            contract = (((1,), (1,)), ((), ()))
            result = lax.dot_general(
                gate_all[...], gate_mat_ref[...], contract, preferred_element_type=f32
            )
            result = result + lax.dot_general(
                up_all[...], up_mat_ref[...], contract, preferred_element_type=f32
            )
            for g, count in enumerate(counts):
                per_part = count // chips
                for b in range(count):
                    start = bases[g] + b // per_part * rooms[g] + b % per_part * rows
                    out_refs[g][b, 0] = result[start : start + rows].astype(bf16)

        if halves == 1:
            multiply(*mat_refs)
        else:
            for h in range(halves):

                @pl.when(step // steps == h)
                def _():
                    multiply(mat_refs[2 * h], mat_refs[2 * h + 1])

    def mat_spec(h):
        return pl.BlockSpec((tile, units), lambda i: (jnp.clip(i - h * steps, 0, steps - 1), 0))

    def row_spec(count):
        return pl.BlockSpec((count, 1, rows, tile), lambda i: (0, i // steps, 0, i % steps))

    return pl.pallas_call(
        body,
        grid=(halves * steps,),
        in_specs=[pl.BlockSpec(memory_space=pltpu.SMEM)]
        + [pl.BlockSpec(v.shape, lambda i: (0, 0, 0)) for v in parts]
        + [mat_spec(h) for h in range(halves) for _ in range(2)]
        + [any_spec()] * len(after),
        out_specs=[row_spec(count) for count in counts],
        out_shape=[
            jax.ShapeDtypeStruct((count, halves, rows, width), bf16) for count in counts
        ],
        scratch_shapes=[pltpu.VMEM((total, units), bf16)] * 2,
        compiler_params=params(),
        cost_estimate=short,
        name="project_back",
    )(chip, *parts, *[m for pair in mats for m in pair], *after)


def combine(returned, scores, rank, gates, router, firsts, groups):
    experts, _, _, width = returned[0][0].shape
    counts = [v.shape[2] for v, _ in returned]
    total = rank.shape[0]
    tokens = total // groups

    def body(*refs):
        returned_refs = refs[: len(returned)]
        score_ref, rank_ref, gate_ref, router_ref = refs[len(returned) : len(returned) + 4]
        out_refs = refs[len(returned) + 4 :]
        acc = jnp.zeros((total, width), f32)
        picked = []
        slots = lax.broadcasted_iota(jnp.int32, (total, score_ref.shape[1]), 1)
        for d in range(experts):
            hit = rank_ref[:, d : d + 1] == slots
            picked.append(
                jnp.sum(jnp.where(hit, score_ref[d : d + 1, :], 0.0), axis=1, keepdims=True)
            )
        mean = sum(gate_ref[:, d : d + 1] * picked[d] for d in range(experts))
        for d in range(experts):
            grad = gate_ref[:, d : d + 1] * (picked[d] - mean)
            acc = acc + grad * router_ref[d : d + 1, :]
        for c, rows_ref in enumerate(returned_refs):
            for d in range(experts):
                value = rows_ref[d, 0]
                slot = lax.broadcasted_iota(jnp.int32, (total, value.shape[0]), 1) + firsts[c]
                weight = jnp.where(rank_ref[:, d : d + 1] == slot, gate_ref[:, d : d + 1], 0.0)
                high = weight.astype(bf16)
                low = (weight - high.astype(f32)).astype(bf16)
                acc = acc + jnp.dot(high, value, preferred_element_type=f32)
                acc = acc + jnp.dot(low, value, preferred_element_type=f32)
        for g in range(groups):
            out_refs[g][...] = acc[g * tokens : (g + 1) * tokens].astype(bf16)

    row_count = experts * sum(counts)

    def half_spec(count, h):
        return pl.BlockSpec((experts, 1, count, width), lambda i: (0, h, 0, 0))

    def whole_spec(v):
        return pl.BlockSpec(v.shape, lambda i: (0, 0))

    return pl.pallas_call(
        body,
        grid=(1,),
        in_specs=[half_spec(v.shape[2], h) for v, h in returned]
        + [whole_spec(v) for v in (scores, rank, gates, router)],
        out_specs=[pl.BlockSpec((tokens, width), lambda i: (0, 0))] * groups,
        out_shape=[jax.ShapeDtypeStruct((tokens, width), bf16)] * groups,
        compiler_params=params(),
        cost_estimate=short,
        name="combine",
    )(*[v for v, _ in returned], scores, rank, gates, router)


def split3(v):
    high = v.astype(bf16)
    rest = v - high.astype(f32)
    middle = rest.astype(bf16)
    return high, middle, (rest - middle.astype(f32)).astype(bf16)


def dot_left(a, b, dims):
    contract = (((dims[0],), (dims[1],)), ((), ()))
    return sum(lax.dot_general(t, b, contract, preferred_element_type=f32) for t in split3(a))


def dot_right(a, b, dims):
    contract = (((dims[0],), (dims[1],)), ((), ()))
    return sum(lax.dot_general(a, t, contract, preferred_element_type=f32) for t in split3(b))


def dot_full(a, b, dims):
    contract = (((dims[0],), (dims[1],)), ((), ()))
    return lax.dot_general(a, b, contract, precision=highest, preferred_element_type=f32)


def head_specs(rollouts, block, head):
    rows = pl.BlockSpec((rollouts, block, head), lambda h: (0, 0, h))
    state = pl.BlockSpec((rollouts, 1, head, head), lambda h: (0, h, 0, 0))
    return pl.BlockSpec(memory_space=pltpu.SMEM), rows, state


def key_value_state(key_rows, value_rows, decay_rate, after):
    rollouts, block, width = key_rows.shape
    heads = decay_rate.shape[0]
    head = width // heads
    smem, rows, state = head_specs(rollouts, block, head)

    def body(rate_ref, key_ref, value_ref, *refs):
        rate = rate_ref[pl.program_id(0)]
        offset = lax.broadcasted_iota(jnp.int32, (block, 1), 0).astype(f32)
        tail = jnp.exp(-rate * (block - 1.0 - offset))
        for r in range(rollouts):
            decayed = key_ref[r].astype(f32) * tail
            refs[-1][r, 0] = dot_left(decayed, value_ref[r], (0, 0))

    return pl.pallas_call(
        body,
        grid=(heads,),
        in_specs=[smem, rows, rows] + [any_spec()] * len(after),
        out_specs=state,
        out_shape=jax.ShapeDtypeStruct((rollouts, heads, head, head), f32),
        compiler_params=params(),
        cost_estimate=short,
        name="key_value_state",
    )(decay_rate, key_rows, value_rows, *after)


def local_grads(
    queries, key_rows, value_rows, attn_probe, gain, coeff, decay_rate, state, after
):
    rollouts, block, width = queries.shape
    heads = decay_rate.shape[0]
    head = width // heads
    smem, rows, state_spec = head_specs(rollouts, block, head)

    def body(rate_ref, q_ref, k_ref, v_ref, probe_ref, gain_ref, coeff_ref, state_ref, *refs):
        grad_q_ref, grad_k_ref, grad_v_ref, summary_ref = refs[-4:]
        rate = rate_ref[pl.program_id(0)]
        offset = lax.broadcasted_iota(jnp.int32, (block, 1), 0).astype(f32)
        lead = jnp.exp(-rate * (offset + 1.0))
        tail = jnp.exp(-rate * offset)
        line = lax.broadcasted_iota(jnp.int32, (block, block), 0)
        column = lax.broadcasted_iota(jnp.int32, (block, block), 1)
        distance = (line - column).astype(f32)
        within = jnp.where(line >= column, jnp.exp(-rate * jnp.maximum(distance, 0.0)), 0.0)
        for r in range(rollouts):
            query, key, value, before = q_ref[r], k_ref[r], v_ref[r], state_ref[r, 0]
            scores = lax.dot_general(
                query, key, (((1,), (1,)), ((), ())), preferred_element_type=f32
            )
            scores = scores * within
            output = dot_left(scores, value, (1, 0))
            output = output + lead * dot_right(query, before, (1, 0))
            inverse = lax.rsqrt(
                jnp.mean(output * output, axis=-1, keepdims=True) + norm_epsilon
            )
            scaled = gain_ref[...] * (coeff_ref[:, r : r + 1] * probe_ref[r].astype(f32))
            grad_out = inverse * scaled - output * inverse**3 * jnp.mean(
                scaled * output, axis=-1, keepdims=True
            )
            summary_ref[r, 0] = dot_right(query, tail * grad_out, (0, 0))
            product = dot_left(grad_out, value, (1, 1)) * within
            grad_q = dot_left(product, key, (1, 0))
            grad_q = grad_q + lead * dot_full(grad_out, before, (1, 1))
            grad_q_ref[r] = grad_q.astype(bf16)
            grad_k_ref[r] = dot_left(product, query, (0, 0))
            grad_v_ref[r] = dot_full(scores, grad_out, (0, 0))

    return pl.pallas_call(
        body,
        grid=(heads,),
        in_specs=[
            smem,
            rows,
            rows,
            rows,
            rows,
            pl.BlockSpec((1, head), lambda h: (0, h)),
            pl.BlockSpec((block, rollouts), lambda h: (0, 0)),
            state_spec,
        ]
        + [any_spec()] * len(after),
        out_specs=[rows, rows, rows, state_spec],
        out_shape=[
            jax.ShapeDtypeStruct(queries.shape, bf16),
            jax.ShapeDtypeStruct(queries.shape, f32),
            jax.ShapeDtypeStruct(queries.shape, f32),
            jax.ShapeDtypeStruct(state.shape, f32),
        ],
        compiler_params=params(),
        cost_estimate=short,
        name="local_grads",
    )(decay_rate, queries, key_rows, value_rows, attn_probe, gain, coeff, state, *after)


def later_grads(key_rows, value_rows, grad_k, grad_v, decay_rate, state, after):
    rollouts, block, width = key_rows.shape
    heads = decay_rate.shape[0]
    head = width // heads
    smem, rows, state_spec = head_specs(rollouts, block, head)

    def body(rate_ref, k_ref, v_ref, grad_k_ref, grad_v_ref, state_ref, *refs):
        out_k_ref, out_v_ref = refs[-2:]
        rate = rate_ref[pl.program_id(0)]
        offset = lax.broadcasted_iota(jnp.int32, (block, 1), 0).astype(f32)
        tail = jnp.exp(-rate * (block - offset))
        for r in range(rollouts):
            after_state = state_ref[r, 0]
            grad_k = grad_k_ref[r] + tail * dot_right(v_ref[r], after_state, (1, 1))
            grad_v = grad_v_ref[r] + tail * dot_right(k_ref[r], after_state, (1, 0))
            out_k_ref[r] = grad_k.astype(bf16)
            out_v_ref[r] = grad_v.astype(bf16)

    return pl.pallas_call(
        body,
        grid=(heads,),
        in_specs=[smem, rows, rows, rows, rows, state_spec] + [any_spec()] * len(after),
        out_specs=[rows, rows],
        out_shape=[jax.ShapeDtypeStruct(key_rows.shape, bf16)] * 2,
        compiler_params=params(),
        cost_estimate=short,
        name="later_grads",
    )(decay_rate, key_rows, value_rows, grad_k, grad_v, state, *after)


def carried(place, summary, decay_rate, block_size, direction):
    def block_decay(blocks):
        return jnp.exp(-decay_rate * (block_size * blocks)).reshape(1, -1, 1, 1)

    partner = place.swap_core(summary)
    first = (place.core == 0) if direction > 0 else (place.core == 1)
    one = block_decay(1)
    near = jnp.where(first, partner + one * summary, summary + one * partner)
    outside = jnp.zeros_like(summary)
    for p in range(1, place.chips):
        outside = outside + block_decay(2 * (p - 1)) * place.later_chip(near, direction * p)
    return jnp.where(first, outside, partner + one * outside)


def cut_features(v, scale, chip_core, chips, after):
    tokens, model_width = v.shape
    width = model_width // (2 * chips)

    def body(where_ref, v_ref, *refs):
        keep_ref, send_ref = refs[-2:]
        for p in range(chips):
            chip = (where_ref[0] + p) % chips
            for h in range(2):
                core = where_ref[1] if h == 0 else 1 - where_ref[1]
                start = pl.multiple_of((2 * chip + core) * width, 128)
                value = v_ref[:, pl.ds(start, width)]
                if scale is not None:
                    value = (refs[0][...] * value.astype(f32)).astype(bf16)
                if p == 0:
                    keep_ref[h] = value
                else:
                    send_ref[p - 1, h] = value

    vmem = pl.BlockSpec(memory_space=pltpu.VMEM)
    extra = [] if scale is None else [scale]
    return pl.pallas_call(
        body,
        in_specs=[pl.BlockSpec(memory_space=pltpu.SMEM), vmem]
        + [vmem] * len(extra)
        + [any_spec()] * len(after),
        out_specs=[vmem, vmem],
        out_shape=[
            jax.ShapeDtypeStruct((2, tokens, width), bf16),
            jax.ShapeDtypeStruct((chips - 1, 2, tokens, width), bf16),
        ],
        compiler_params=params(),
        cost_estimate=short,
        name="cut_features",
    )(chip_core, v, *extra, *after)


def expert_and_attention(
    place,
    hidden_in,
    moe_probe,
    router_weight,
    routes,
    gate_weight,
    up_weight,
    down_weight,
    coeff,
    queries,
    key_rows,
    value_rows,
    decay_rate,
    norm_gain,
    attn_probe,
):
    rollouts, positions, model_width = hidden_in.shape
    chips, experts, slices = place.chips, place.experts, place.slices
    tokens = rollouts * positions
    width = gate_weight.shape[1]
    own_mats = (gate_weight[0], up_weight[0], down_weight[0])

    hidden = hidden_in.reshape(tokens, model_width)
    local_coeff = lax.dynamic_slice_in_dim(
        coeff, lax.axis_index("expert") * positions, positions, 1
    )
    chip_here = place.chip.reshape(1).astype(jnp.int32)
    chip_core = jnp.stack([place.chip, place.core]).astype(jnp.int32)
    last = []

    def ordered(kernel, *args, needs=()):
        result = kernel(*args, (*last, *needs))
        last[:] = [result[0] if isinstance(result, (list, tuple)) else result]
        return result

    def across(v, scale):
        keep, send = ordered(cut_features, v, scale, chip_core, chips)
        return [keep] + [place.turn_chip(send[p - 1], p) for p in range(1, chips)]

    hidden_groups = across(hidden, None)
    grad_groups = across(
        moe_probe.reshape(tokens, model_width), local_coeff.reshape(tokens, 1)
    )

    def halves_of(v, p):
        chip = (place.chip + p) % chips
        return jnp.stack(
            [
                lax.dynamic_slice_in_dim(v, (2 * chip + core) * width, width, 1)
                for core in (place.core, 1 - place.core)
            ]
        )

    logits = jnp.dot(hidden, router_weight, preferred_element_type=f32)
    flat_routes = routes.reshape(tokens, -1)
    onehot = (flat_routes[:, :, None] == jnp.arange(experts, dtype=jnp.int32)).astype(f32)
    chosen = jnp.sum(onehot * logits[:, None, :], axis=-1)
    exponent = jnp.exp(chosen)
    gate = exponent / jnp.sum(exponent, axis=-1, keepdims=True)
    facts = jnp.concatenate(
        [onehot.sum(axis=1), jnp.sum(onehot * gate[:, :, None], axis=1)], axis=1
    )
    all_facts = [facts] + [place.turn_chip(facts, p) for p in range(1, chips)]

    pairs = [(m, place.swap_core(m)) for m in own_mats[:2]]

    fact_stack = jnp.stack(all_facts)
    member, gates = fact_stack[:, :, :experts], fact_stack[:, :, experts:]
    whose = (place.chip - jnp.arange(chips)) % chips
    earlier = (whose[None, :] < whose[:, None]).astype(f32)
    offset = jnp.sum(earlier[:, :, None] * member.sum(axis=1)[None], axis=1)
    step = jnp.arange(tokens)
    below = (step[:, None] > step[None, :]).astype(f32)
    rank = jnp.einsum("ts,gse->gte", below, member) + offset[:, None, :]
    rank = jnp.where(member > 0, rank, -1.0).astype(jnp.int32)
    rank = rank.reshape(chips * tokens, experts)
    gates = gates.reshape(chips * tokens, experts)
    rank_lanes = rank.T

    most = chips * rollouts * (positions // 2 + 1)
    small = max(16, most // 2 // 16 * 16)
    chunks = [(0, small), (small, most - small)]
    def dispatch(groups, first, count, needs=()):
        padded = -(-count // 8) * 8
        return ordered(pick_rows, groups, rank_lanes, first, count, padded, needs=needs)

    def behind(v, *others):
        return lax.optimization_barrier((v, *others))[0] if others else v

    def relay(mine):
        return [place.turn_slice(mine, k) for k in range(1, slices)]

    def partial(arrays, count, mats, scale, needs=()):
        arrays = [behind(v, *needs) for v in arrays]
        keep, send = ordered(project, [(arrays, mats)], count, chip_here, chips)
        ready = (send * scale).astype(jnp.float16)
        arrived = [place.turn_chip(ready[p - 1], p) for p in range(1, chips)]
        return keep, arrived, scale

    def settle(part):
        keep, arrived, scale = part
        return keep + sum(v.astype(f32) for v in arrived) * (1.0 / scale)

    def ring(v):
        found = [v] + [None] * (chips - 1)
        for p in range(1, chips):
            found[chips - p] = place.turn_chip(v, p)
        return found

    def middle(inner, outer):
        pre_gate, pre_up = settle(inner)
        unit_grad = settle(outer)[0]
        sigmoid_gate = jax.nn.sigmoid(pre_gate)
        activated = pre_gate * sigmoid_gate
        units = activated * pre_up
        score = jnp.sum(units * unit_grad, axis=-1).astype(bf16)
        slope = pre_up * sigmoid_gate * (1.0 + pre_gate * (1.0 - sigmoid_gate))
        which = jnp.arange(2).reshape(2, 1, 1)
        both = (unit_grad * jnp.where(which == 0, slope, activated)).astype(bf16)
        return ring(both), score

    def back(groups, halves, count, needs=()):
        mats = [(pairs[0][h], pairs[1][h]) for h in halves]
        return ordered(project_back, groups, mats, chip_here, count, needs=needs)

    def to_slices(dx):
        return [
            place.turn_slice(dx[(k - 1) * experts : k * experts], -k) for k in range(1, slices)
        ]

    (first_a, count_a), (first_b, count_b) = chunks

    block = queries.shape[1]
    def held(part, kernel_result):
        keep, arrived, scale = part
        return keep, [behind(v, kernel_result) for v in arrived], scale

    summary = ordered(key_value_state, key_rows, value_rows, decay_rate)
    state_before = carried(place, summary, decay_rate, block, 1)
    picked_hidden_a = dispatch(hidden_groups, first_a, count_a)
    picked_hidden_b = dispatch(hidden_groups, first_b, count_b)
    picked_grads_a = dispatch(grad_groups, first_a, count_a, [state_before])
    hidden_a = place.between_experts(behind(picked_hidden_a, picked_grads_a))
    picked_grads_b = dispatch(
        grad_groups, first_b, count_b, [pairs[0][1], pairs[1][1]]
    )
    grad_queries, local_k, local_v, summary = ordered(
        local_grads,
        queries,
        key_rows,
        value_rows,
        attn_probe,
        norm_gain.reshape(1, -1),
        coeff.T,
        decay_rate,
        state_before,
    )
    state_after = carried(place, summary, decay_rate, block, -1)
    far_hidden_a = relay(hidden_a)
    pairs.append((own_mats[2], place.swap_core(behind(own_mats[2], picked_grads_b))))
    inner_own_a = partial([hidden_a], count_a, pairs[:2], in_scale, [state_after])
    grads_a = place.between_experts(behind(picked_grads_a, hidden_a))
    far_grads_a = relay(grads_a)
    outer_own_a = partial([grads_a], count_a, pairs[2:], out_scale)
    grad_keys, grad_values = ordered(
        later_grads, key_rows, value_rows, local_k, local_v, decay_rate, state_after
    )
    hidden_b = place.between_experts(behind(picked_hidden_b, grads_a, inner_own_a[0]))
    own_a, score_own_a = middle(inner_own_a, outer_own_a)
    inner_far_a = partial(far_hidden_a, count_a, pairs[:2], in_scale, own_a[:1])
    outer_far_a = partial(far_grads_a, count_a, pairs[2:], out_scale, own_a[1:])
    far_hidden_b = relay(behind(hidden_b, outer_far_a[0]))
    grads_b = place.between_experts(behind(picked_grads_b, hidden_b, outer_far_a[0]))
    inner_own_b = partial([hidden_b], count_b, pairs[:2], in_scale, inner_far_a[1])
    far_grads_b = relay(grads_b)
    far_a, score_far_a = middle(
        held(inner_far_a, inner_own_b[0]), held(outer_far_a, inner_own_b[0])
    )
    inner_far_b = partial(far_hidden_b, count_b, pairs[:2], in_scale, far_a[:1])
    outer_own_b = partial([grads_b], count_b, pairs[2:], out_scale)
    dx_own_a, dx_far_a = back([own_a, far_a], (0, 1), count_a)
    outer_far_b = partial(far_grads_b, count_b, pairs[2:], out_scale, inner_own_b[1])
    far_b, score_far_b = middle(inner_far_b, outer_far_b)
    own_b, score_own_b = middle(held(inner_own_b, far_b[0]), held(outer_own_b, far_b[0]))
    from_far_a = to_slices(dx_far_a)
    total_a = dx_own_a.astype(f32) + sum(
        behind(v, own_b[1]).astype(f32) for v in from_far_a
    )
    home_a = place.between_experts(total_a.astype(bf16))
    from_far_b = [to_slices(back([far_b], (h,), count_b)[0]) for h in range(2)]
    (dx_own_b,) = back([own_b], (0, 1), count_b)
    total_b = dx_own_b.astype(f32) + sum(
        behind(jnp.concatenate(halves, axis=1), home_a).astype(f32) for halves in zip(*from_far_b)
    )
    home_b = place.between_experts(total_b.astype(bf16))

    kinds = [score_own_a, score_far_a, score_own_b, score_far_b]
    sizes = [v.shape[0] for v in kinds]
    every = jnp.stack(ring(behind(jnp.concatenate(kinds), *far_b)))
    every = jnp.take(every, (jnp.arange(chips) - place.chip) % chips, axis=0)
    split, at = [], 0
    for size in sizes:
        split.append(every[:, at : at + size].reshape(chips * size))
        at += size
    near = [
        v.reshape(experts, count) for v, count in ((split[0], count_a), (split[2], count_b))
    ]
    beyond = [
        v.reshape(slices - 1, experts, count)
        for v, count in ((split[1], count_a), (split[3], count_b))
    ]
    score_rows = jnp.concatenate(near, axis=1).astype(f32)
    beyond = jnp.concatenate(beyond, axis=2)
    for k in range(1, slices):
        score_rows = score_rows + place.turn_slice(beyond[k - 1], -k).astype(f32)
    turned = [score_rows] + [place.turn_expert(score_rows, d) for d in range(1, experts)]
    turned = lax.dynamic_index_in_dim(jnp.stack(turned), place.expert, 1, keepdims=False)
    source = (place.expert - jnp.arange(experts)) % experts
    score_home = jnp.take(turned, source, axis=0)

    router_rows = halves_of(router_weight.T.astype(f32), 0)
    result = jnp.zeros((tokens, model_width), bf16)
    for h in range(2):
        groups = combine(
            [(home_a, h), (home_b, h)],
            score_home,
            rank,
            gates,
            router_rows[h],
            [first_a, first_b],
            chips,
        )
        core = place.core if h == 0 else 1 - place.core
        for g in range(chips):
            part = groups[g] if g == 0 else place.turn_chip(groups[g], -g)
            chip = (place.chip + g) % chips
            result = lax.dynamic_update_slice_in_dim(result, part, (2 * chip + core) * width, 1)
    grad_hidden = result.reshape(rollouts, positions, model_width)
    return grad_queries, grad_keys, grad_values, grad_hidden


def on_device(
    queries,
    key_rows,
    value_rows,
    decay_rate,
    norm_gain,
    attn_probe,
    hidden_in,
    moe_probe,
    router_weight,
    routes,
    gate_weight,
    up_weight,
    down_weight,
    rollout_logprob,
    trainer_logprob,
    advantage,
    clip_low,
    clip_high,
):
    place = Layout(router_weight.shape[1])
    importance = jnp.exp(trainer_logprob - rollout_logprob)
    clipped = jnp.minimum(jnp.maximum(importance, clip_low[0]), clip_high[0])
    coeff = -(clipped * advantage) / queries.shape[0]
    objective = coeff * trainer_logprob
    grads = expert_and_attention(
        place,
        hidden_in,
        moe_probe,
        router_weight,
        routes,
        gate_weight,
        up_weight,
        down_weight,
        coeff,
        queries,
        key_rows,
        value_rows,
        decay_rate,
        norm_gain,
        attn_probe,
    )
    return (objective, *grads)


def solution(mesh):
    in_specs = (
        P(None, "seq", "expert"),
        P(None, "seq", "expert"),
        P(None, "seq", "expert"),
        P("expert"),
        P("expert"),
        P(None, "seq", "expert"),
        P(None, ("seq", "expert"), None),
        P(None, ("seq", "expert"), None),
        P(),
        P(None, ("seq", "expert"), None),
        P("expert", "seq", None),
        P("expert", "seq", None),
        P("expert", "seq", None),
        P(None, "seq"),
        P(None, "seq"),
        P(None, "seq"),
        P(),
        P(),
    )
    out_specs = (
        P(None, "seq"),
        P(None, "seq", "expert"),
        P(None, "seq", "expert"),
        P(None, "seq", "expert"),
        P(None, ("seq", "expert"), None),
    )
    return jax.shard_map(
        on_device, mesh=mesh, in_specs=in_specs, out_specs=out_specs, check_vma=False
    )
```

time: 416 us -> 355 us (0.85)
  waiting for transfers between devices: 150 us -> 73.3 us
  starting transfers between devices: 110 us -> 65.5 us
  Pallas kernels: 109 us -> 147 us
  blocking collectives: 0 us -> 25.5 us
  matrix products: 15.7 us -> 1.53 us
  local copies, waits for them, and re-layouts: 10.1 us -> 17 us
  other arithmetic: 15.4 us -> 20.9 us
    ppermute x27 -> x3, starting transfers between devices: 68.8 us -> 5.85 us  [turn_expert(): lax.ppermute(v, 'expert', [(i, (i // m + d) % n * m + i % m) for i in ran...]
    ppermute x27 -> x3, waiting for transfers between devices: 48.3 us -> 5.36 us  [turn_expert(): lax.ppermute(v, 'expert', [(i, (i // m + d) % n * m + i % m) for i in ran...]
    pallas_call x10 -> x15, Pallas kernels: 43.1 us -> 72.7 us  [the longest x4 52.2 us: project_back(): pl.pallas_call(body, grid=(halves * steps,), in_specs=[pl.BlockSpec(memor...]
    ppermute x22 -> x8, waiting for transfers between devices: 30.1 us -> 1.96 us  [turn_slice(): lax.ppermute(v, 'expert', [(i, i // m * m + (i % m + k) % m) for i in ran...]
    all_to_all x0 -> x1, blocking collectives: none -> 25.5 us  [between_experts(): lax.all_to_all(v, 'expert', 0, 0, axis_index_groups=groups, tiled=True)]
    all_to_all x0 -> x5, starting transfers between devices: none -> 21.3 us  [between_experts(): lax.all_to_all(v, 'expert', 0, 0, axis_index_groups=groups, tiled=True)]
    ppermute x17 -> x18, waiting for transfers between devices: 66.3 us -> 48.8 us  [turn_chip(): lax.ppermute(v, 'seq', [(i, (i // 2 + p) % n * 2 + i % 2) for i in range(...]
    dot_general x14 -> x2, matrix products: 15.7 us -> 1.53 us  [the longest x1 1.44 us: expert_and_attention(): logits = jnp.dot(hidden, router_weight, preferred_element_type=f32)]
  transfers between devices with their start and end apart: 73 -> 41, of which waited for: 32 -> 16; matrix products, arithmetic and copies ran while one was open for 8% -> 7% of each run, Pallas kernels for 26% -> 41%
where the time goes in v2:
time: 355 us; the launch traced here: 354 us
  Pallas kernels  147 us (41%)
  waiting for transfers between devices  73.3 us (21%)
  starting transfers between devices  65.5 us (18%)
  blocking collectives  25.5 us (7%)
  other arithmetic  20.9 us (6%)
  local copies, waits for them, and re-layouts  17 us (5%)
    pallas_call x8, Pallas kernels, project(): pl.pallas_call(body, grid=(units // tile,), in_specs=[pl.BlockSpec(memory...  74.3 us
    pallas_call x4, Pallas kernels, project_back(): pl.pallas_call(body, grid=(halves * steps,), in_specs=[pl.BlockSpec(memor...  52.2 us
    ppermute x18, waiting for transfers between devices, turn_chip(): lax.ppermute(v, 'seq', [(i, (i // 2 + p) % n * 2 + i % 2) for i in range(...  48.8 us
    all_to_all x1, blocking collectives, between_experts(): lax.all_to_all(v, 'expert', 0, 0, axis_index_groups=groups, tiled=True)  25.5 us
    ppermute x18, starting transfers between devices, turn_chip(): lax.ppermute(v, 'seq', [(i, (i // 2 + p) % n * 2 + i % 2) for i in range(...  22 us
    all_to_all x5, starting transfers between devices, between_experts(): lax.all_to_all(v, 'expert', 0, 0, axis_index_groups=groups, tiled=True)  21.3 us
    unnamed x82, local copies, waits for them, and re-layouts  12.8 us
    ppermute x8, starting transfers between devices, turn_slice(): lax.ppermute(v, 'expert', [(i, i // m * m + (i % m + k) % m) for i in ran...  9.5 us
  transfers between devices with their start and end apart: 41, of which 16 were waited for; matrix products, arithmetic and copies ran while one was open for 7% of the time, Pallas kernels for 41%

profile of v2, /device:TPU:0, one launch (start us, length us, event | category | flops | bytes accessed | tf_op | source)
XLA Modules:
  0.0 353.5 jit_solution(5114848298353024117)
XLA Ops:
  3.1 3.0 collective-permute-start.4
  17.3 5.2 %collective-permute-done = f32[2,2,128,128]{3,2,1,0:T(8,128)S(1)} collective-permute-done((f32[2,2,128,128]{3,2,1,0:T(8,128)S(1)}, f32[2,2,128,128]{3,2,1,0:T(8,128)S(1)}, u32[]{:S(2)}, u32[]{:S(2)}) %collective-permute-start) | collective-permute-done | bytes 262176 | tf_op jit(solution)/shard_map/ppermute | solution.py:30
  23.4 4.8 %collective-permute-start.1 = (f32[2,2,128,128]{3,2,1,0:T(8,128)}, f32[2,2,128,128]{3,2,1,0:T(8,128)S(1)}, u32[]{:S(2)}, u32[]{:S(2)}) collective-permute-start(f32[2,2,128,128]{3,2,1,0:T(8,128)} %add_select_fusion.3), channel_id=1, source_target_pairs={{0,16},{8,24},{1,17},{9,25},{2,18},{10,26},{3,19},{11,27},{4,20},{... | collective-permute-start | bytes 786440 | tf_op jit(solution)/shard_map/ppermute | solution.py:40
  30.7 3.6 %collective-permute-done.1 = f32[2,2,128,128]{3,2,1,0:T(8,128)S(1)} collective-permute-done((f32[2,2,128,128]{3,2,1,0:T(8,128)}, f32[2,2,128,128]{3,2,1,0:T(8,128)S(1)}, u32[]{:S(2)}, u32[]{:S(2)}) %collective-permute-start.1) | collective-permute-done | bytes 262176 | tf_op jit(solution)/shard_map/ppermute | solution.py:40
  37.5 25.5 %all_to_all.30.refs_0_ = bf16[4,2,32,1536]{3,2,1,0:T(8,128)(2,1)} all-to-all(bf16[4,2,32,1536]{3,2,1,0:T(8,128)(2,1)S(1)} %pick_rows.4.refs_2_), channel_id=1, replica_groups={{0,2,4,6},{1,3,5,7},{8,10,12,14},{9,11,13,15},{16,18,20,22},{17,19,21,2..., dimensions={0} | all-to-all | bytes 1572864 | tf_op jit(solution)/shard_map/all_to_all | solution.py:45
  63.0 3.5 all-to-all-start.1
  66.6 6.8 %local_grads.1 = (bf16[2,256,256]{2,1,0:T(8,128)(2,1)}, f32[2,256,256]{2,1,0:T(8,128)S(1)}, f32[2,256,256]{2,1,0:T(8,128)S(1)}, f32[2,2,128,128]{3,2,1,0:T(8,128)S(1)}) custom-call(f32[2]{0:T(128)S(1)} %copy-done.30, bf16[2,256,256]{2,1,0:T(8,128)(2,1)S(1)} %copy-done.28, bf16[2,256,256]{2,1,0:T(8,128)(2,1)S(1)} %copy-done.6, ...), custom_call_target="tpu_custom_call" | custom-call | flops 1000 | bytes 1000 | tf_op jit(solution)/shard_map/local_grads/pallas_call | solution.py:394
  79.5 6.7 %all-to-all-done.1.refs_0_ = bf16[4,2,32,1536]{3,2,1,0:T(8,128)(2,1)S(1)} async-done(((bf16[4,2,32,1536]{3,2,1,0:T(8,128)(2,1)}), bf16[4,2,32,1536]{3,2,1,0:T(8,128)(2,1)S(1)}, u32[]{:S(2)}, u32[]{:S(2)}) %all-to-all-start.1) | async-done | bytes 786464 | tf_op jit(solution)/shard_map/all_to_all | solution.py:45
  88.6 11.6 %project.8 = (f32[2,64,2304]{2,1,0:T(8,128)S(1)}, f32[1,2,64,2304]{3,2,1,0:T(8,128)S(1)}) custom-call(s32[1]{0:T(128)} %bitcast.4.chip_ref, bf16[4,2,32,1536]{3,2,1,0:T(8,128)(2,1)} %all_to_all.30.refs_0_, bf16[1536,2304]{1,0:T(8,128)(2,1)} %bitcast.148, bf16[1536,2304]{1,0:T(8,128)(2,1)} %collective-permute-done.5.refs_3_.refs_2_.refs_6_.refs_4_, ...), custom_call_target="tpu_custom_call" | custom-call | flops 1000 | bytes 1000 | tf_op jit(solution)/shard_map/project/pallas_call | solution.py:145
  101.1 2.4 collective-permute-start.11
  103.5 3.7 %all-to-all-start.2 = ((bf16[4,2,40,1536]{3,2,1,0:T(8,128)(2,1)}), bf16[4,2,40,1536]{3,2,1,0:T(8,128)(2,1)S(1)}, u32[]{:S(2)}, u32[]{:S(2)}) async-start(bf16[4,2,40,1536]{3,2,1,0:T(8,128)(2,1)} %pick_rows.5.refs_2_), calls=%async_computation.2 | async-start | bytes 1966080 | tf_op jit(solution)/shard_map/all_to_all | solution.py:45
  107.2 6.7 %project.9 = (f32[1,64,2304]{2,1,0:T(8,128)S(1)}, f32[1,1,64,2304]{3,2,1,0:T(8,128)S(1)}) custom-call(s32[1]{0:T(128)} %bitcast.4.chip_ref, bf16[4,2,32,1536]{3,2,1,0:T(8,128)(2,1)S(1)} %all-to-all-done.1.refs_0_, bf16[1536,2304]{1,0:T(8,128)(2,1)} %bitcast.19.refs_1_, bf16[1536,2304]{1,0:T(8,128)(2,1)} %collective-permute-done.9.refs_2_, ...), custom_call_target="tpu_custom_call" | custom-call | flops 1000 | bytes 1000 | tf_op jit(solution)/shard_map/project/pallas_call | solution.py:145
  114.2 3.2 collective-permute-done.11
  124.7 11.6 %project.10 = (f32[2,64,2304]{2,1,0:T(8,128)S(1)}, f32[1,2,64,2304]{3,2,1,0:T(8,128)S(1)}) custom-call(s32[1]{0:T(128)} %bitcast.4.chip_ref, bf16[4,2,32,1536]{3,2,1,0:T(8,128)(2,1)} %collective-permute-done.14.refs_0_, bf16[1536,2304]{1,0:T(8,128)(2,1)} %bitcast.149, bf16[1536,2304]{1,0:T(8,128)(2,1)} %collective-permute-done.5.refs_3_.refs_2_.refs_6_.refs_4_, ...), custom_call_target="tpu_custom_call" | custom-call | flops 1000 | bytes 1000 | tf_op jit(solution)/shard_map/project/pallas_call | solution.py:145
  138.8 6.9 %project.11 = (f32[1,64,2304]{2,1,0:T(8,128)S(1)}, f32[1,1,64,2304]{3,2,1,0:T(8,128)S(1)}) custom-call(s32[1]{0:T(128)} %bitcast.4.chip_ref, bf16[4,2,32,1536]{3,2,1,0:T(8,128)(2,1)} %collective-permute-done.13.refs_0_, bf16[1536,2304]{1,0:T(8,128)(2,1)} %bitcast.19.refs_1_, bf16[1536,2304]{1,0:T(8,128)(2,1)} %collective-permute-done.9.refs_2_, ...), custom_call_target="tpu_custom_call" | custom-call | flops 1000 | bytes 1000 | tf_op jit(solution)/shard_map/project/pallas_call | solution.py:145
  146.5 4.3 %all-to-all-start.3 = ((bf16[4,2,40,1536]{3,2,1,0:T(8,128)(2,1)}), bf16[4,2,40,1536]{3,2,1,0:T(8,128)(2,1)}, u32[]{:S(2)}, u32[]{:S(2)}) async-start(bf16[4,2,40,1536]{3,2,1,0:T(8,128)(2,1)} %pick_rows.7.refs_0_), calls=%async_computation.3 | async-start | bytes 1966080 | tf_op jit(solution)/shard_map/all_to_all | solution.py:45
  153.1 11.6 %project.12 = (f32[2,72,2304]{2,1,0:T(8,128)S(1)}, f32[1,2,72,2304]{3,2,1,0:T(8,128)S(1)}) custom-call(s32[1]{0:T(128)} %bitcast.4.chip_ref, bf16[4,2,40,1536]{3,2,1,0:T(8,128)(2,1)S(1)} %copy-done.1, bf16[1536,2304]{1,0:T(8,128)(2,1)} %bitcast.150, bf16[1536,2304]{1,0:T(8,128)(2,1)} %collective-permute-done.5.refs_3_.refs_2_.refs_6_.refs_4_, ...), custom_call_target="tpu_custom_call" | custom-call | flops 1000 | bytes 1000 | tf_op jit(solution)/shard_map/project/pallas_call | solution.py:145
  170.2 16.6 %collective-permute-done.15 = f16[1,64,2304]{2,1,0:T(8,128)(2,1)S(1)} collective-permute-done((f16[1,64,2304]{2,1,0:T(8,128)(2,1)S(1)}, f16[1,64,2304]{2,1,0:T(8,128)(2,1)S(1)}, u32[]{:S(2)}, u32[]{:S(2)}) %collective-permute-start.15) | collective-permute-done | bytes 294944 | tf_op jit(solution)/shard_map/ppermute | solution.py:34
  189.3 11.6 %project.13 = (f32[2,72,2304]{2,1,0:T(8,128)S(1)}, f32[1,2,72,2304]{3,2,1,0:T(8,128)S(1)}) custom-call(s32[1]{0:T(128)} %bitcast.4.chip_ref, bf16[4,2,40,1536]{3,2,1,0:T(8,128)(2,1)S(1)} %collective-permute-done.18.refs_0_, bf16[1536,2304]{1,0:T(8,128)(2,1)} %bitcast.151, bf16[1536,2304]{1,0:T(8,128)(2,1)} %collective-permute-done.5.refs_3_.refs_2_.refs_6_.refs_4_, ...), custom_call_target="tpu_custom_call" | custom-call | flops 1000 | bytes 1000 | tf_op jit(solution)/shard_map/project/pallas_call | solution.py:145
  205.8 7.3 %project.14 = (f32[1,72,2304]{2,1,0:T(8,128)S(1)}, f32[1,1,72,2304]{3,2,1,0:T(8,128)S(1)}) custom-call(s32[1]{0:T(128)} %bitcast.4.chip_ref, bf16[4,2,40,1536]{3,2,1,0:T(8,128)(2,1)} %all-to-all-done.3.refs_0_, bf16[1536,2304]{1,0:T(8,128)(2,1)} %bitcast.19.refs_1_, bf16[1536,2304]{1,0:T(8,128)(2,1)} %collective-permute-done.9.refs_2_, ...), custom_call_target="tpu_custom_call" | custom-call | flops 1000 | bytes 1000 | tf_op jit(solution)/shard_map/project/pallas_call | solution.py:145
  214.4 16.7 %project_back.4 = (bf16[4,2,32,1536]{3,2,1,0:T(8,128)(2,1)S(1)}, bf16[4,2,32,1536]{3,2,1,0:T(8,128)(2,1)}) custom-call(s32[1]{0:T(128)} %bitcast.4.chip_ref, bf16[2,64,2304]{2,1,0:T(8,128)(2,1)S(1)} %multiply_convert_fusion.6.refs_0_, bf16[2,64,2304]{2,1,0:T(8,128)(2,1)S(1)} %copy-done.21, bf16[2,64,2304]{2,1,0:T(8,128)(2,1)} %multiply_convert_fusion.4.refs_2_, ...), custom_call_target="tpu_custom_call" | custom-call | flops 1000 | bytes 1000 | tf_op jit(solution)/shard_map/project_back/pallas_call | solution.py:226
  231.6 7.0 %project.15 = (f32[1,72,2304]{2,1,0:T(8,128)S(1)}, f32[1,1,72,2304]{3,2,1,0:T(8,128)S(1)}) custom-call(s32[1]{0:T(128)} %bitcast.4.chip_ref, bf16[4,2,40,1536]{3,2,1,0:T(8,128)(2,1)S(1)} %collective-permute-done.21.refs_0_, bf16[1536,2304]{1,0:T(8,128)(2,1)} %bitcast.19.refs_1_, bf16[1536,2304]{1,0:T(8,128)(2,1)} %collective-permute-done.9.refs_2_, ...), custom_call_target="tpu_custom_call" | custom-call | flops 1000 | bytes 1000 | tf_op jit(solution)/shard_map/project/pallas_call | solution.py:145
  240.0 5.9 %collective-permute-done.23 = f16[1,72,2304]{2,1,0:T(8,128)(2,1)S(1)} collective-permute-done((f16[1,72,2304]{2,1,0:T(8,128)(2,1)S(1)}, f16[1,72,2304]{2,1,0:T(8,128)(2,1)S(1)}, u32[]{:S(2)}, u32[]{:S(2)}) %collective-permute-start.23) | collective-permute-done | bytes 331808 | tf_op jit(solution)/shard_map/ppermute | solution.py:34
  250.8 15.8 %collective-permute-done.25.refs_1_ = bf16[2,72,2304]{2,1,0:T(8,128)(2,1)} collective-permute-done((bf16[2,72,2304]{2,1,0:T(8,128)(2,1)S(1)}, bf16[2,72,2304]{2,1,0:T(8,128)(2,1)}, u32[]{:S(2)}, u32[]{:S(2)}) %collective-permute-start.25) | collective-permute-done | bytes 663584 | tf_op jit(solution)/shard_map/ppermute | solution.py:34
  268.9 4.9 %all-to-all-start.4 = ((bf16[4,2,32,1536]{3,2,1,0:T(8,128)(2,1)}), bf16[4,2,32,1536]{3,2,1,0:T(8,128)(2,1)S(1)}, u32[]{:S(2)}, u32[]{:S(2)}) async-start(bf16[4,2,32,1536]{3,2,1,0:T(8,128)(2,1)} %add_convert_fusion.1), calls=%async_computation.4 | async-start | bytes 1572864 | tf_op jit(solution)/shard_map/all_to_all | solution.py:45
  275.8 8.8 %project_back.5.refs_4_ = bf16[4,1,36,1536]{3,2,1,0:T(8,128)(2,1)} custom-call(s32[1]{0:T(128)} %bitcast.4.chip_ref, bf16[2,72,2304]{2,1,0:T(8,128)(2,1)S(1)} %multiply_convert_fusion.1.refs_0_, bf16[2,72,2304]{2,1,0:T(8,128)(2,1)S(1)} %collective-permute-done.26.refs_1_, bf16[1536,2304]{1,0:T(8,128)(2,1)} %bitcast.153, bf16[1536,2304]{1,0:T(8,128)(2,1)} %bitcast.161, ...), custom_call_target="tpu_custom_call" | custom-call | flops 1000 | bytes 1000 | tf_op jit(solution)/shard_map/project_back/pallas_call | solution.py:226
  286.1 8.8 %project_back.6.refs_6_ = bf16[4,1,36,1536]{3,2,1,0:T(8,128)(2,1)} custom-call(s32[1]{0:T(128)} %bitcast.4.chip_ref, bf16[2,72,2304]{2,1,0:T(8,128)(2,1)S(1)} %multiply_convert_fusion.1.refs_0_, bf16[2,72,2304]{2,1,0:T(8,128)(2,1)S(1)} %collective-permute-done.26.refs_1_, bf16[1536,2304]{1,0:T(8,128)(2,1)} %collective-permute-done.5.refs_3_.refs_2_.refs_6_.refs_4_, ...), custom_call_target="tpu_custom_call" | custom-call | flops 1000 | bytes 1000 | tf_op jit(solution)/shard_map/project_back/pallas_call | solution.py:226
  296.8 17.9 %project_back.7 = bf16[4,2,36,1536]{3,2,1,0:T(8,128)(2,1)S(1)} custom-call(s32[1]{0:T(128)} %bitcast.4.chip_ref, bf16[2,72,2304]{2,1,0:T(8,128)(2,1)S(1)} %multiply_convert_fusion.refs_0_, bf16[2,72,2304]{2,1,0:T(8,128)(2,1)} %collective-permute-done.25.refs_1_, bf16[1536,2304]{1,0:T(8,128)(2,1)} %bitcast.154, bf16[1536,2304]{1,0:T(8,128)(2,1)} %bitcast.162, ...), custom_call_target="tpu_custom_call" | custom-call | flops 1000 | bytes 1000 | tf_op jit(solution)/shard_map/project_back/pallas_call | solution.py:226
  320.6 5.0 %all-to-all-start.5 = ((bf16[4,2,36,1536]{3,1,2,0:T(2,128)(2,1)}), bf16[4,2,36,1536]{3,1,2,0:T(2,128)(2,1)S(1)}, u32[]{:S(2)}, u32[]{:S(2)}) async-start(bf16[4,2,36,1536]{3,1,2,0:T(2,128)(2,1)} %copy.86), calls=%async_computation.5 | async-start | bytes 1769472 | tf_op jit(solution)/shard_map/all_to_all | solution.py:45
  331.7 2.4 collective-permute-start.32
  338.3 3.3 collective-permute-done.32
  350.1 2.5 collective-permute-done.35
  (239 shorter events, 95.2 us)
Async XLA Ops:
  0.7 35.2 %collective-permute-start.5 = (bf16[1536,2304]{1,0:T(8,128)(2,1)}, bf16[1536,2304]{1,0:T(8,128)(2,1)}, u32[]{:S(2)}, u32[]{:S(2)}) collective-permute-start(bf16[1536,2304]{1,0:T(8,128)(2,1)} %bitcast.147), channel_id=1, source_target_pairs={{0,8},{8,0},{16,24},{24,16},{1,9},{9,1},{17,25},{25,17},{2,10},{10... | collective-permute-start | bytes 21233672 | tf_op jit(solution)/shard_map/ppermute | solution.py:30
  1.2 34.7 %collective-permute-start.6 = (bf16[1536,2304]{1,0:T(8,128)(2,1)}, bf16[1536,2304]{1,0:T(8,128)(2,1)}, u32[]{:S(2)}, u32[]{:S(2)}) collective-permute-start(bf16[1536,2304]{1,0:T(8,128)(2,1)} %bitcast.155), channel_id=1, source_target_pairs={{0,8},{8,0},{16,24},{24,16},{1,9},{9,1},{17,25},{25,17},{2,10},{10... | collective-permute-start | bytes 21233672 | tf_op jit(solution)/shard_map/ppermute | solution.py:30
  3.1 25.5 %collective-permute-start.4 = (bf16[2,64,1536]{2,1,0:T(8,128)(2,1)S(1)}, bf16[2,64,1536]{2,1,0:T(8,128)(2,1)S(1)}, u32[]{:S(2)}, u32[]{:S(2)}) collective-permute-start(bf16[2,64,1536]{2,1,0:T(8,128)(2,1)S(1)} %bitcast.145), channel_id=1, source_target_pairs={{0,16},{8,24},{16,0},{24,8},{1,17},{9,25},{17,1},{25,9},{2,18},{10... | collective-permute-start | bytes 1179656 | tf_op jit(solution)/shard_map/ppermute | solution.py:34
  15.5 18.9 %collective-permute-start.3 = (bf16[2,64,1536]{2,1,0:T(8,128)(2,1)}, bf16[2,64,1536]{2,1,0:T(8,128)(2,1)S(1)}, u32[]{:S(2)}, u32[]{:S(2)}) collective-permute-start(bf16[2,64,1536]{2,1,0:T(8,128)(2,1)} %bitcast.146), channel_id=1, source_target_pairs={{0,16},{8,24},{16,0},{24,8},{1,17},{9,25},{17,1},{25,9},{2,18},{10... | collective-permute-start | bytes 1179656 | tf_op jit(solution)/shard_map/ppermute | solution.py:34
  23.4 10.9 %collective-permute-start.1 = (f32[2,2,128,128]{3,2,1,0:T(8,128)}, f32[2,2,128,128]{3,2,1,0:T(8,128)S(1)}, u32[]{:S(2)}, u32[]{:S(2)}) collective-permute-start(f32[2,2,128,128]{3,2,1,0:T(8,128)} %add_select_fusion.3), channel_id=1, source_target_pairs={{0,16},{8,24},{1,17},{9,25},{2,18},{10,26},{3,19},{11,27},{4,20},{... | collective-permute-start | bytes 786440 | tf_op jit(solution)/shard_map/ppermute | solution.py:40
  37.4 69.8 %collective-permute-start.9 = (bf16[1536,2304]{1,0:T(8,128)(2,1)}, bf16[1536,2304]{1,0:T(8,128)(2,1)}, u32[]{:S(2)}, u32[]{:S(2)}) collective-permute-start(bf16[1536,2304]{1,0:T(8,128)(2,1)} %bitcast.19.refs_1_), channel_id=1, source_target_pairs={{0,8},{8,0},{16,24},{24,16},{1,9},{9,1},{17,25},{25,17},{2,10},{10... | collective-permute-start | bytes 21233672 | tf_op jit(solution)/shard_map/ppermute | solution.py:30
  63.0 23.3 %all-to-all-start.1 = ((bf16[4,2,32,1536]{3,2,1,0:T(8,128)(2,1)}), bf16[4,2,32,1536]{3,2,1,0:T(8,128)(2,1)S(1)}, u32[]{:S(2)}, u32[]{:S(2)}) async-start(bf16[4,2,32,1536]{3,2,1,0:T(8,128)(2,1)} %pick_rows.6.refs_2_), calls=%async_computation.1 | async-start | bytes 1572864 | tf_op jit(solution)/shard_map/all_to_all | solution.py:45
  76.7 11.1 %collective-permute-start.8 = (f32[2,2,128,128]{3,2,1,0:T(8,128)S(1)}, f32[2,2,128,128]{3,2,1,0:T(8,128)S(1)}, u32[]{:S(2)}, u32[]{:S(2)}) collective-permute-start(f32[2,2,128,128]{3,2,1,0:T(8,128)S(1)} %add_select_fusion.1), channel_id=1, source_target_pairs={{16,0},{24,8},{17,1},{25,9},{18,2},{26,10},{19,3},{27,11},{20,4},{... | collective-permute-start | bytes 786440 | tf_op jit(solution)/shard_map/ppermute | solution.py:40
  78.0 46.7 %collective-permute-start.14 = (bf16[4,2,32,1536]{3,2,1,0:T(8,128)(2,1)}, bf16[4,2,32,1536]{3,2,1,0:T(8,128)(2,1)}, u32[]{:S(2)}, u32[]{:S(2)}) collective-permute-start(bf16[4,2,32,1536]{3,2,1,0:T(8,128)(2,1)} %all_to_all.30.refs_0_), channel_id=1, source_target_pairs={{0,1},{1,0},{2,3},{3,2},{4,5},{5,4},{6,7},{7,6},{8,9},{9,8},{10,11... | collective-permute-start | bytes 2359304 | tf_op jit(solution)/shard_map/ppermute | solution.py:55
  86.3 51.7 %collective-permute-start.13 = (bf16[4,2,32,1536]{3,2,1,0:T(8,128)(2,1)S(1)}, bf16[4,2,32,1536]{3,2,1,0:T(8,128)(2,1)}, u32[]{:S(2)}, u32[]{:S(2)}) collective-permute-start(bf16[4,2,32,1536]{3,2,1,0:T(8,128)(2,1)S(1)} %all-to-all-done.1.refs_0_), channel_id=1, source_target_pairs={{0,1},{1,0},{2,3},{3,2},{4,5},{5,4},{6,7},{7,6},{8,9},{9,8},{10,11... | collective-permute-start | bytes 2359304 | tf_op jit(solution)/shard_map/ppermute | solution.py:55
  101.1 16.2 %collective-permute-start.11 = (f16[2,64,2304]{2,1,0:T(8,128)(2,1)}, f16[2,64,2304]{2,1,0:T(8,128)(2,1)}, u32[]{:S(2)}, u32[]{:S(2)}) collective-permute-start(f16[2,64,2304]{2,1,0:T(8,128)(2,1)} %fusion.5), channel_id=1, source_target_pairs={{0,16},{8,24},{16,0},{24,8},{1,17},{9,25},{17,1},{25,9},{2,18},{10... | collective-permute-start | bytes 1769480 | tf_op jit(solution)/shard_map/ppermute | solution.py:34
  103.5 43.0 %all-to-all-start.2 = ((bf16[4,2,40,1536]{3,2,1,0:T(8,128)(2,1)}), bf16[4,2,40,1536]{3,2,1,0:T(8,128)(2,1)S(1)}, u32[]{:S(2)}, u32[]{:S(2)}) async-start(bf16[4,2,40,1536]{3,2,1,0:T(8,128)(2,1)} %pick_rows.5.refs_2_), calls=%async_computation.2 | async-start | bytes 1966080 | tf_op jit(solution)/shard_map/all_to_all | solution.py:45
  122.9 15.0 %collective-permute-start.12 = (bf16[2,64,2304]{2,1,0:T(8,128)(2,1)S(1)}, bf16[2,64,2304]{2,1,0:T(8,128)(2,1)S(1)}, u32[]{:S(2)}, u32[]{:S(2)}) collective-permute-start(bf16[2,64,2304]{2,1,0:T(8,128)(2,1)S(1)} %multiply_convert_fusion.6.refs_0_), channel_id=1, source_target_pairs={{0,16},{8,24},{16,0},{24,8},{1,17},{9,25},{17,1},{25,9},{2,18},{10... | collective-permute-start | bytes 1769480 | tf_op jit(solution)/shard_map/ppermute | solution.py:34
  137.2 13.6 %collective-permute-start.16 = (f16[2,64,2304]{2,1,0:T(8,128)(2,1)}, f16[2,64,2304]{2,1,0:T(8,128)(2,1)}, u32[]{:S(2)}, u32[]{:S(2)}) collective-permute-start(f16[2,64,2304]{2,1,0:T(8,128)(2,1)} %fusion.6), channel_id=1, source_target_pairs={{0,16},{8,24},{16,0},{24,8},{1,17},{9,25},{17,1},{25,9},{2,18},{10... | collective-permute-start | bytes 1769480 | tf_op jit(solution)/shard_map/ppermute | solution.py:34
  146.5 55.4 %all-to-all-start.3 = ((bf16[4,2,40,1536]{3,2,1,0:T(8,128)(2,1)}), bf16[4,2,40,1536]{3,2,1,0:T(8,128)(2,1)}, u32[]{:S(2)}, u32[]{:S(2)}) async-start(bf16[4,2,40,1536]{3,2,1,0:T(8,128)(2,1)} %pick_rows.7.refs_0_), calls=%async_computation.3 | async-start | bytes 1966080 | tf_op jit(solution)/shard_map/all_to_all | solution.py:45
  165.6 66.0 %collective-permute-start.22 = (f16[2,72,2304]{2,1,0:T(8,128)(2,1)}, f16[2,72,2304]{2,1,0:T(8,128)(2,1)}, u32[]{:S(2)}, u32[]{:S(2)}) collective-permute-start(f16[2,72,2304]{2,1,0:T(8,128)(2,1)} %fusion.1), channel_id=1, source_target_pairs={{0,16},{8,24},{16,0},{24,8},{1,17},{9,25},{17,1},{25,9},{2,18},{10... | collective-permute-start | bytes 1990664 | tf_op jit(solution)/shard_map/ppermute | solution.py:34
  166.9 22.3 %collective-permute-start.18 = (bf16[4,2,40,1536]{3,2,1,0:T(8,128)(2,1)S(1)}, bf16[4,2,40,1536]{3,2,1,0:T(8,128)(2,1)S(1)}, u32[]{:S(2)}, u32[]{:S(2)}) collective-permute-start(bf16[4,2,40,1536]{3,2,1,0:T(8,128)(2,1)S(1)} %copy-done.1), channel_id=1, source_target_pairs={{0,1},{1,0},{2,3},{3,2},{4,5},{5,4},{6,7},{7,6},{8,9},{9,8},{10,11... | collective-permute-start | bytes 2949128 | tf_op jit(solution)/shard_map/ppermute | solution.py:55
  167.9 18.9 %collective-permute-start.15 = (f16[1,64,2304]{2,1,0:T(8,128)(2,1)S(1)}, f16[1,64,2304]{2,1,0:T(8,128)(2,1)S(1)}, u32[]{:S(2)}, u32[]{:S(2)}) collective-permute-start(f16[1,64,2304]{2,1,0:T(8,128)(2,1)S(1)} %fusion.12), channel_id=1, source_target_pairs={{0,16},{8,24},{16,0},{24,8},{1,17},{9,25},{17,1},{25,9},{2,18},{10... | collective-permute-start | bytes 884744 | tf_op jit(solution)/shard_map/ppermute | solution.py:34
  188.2 26.2 %collective-permute-start.17 = (bf16[2,64,2304]{2,1,0:T(8,128)(2,1)}, bf16[2,64,2304]{2,1,0:T(8,128)(2,1)}, u32[]{:S(2)}, u32[]{:S(2)}) collective-permute-start(bf16[2,64,2304]{2,1,0:T(8,128)(2,1)} %multiply_convert_fusion.4.refs_2_), channel_id=1, source_target_pairs={{0,16},{8,24},{16,0},{24,8},{1,17},{9,25},{17,1},{25,9},{2,18},{10... | collective-permute-start | bytes 1769480 | tf_op jit(solution)/shard_map/ppermute | solution.py:34
  201.9 29.7 %collective-permute-start.21 = (bf16[4,2,40,1536]{3,2,1,0:T(8,128)(2,1)}, bf16[4,2,40,1536]{3,2,1,0:T(8,128)(2,1)S(1)}, u32[]{:S(2)}, u32[]{:S(2)}) collective-permute-start(bf16[4,2,40,1536]{3,2,1,0:T(8,128)(2,1)} %all-to-all-done.3.refs_0_), channel_id=1, source_target_pairs={{0,1},{1,0},{2,3},{3,2},{4,5},{5,4},{6,7},{7,6},{8,9},{9,8},{10,11... | collective-permute-start | bytes 2949128 | tf_op jit(solution)/shard_map/ppermute | solution.py:55
  204.8 34.9 %collective-permute-start.24 = (f16[2,72,2304]{2,1,0:T(8,128)(2,1)S(1)}, f16[2,72,2304]{2,1,0:T(8,128)(2,1)S(1)}, u32[]{:S(2)}, u32[]{:S(2)}) collective-permute-start(f16[2,72,2304]{2,1,0:T(8,128)(2,1)S(1)} %fusion.2), channel_id=1, source_target_pairs={{0,16},{8,24},{16,0},{24,8},{1,17},{9,25},{17,1},{25,9},{2,18},{10... | collective-permute-start | bytes 1990664 | tf_op jit(solution)/shard_map/ppermute | solution.py:34
  213.2 33.4 %collective-permute-start.20 = (f16[1,72,2304]{2,1,0:T(8,128)(2,1)S(1)}, f16[1,72,2304]{2,1,0:T(8,128)(2,1)S(1)}, u32[]{:S(2)}, u32[]{:S(2)}) collective-permute-start(f16[1,72,2304]{2,1,0:T(8,128)(2,1)S(1)} %fusion.9), channel_id=1, source_target_pairs={{0,16},{8,24},{16,0},{24,8},{1,17},{9,25},{17,1},{25,9},{2,18},{10... | collective-permute-start | bytes 995336 | tf_op jit(solution)/shard_map/ppermute | solution.py:34
  231.0 19.8 %collective-permute-start.19 = (bf16[4,2,32,1536]{3,2,1,0:T(8,128)(2,1)}, bf16[4,2,32,1536]{3,2,1,0:T(8,128)(2,1)}, u32[]{:S(2)}, u32[]{:S(2)}) collective-permute-start(bf16[4,2,32,1536]{3,2,1,0:T(8,128)(2,1)} %get-tuple-element.91), channel_id=1, source_target_pairs={{0,1},{1,0},{2,3},{3,2},{4,5},{5,4},{6,7},{7,6},{8,9},{9,8},{10,11... | collective-permute-start | bytes 2359304 | tf_op jit(solution)/shard_map/ppermute | solution.py:55
  248.6 18.0 %collective-permute-start.25 = (bf16[2,72,2304]{2,1,0:T(8,128)(2,1)S(1)}, bf16[2,72,2304]{2,1,0:T(8,128)(2,1)}, u32[]{:S(2)}, u32[]{:S(2)}) collective-permute-start(bf16[2,72,2304]{2,1,0:T(8,128)(2,1)S(1)} %multiply_convert_fusion.refs_0_), channel_id=1, source_target_pairs={{0,16},{8,24},{16,0},{24,8},{1,17},{9,25},{17,1},{25,9},{2,18},{10... | collective-permute-start | bytes 1990664 | tf_op jit(solution)/shard_map/ppermute | solution.py:34
  249.7 25.1 %collective-permute-start.26 = (bf16[2,72,2304]{2,1,0:T(8,128)(2,1)S(1)}, bf16[2,72,2304]{2,1,0:T(8,128)(2,1)S(1)}, u32[]{:S(2)}, u32[]{:S(2)}) collective-permute-start(bf16[2,72,2304]{2,1,0:T(8,128)(2,1)S(1)} %multiply_convert_fusion.1.refs_0_), channel_id=1, source_target_pairs={{0,16},{8,24},{16,0},{24,8},{1,17},{9,25},{17,1},{25,9},{2,18},{10... | collective-permute-start | bytes 1990664 | tf_op jit(solution)/shard_map/ppermute | solution.py:34
  268.9 48.6 %all-to-all-start.4 = ((bf16[4,2,32,1536]{3,2,1,0:T(8,128)(2,1)}), bf16[4,2,32,1536]{3,2,1,0:T(8,128)(2,1)S(1)}, u32[]{:S(2)}, u32[]{:S(2)}) async-start(bf16[4,2,32,1536]{3,2,1,0:T(8,128)(2,1)} %add_convert_fusion.1), calls=%async_computation.4 | async-start | bytes 1572864 | tf_op jit(solution)/shard_map/all_to_all | solution.py:45
  284.6 30.7 %collective-permute-start.27 = (bf16[4,1,36,1536]{3,2,1,0:T(8,128)(2,1)}, bf16[4,1,36,1536]{3,2,1,0:T(8,128)(2,1)}, u32[]{:S(2)}, u32[]{:S(2)}) collective-permute-start(bf16[4,1,36,1536]{3,2,1,0:T(8,128)(2,1)} %project_back.5.refs_4_), channel_id=1, source_target_pairs={{0,1},{1,0},{2,3},{3,2},{4,5},{5,4},{6,7},{7,6},{8,9},{9,8},{10,11... | collective-permute-start | bytes 1327112 | tf_op jit(solution)/shard_map/ppermute | solution.py:55
  295.0 20.4 %collective-permute-start.28 = (bf16[4,1,36,1536]{3,2,1,0:T(8,128)(2,1)}, bf16[4,1,36,1536]{3,2,1,0:T(8,128)(2,1)S(1)}, u32[]{:S(2)}, u32[]{:S(2)}) collective-permute-start(bf16[4,1,36,1536]{3,2,1,0:T(8,128)(2,1)} %project_back.6.refs_6_), channel_id=1, source_target_pairs={{0,1},{1,0},{2,3},{3,2},{4,5},{5,4},{6,7},{7,6},{8,9},{9,8},{10,11... | collective-permute-start | bytes 1327112 | tf_op jit(solution)/shard_map/ppermute | solution.py:55
  295.6 19.1 %collective-permute-start.29 = (bf16[272]{0:T(512)(128)(2,1)S(1)}, bf16[272]{0:T(512)(128)(2,1)S(1)}, u32[]{:S(2)}, u32[]{:S(2)}) collective-permute-start(bf16[272]{0:T(512)(128)(2,1)S(1)} %pad_maximum_fusion.4), channel_id=1, source_target_pairs={{0,16},{8,24},{16,0},{24,8},{1,17},{9,25},{17,1},{25,9},{2,18},{10... | collective-permute-start | bytes 1640 | tf_op jit(solution)/shard_map/ppermute | solution.py:34
  320.6 21.7 %all-to-all-start.5 = ((bf16[4,2,36,1536]{3,1,2,0:T(2,128)(2,1)}), bf16[4,2,36,1536]{3,1,2,0:T(2,128)(2,1)S(1)}, u32[]{:S(2)}, u32[]{:S(2)}) async-start(bf16[4,2,36,1536]{3,1,2,0:T(2,128)(2,1)} %copy.86), calls=%async_computation.5 | async-start | bytes 1769472 | tf_op jit(solution)/shard_map/all_to_all | solution.py:45
  329.7 8.7 %collective-permute-start.31 = (f32[4,68]{1,0:T(4,128)S(1)}, f32[4,68]{1,0:T(4,128)S(1)}, u32[]{:S(2)}, u32[]{:S(2)}) collective-permute-start(f32[4,68]{1,0:T(4,128)S(1)} %convert_add_fusion), channel_id=1, source_target_pairs={{0,2},{1,3},{2,4},{3,5},{4,6},{5,7},{6,0},{7,1},{8,10},{9,11},{10,... | collective-permute-start | bytes 3272 | tf_op jit(solution)/shard_map/ppermute | solution.py:49
  331.7 9.9 %collective-permute-start.32 = (f32[4,68]{1,0:T(4,128)S(1)}, f32[4,68]{1,0:T(4,128)S(1)}, u32[]{:S(2)}, u32[]{:S(2)}) collective-permute-start(f32[4,68]{1,0:T(4,128)S(1)} %convert_add_fusion), channel_id=1, source_target_pairs={{0,4},{1,5},{2,6},{3,7},{4,0},{5,1},{6,2},{7,3},{8,12},{9,13},{10,... | collective-permute-start | bytes 3272 | tf_op jit(solution)/shard_map/ppermute | solution.py:49
  (48 other events, 345.0 us)

commit v3 on v2

--- a/solution.py
+++ b/solution.py
@@ -448,18 +448,20 @@
     )(decay_rate, key_rows, value_rows, grad_k, grad_v, state, *after)
 
 
-def carried(place, summary, decay_rate, block_size, direction):
+def carried(place, summary, decay_rate, block_size, direction, hold=None):
     def block_decay(blocks):
         return jnp.exp(-decay_rate * (block_size * blocks)).reshape(1, -1, 1, 1)
 
-    partner = place.swap_core(summary)
+    found = [place.later_chip(summary, direction * p) for p in range(1, place.chips)]
+    if hold is not None:
+        hold.extend(found)
+    mine = jnp.stack([summary, *found])
+    partner = place.swap_core(mine)
     first = (place.core == 0) if direction > 0 else (place.core == 1)
     one = block_decay(1)
-    near = jnp.where(first, partner + one * summary, summary + one * partner)
-    outside = jnp.zeros_like(summary)
-    for p in range(1, place.chips):
-        outside = outside + block_decay(2 * (p - 1)) * place.later_chip(near, direction * p)
-    return jnp.where(first, outside, partner + one * outside)
+    near = jnp.where(first, partner + one * mine, mine + one * partner)
+    outside = sum(block_decay(2 * (p - 1)) * near[p] for p in range(1, place.chips))
+    return jnp.where(first, outside, partner[0] + one * outside)
 
 
 def cut_features(v, scale, chip_core, chips, after):
@@ -592,16 +594,18 @@
     def relay(mine):
         return [place.turn_slice(mine, k) for k in range(1, slices)]
 
-    def partial(arrays, count, mats, scale, needs=()):
-        arrays = [behind(v, *needs) for v in arrays]
-        keep, send = ordered(project, [(arrays, mats)], count, chip_here, chips)
-        ready = (send * scale).astype(jnp.float16)
-        arrived = [place.turn_chip(ready[p - 1], p) for p in range(1, chips)]
-        return keep, arrived, scale
+    def partial(jobs, count, needs=()):
+        scales = jnp.asarray([scale for _, mats, scale in jobs for _ in mats], f32)
+        scales = scales.reshape(-1, 1, 1)
+        ready = [([behind(v, *needs) for v in arrays], mats) for arrays, mats, _ in jobs]
+        keep, send = ordered(project, ready, count, chip_here, chips)
+        send = (send * scales).astype(jnp.float16)
+        arrived = [place.turn_chip(send[p - 1], p) for p in range(1, chips)]
+        return keep, arrived, scales
 
     def settle(part):
         keep, arrived, scale = part
-        return keep + sum(v.astype(f32) for v in arrived) * (1.0 / scale)
+        return keep + sum(v.astype(f32) for v in arrived) / scale
 
     def ring(v):
         found = [v] + [None] * (chips - 1)
@@ -609,9 +613,8 @@
             found[chips - p] = place.turn_chip(v, p)
         return found
 
-    def middle(inner, outer):
-        pre_gate, pre_up = settle(inner)
-        unit_grad = settle(outer)[0]
+    def middle(*some):
+        pre_gate, pre_up, unit_grad = jnp.concatenate([settle(v) for v in some])
         sigmoid_gate = jax.nn.sigmoid(pre_gate)
         activated = pre_gate * sigmoid_gate
         units = activated * pre_up
@@ -638,14 +641,16 @@
         return keep, [behind(v, kernel_result) for v in arrived], scale
 
     summary = ordered(key_value_state, key_rows, value_rows, decay_rate)
-    state_before = carried(place, summary, decay_rate, block, 1)
+    early = []
+    state_before = carried(place, summary, decay_rate, block, 1, early)
     picked_hidden_a = dispatch(hidden_groups, first_a, count_a)
     picked_hidden_b = dispatch(hidden_groups, first_b, count_b)
-    picked_grads_a = dispatch(grad_groups, first_a, count_a, [state_before])
+    picked_grads_a = dispatch(grad_groups, first_a, count_a, early)
     hidden_a = place.between_experts(behind(picked_hidden_a, picked_grads_a))
-    picked_grads_b = dispatch(
-        grad_groups, first_b, count_b, [pairs[0][1], pairs[1][1]]
-    )
+    picked_grads_b = dispatch(grad_groups, first_b, count_b, [pairs[0][1], pairs[1][1]])
+    far_hidden_a = relay(hidden_a)
+    pairs.append((own_mats[2], place.swap_core(behind(own_mats[2], picked_grads_b))))
+    inner_own_a = partial([([hidden_a], pairs[:2], in_scale)], count_a)
     grad_queries, local_k, local_v, summary = ordered(
         local_grads,
         queries,
@@ -655,46 +660,46 @@
         norm_gain.reshape(1, -1),
         coeff.T,
         decay_rate,
-        state_before,
-    )
-    state_after = carried(place, summary, decay_rate, block, -1)
-    far_hidden_a = relay(hidden_a)
-    pairs.append((own_mats[2], place.swap_core(behind(own_mats[2], picked_grads_b))))
-    inner_own_a = partial([hidden_a], count_a, pairs[:2], in_scale, [state_after])
+        behind(state_before, inner_own_a[0]),
+    )
     grads_a = place.between_experts(behind(picked_grads_a, hidden_a))
-    far_grads_a = relay(grads_a)
-    outer_own_a = partial([grads_a], count_a, pairs[2:], out_scale)
+    far_grads_a = relay(behind(grads_a, summary))
+    outer_own_a = partial([([grads_a], pairs[2:], out_scale)], count_a)
+    hidden_b = place.between_experts(behind(picked_hidden_b, grads_a, summary))
+    own_a, score_own_a = middle(inner_own_a, outer_own_a)
+    whole_far_a = partial(
+        [(far_hidden_a, pairs[:2], in_scale), (far_grads_a, pairs[2:], out_scale)],
+        count_a,
+        own_a[:1],
+    )
+    far_hidden_b = relay(behind(hidden_b, whole_far_a[0]))
+    grads_b = place.between_experts(behind(picked_grads_b, hidden_b, whole_far_a[0]))
+    inner_own_b = partial([([hidden_b], pairs[:2], in_scale)], count_b, own_a[1:])
+    far_grads_b = relay(grads_b)
+    far_a, score_far_a = middle(whole_far_a)
+    state_after = carried(place, behind(summary, whole_far_a[0]), decay_rate, block, -1)
+    inner_far_b = partial([(far_hidden_b, pairs[:2], in_scale)], count_b, far_a[:1])
+    outer_own_b = partial([([grads_b], pairs[2:], out_scale)], count_b)
+    dx_own_a, dx_far_a = back([own_a, far_a], (0, 1), count_a)
+    outer_far_b = partial([(far_grads_b, pairs[2:], out_scale)], count_b, inner_own_b[1])
     grad_keys, grad_values = ordered(
         later_grads, key_rows, value_rows, local_k, local_v, decay_rate, state_after
     )
-    hidden_b = place.between_experts(behind(picked_hidden_b, grads_a, inner_own_a[0]))
-    own_a, score_own_a = middle(inner_own_a, outer_own_a)
-    inner_far_a = partial(far_hidden_a, count_a, pairs[:2], in_scale, own_a[:1])
-    outer_far_a = partial(far_grads_a, count_a, pairs[2:], out_scale, own_a[1:])
-    far_hidden_b = relay(behind(hidden_b, outer_far_a[0]))
-    grads_b = place.between_experts(behind(picked_grads_b, hidden_b, outer_far_a[0]))
-    inner_own_b = partial([hidden_b], count_b, pairs[:2], in_scale, inner_far_a[1])
-    far_grads_b = relay(grads_b)
-    far_a, score_far_a = middle(
-        held(inner_far_a, inner_own_b[0]), held(outer_far_a, inner_own_b[0])
-    )
-    inner_far_b = partial(far_hidden_b, count_b, pairs[:2], in_scale, far_a[:1])
-    outer_own_b = partial([grads_b], count_b, pairs[2:], out_scale)
-    dx_own_a, dx_far_a = back([own_a, far_a], (0, 1), count_a)
-    outer_far_b = partial(far_grads_b, count_b, pairs[2:], out_scale, inner_own_b[1])
     far_b, score_far_b = middle(inner_far_b, outer_far_b)
     own_b, score_own_b = middle(held(inner_own_b, far_b[0]), held(outer_own_b, far_b[0]))
     from_far_a = to_slices(dx_far_a)
     total_a = dx_own_a.astype(f32) + sum(
-        behind(v, own_b[1]).astype(f32) for v in from_far_a
-    )
-    home_a = place.between_experts(total_a.astype(bf16))
-    from_far_b = [to_slices(back([far_b], (h,), count_b)[0]) for h in range(2)]
-    (dx_own_b,) = back([own_b], (0, 1), count_b)
-    total_b = dx_own_b.astype(f32) + sum(
-        behind(jnp.concatenate(halves, axis=1), home_a).astype(f32) for halves in zip(*from_far_b)
-    )
-    home_b = place.between_experts(total_b.astype(bf16))
+        behind(v, grad_keys).astype(f32) for v in from_far_a
+    )
+    total_a = total_a.astype(bf16)
+    home_a = place.between_experts(total_a)
+    total_b = []
+    for h in range(2):
+        dx_own_b, dx_far_b = back([own_b, far_b], (h,), count_b, [total_a])
+        found = sum(v.astype(f32) for v in to_slices(dx_far_b))
+        total_b.append((dx_own_b.astype(f32) + found).astype(bf16))
+    total_b = behind(jnp.concatenate(total_b, axis=1), home_a)
+    home_b = place.between_experts(total_b)
 
     kinds = [score_own_a, score_far_a, score_own_b, score_far_b]
     sizes = [v.shape[0] for v in kinds]

time: 355 us -> 324 us (0.913)
  blocking collectives: 25.5 us -> 0 us
  Pallas kernels: 147 us -> 129 us
  waiting for transfers between devices: 73.3 us -> 89.2 us
    all_to_all x1 -> x0, blocking collectives: 25.5 us -> none  [between_experts(): lax.all_to_all(v, 'expert', 0, 0, axis_index_groups=groups, tiled=True)]
    pallas_call x4 -> x3, Pallas kernels: 52.2 us -> 34.6 us  [project_back(): pl.pallas_call(body, grid=(halves * steps,), in_specs=[pl.BlockSpec(memor...]
    all_to_all x5 -> x6, waiting for transfers between devices: 6.74 us -> 17.9 us  [between_experts(): lax.all_to_all(v, 'expert', 0, 0, axis_index_groups=groups, tiled=True)]
    ppermute x8, waiting for transfers between devices: 1.96 us -> 11.3 us  [turn_slice(): lax.ppermute(v, 'expert', [(i, i // m * m + (i % m + k) % m) for i in ran...]
    all_to_all x5 -> x6, starting transfers between devices: 21.3 us -> 28.3 us  [between_experts(): lax.all_to_all(v, 'expert', 0, 0, axis_index_groups=groups, tiled=True)]
    ppermute x5, waiting for transfers between devices: 6.79 us -> 0.01 us  [swap_core(): return lax.ppermute(v, 'seq', [(i, i ^ 1) for i in range(self.seq)])]
    unnamed x82 -> x92, local copies, waits for them, and re-layouts: 12.8 us -> 9.09 us
    ppermute x18 -> x17, starting transfers between devices: 22 us -> 18.7 us  [turn_chip(): lax.ppermute(v, 'seq', [(i, (i // 2 + p) % n * 2 + i % 2) for i in range(...]
  transfers between devices with their start and end apart: 41 -> 41, of which waited for: 16 -> 14; matrix products, arithmetic and copies ran while one was open for 7% -> 9% of each run, Pallas kernels for 41% -> 36%
where the time goes in v3:
time: 324 us; the launch traced here: 323 us
  Pallas kernels  129 us (40%)
  waiting for transfers between devices  89.2 us (28%)
  starting transfers between devices  64.9 us (20%)
  other arithmetic  21.4 us (7%)
  local copies, waits for them, and re-layouts  14.1 us (4%)
    pallas_call x7, Pallas kernels, project(): pl.pallas_call(body, grid=(units // tile,), in_specs=[pl.BlockSpec(memory...  72.3 us
    ppermute x17, waiting for transfers between devices, turn_chip(): lax.ppermute(v, 'seq', [(i, (i // 2 + p) % n * 2 + i % 2) for i in range(...  48.5 us
    pallas_call x3, Pallas kernels, project_back(): pl.pallas_call(body, grid=(halves * steps,), in_specs=[pl.BlockSpec(memor...  34.6 us
    all_to_all x6, starting transfers between devices, between_experts(): lax.all_to_all(v, 'expert', 0, 0, axis_index_groups=groups, tiled=True)  28.3 us
    ppermute x17, starting transfers between devices, turn_chip(): lax.ppermute(v, 'seq', [(i, (i // 2 + p) % n * 2 + i % 2) for i in range(...  18.7 us
    all_to_all x6, waiting for transfers between devices, between_experts(): lax.all_to_all(v, 'expert', 0, 0, axis_index_groups=groups, tiled=True)  17.9 us
    ppermute x8, waiting for transfers between devices, turn_slice(): lax.ppermute(v, 'expert', [(i, i // m * m + (i % m + k) % m) for i in ran...  11.3 us
    unnamed x92, local copies, waits for them, and re-layouts  9.09 us
  transfers between devices with their start and end apart: 41, of which 14 were waited for; matrix products, arithmetic and copies ran while one was open for 9% of the time, Pallas kernels for 36%

profile of v3, /device:TPU:0, one launch (start us, length us, event | category | flops | bytes accessed | tf_op | source)
XLA Modules:
  0.0 323.3 jit_solution(3331193782133248846)
XLA Ops:
  3.7 3.0 collective-permute-start.2
  13.7 3.9 %collective-permute-start = (f32[2,2,128,128]{3,2,1,0:T(8,128)S(1)}, f32[2,2,128,128]{3,2,1,0:T(8,128)S(1)}, u32[]{:S(2)}, u32[]{:S(2)}) collective-permute-start(f32[2,2,128,128]{3,2,1,0:T(8,128)S(1)} %key_value_state.1.refs_2_), channel_id=1, source_target_pairs={{0,16},{8,24},{1,17},{9,25},{2,18},{10,26},{3,19},{11,27},{4,20},{... | collective-permute-start | bytes 786440 | tf_op jit(solution)/shard_map/ppermute | solution.py:40
  21.2 3.0 collective-permute-done.refs_3_
  24.3 7.0 %collective-permute-done.4.refs_1_ = bf16[2,64,1536]{2,1,0:T(8,128)(2,1)S(1)} collective-permute-done((bf16[2,64,1536]{2,1,0:T(8,128)(2,1)}, bf16[2,64,1536]{2,1,0:T(8,128)(2,1)S(1)}, u32[]{:S(2)}, u32[]{:S(2)}) %collective-permute-start.4) | collective-permute-done | bytes 393248 | tf_op jit(solution)/shard_map/ppermute | solution.py:34
  34.2 5.0 %all-to-all-start = ((bf16[4,2,32,1536]{3,2,1,0:T(8,128)(2,1)}), bf16[4,2,32,1536]{3,2,1,0:T(8,128)(2,1)S(1)}, u32[]{:S(2)}, u32[]{:S(2)}) async-start(bf16[4,2,32,1536]{3,2,1,0:T(8,128)(2,1)} %pick_rows.4.refs_2_), calls=%async_computation | async-start | bytes 1572864 | tf_op jit(solution)/shard_map/all_to_all | solution.py:45
  42.0 17.9 %all-to-all-done.refs_0_ = bf16[4,2,32,1536]{3,2,1,0:T(8,128)(2,1)S(1)} async-done(((bf16[4,2,32,1536]{3,2,1,0:T(8,128)(2,1)}), bf16[4,2,32,1536]{3,2,1,0:T(8,128)(2,1)S(1)}, u32[]{:S(2)}, u32[]{:S(2)}) %all-to-all-start) | async-done | bytes 786464 | tf_op jit(solution)/shard_map/all_to_all | solution.py:45
  59.9 3.5 %all-to-all-start.1 = ((bf16[4,2,32,1536]{3,2,1,0:T(8,128)(2,1)}), bf16[4,2,32,1536]{3,2,1,0:T(8,128)(2,1)S(1)}, u32[]{:S(2)}, u32[]{:S(2)}) async-start(bf16[4,2,32,1536]{3,2,1,0:T(8,128)(2,1)} %pick_rows.6.refs_2_), calls=%async_computation.1 | async-start | bytes 1572864 | tf_op jit(solution)/shard_map/all_to_all | solution.py:45
  65.4 11.0 %project.7 = (f32[2,64,2304]{2,1,0:T(8,128)S(1)}, f32[1,2,64,2304]{3,2,1,0:T(8,128)S(1)}) custom-call(s32[1]{0:T(128)} %bitcast.4.chip_ref, bf16[4,2,32,1536]{3,2,1,0:T(8,128)(2,1)S(1)} %all-to-all-done.refs_0_, bf16[1536,2304]{1,0:T(8,128)(2,1)} %bitcast.174, bf16[1536,2304]{1,0:T(8,128)(2,1)} %collective-permute-done.5.refs_3_.refs_2_.refs_6_.refs_4_, ...), custom_call_target="tpu_custom_call" | custom-call | flops 1000 | bytes 1000 | tf_op jit(solution)/shard_map/project/pallas_call | solution.py:145
  79.8 7.2 %local_grads.1 = (bf16[2,256,256]{2,1,0:T(8,128)(2,1)}, f32[2,256,256]{2,1,0:T(8,128)S(1)}, f32[2,256,256]{2,1,0:T(8,128)S(1)}, f32[2,2,128,128]{3,2,1,0:T(8,128)}) custom-call(f32[2]{0:T(128)S(1)} %copy-done.29, bf16[2,256,256]{2,1,0:T(8,128)(2,1)S(1)} %copy-done.25, bf16[2,256,256]{2,1,0:T(8,128)(2,1)S(1)} %copy-done.2, ...), custom_call_target="tpu_custom_call" | custom-call | flops 1000 | bytes 1000 | tf_op jit(solution)/shard_map/local_grads/pallas_call | solution.py:394
  88.6 5.2 %all-to-all-start.2 = ((bf16[4,2,40,1536]{3,2,1,0:T(8,128)(2,1)}), bf16[4,2,40,1536]{3,2,1,0:T(8,128)(2,1)}, u32[]{:S(2)}, u32[]{:S(2)}) async-start(bf16[4,2,40,1536]{3,2,1,0:T(8,128)(2,1)} %pick_rows.5.refs_2_), calls=%async_computation.2 | async-start | bytes 1966080 | tf_op jit(solution)/shard_map/all_to_all | solution.py:45
  94.3 6.7 %project.8 = (f32[1,64,2304]{2,1,0:T(8,128)S(1)}, f32[1,1,64,2304]{3,2,1,0:T(8,128)S(1)}) custom-call(s32[1]{0:T(128)} %bitcast.4.chip_ref, bf16[4,2,32,1536]{3,2,1,0:T(8,128)(2,1)S(1)} %all-to-all-done.1.refs_0_, bf16[1536,2304]{1,0:T(8,128)(2,1)} %bitcast.23.refs_1_.refs_6_, bf16[1536,2304]{1,0:T(8,128)(2,1)} %collective-permute-done.8.refs_2_.refs_7_, ...), custom_call_target="tpu_custom_call" | custom-call | flops 1000 | bytes 1000 | tf_op jit(solution)/shard_map/project/pallas_call | solution.py:145
  102.6 5.3 %collective-permute-done.9 = f16[1,64,2304]{2,1,0:T(8,128)(2,1)S(1)} collective-permute-done((f16[1,64,2304]{2,1,0:T(8,128)(2,1)S(1)}, f16[1,64,2304]{2,1,0:T(8,128)(2,1)S(1)}, u32[]{:S(2)}, u32[]{:S(2)}) %collective-permute-start.9) | collective-permute-done | bytes 294944 | tf_op jit(solution)/shard_map/ppermute | solution.py:34
  111.4 16.3 %project.9 = (f32[3,64,2304]{2,1,0:T(8,128)S(1)}, f32[1,3,64,2304]{3,2,1,0:T(8,128)S(1)}) custom-call(s32[1]{0:T(128)} %bitcast.4.chip_ref, bf16[4,2,32,1536]{3,2,1,0:T(8,128)(2,1)} %collective-permute-done.7.refs_0_, bf16[4,2,32,1536]{3,2,1,0:T(8,128)(2,1)S(1)} %collective-permute-done.11.refs_1_, bf16[1536,2304]{1,0:T(8,128)(2,1)} %bitcast.175, ...), custom_call_target="tpu_custom_call" | custom-call | flops 1000 | bytes 1000 | tf_op jit(solution)/shard_map/project/pallas_call | solution.py:145
  130.2 2.7 collective-permute-start.17
  132.9 4.8 %all-to-all-start.3 = ((bf16[4,2,40,1536]{3,2,1,0:T(8,128)(2,1)}), bf16[4,2,40,1536]{3,2,1,0:T(8,128)(2,1)}, u32[]{:S(2)}, u32[]{:S(2)}) async-start(bf16[4,2,40,1536]{3,2,1,0:T(8,128)(2,1)} %pick_rows.7.refs_5_), calls=%async_computation.3 | async-start | bytes 1966080 | tf_op jit(solution)/shard_map/all_to_all | solution.py:45
  141.0 12.4 %project.10 = (f32[2,72,2304]{2,1,0:T(8,128)S(1)}, f32[1,2,72,2304]{3,2,1,0:T(8,128)S(1)}) custom-call(s32[1]{0:T(128)} %bitcast.4.chip_ref, bf16[4,2,40,1536]{3,2,1,0:T(8,128)(2,1)} %all-to-all-done.2.refs_0_, bf16[1536,2304]{1,0:T(8,128)(2,1)} %bitcast.176, bf16[1536,2304]{1,0:T(8,128)(2,1)} %collective-permute-done.5.refs_3_.refs_2_.refs_6_.refs_4_, ...), custom_call_target="tpu_custom_call" | custom-call | flops 1000 | bytes 1000 | tf_op jit(solution)/shard_map/project/pallas_call | solution.py:145
  159.2 11.6 %project.11 = (f32[2,72,2304]{2,1,0:T(8,128)S(1)}, f32[1,2,72,2304]{3,2,1,0:T(8,128)S(1)}) custom-call(s32[1]{0:T(128)} %bitcast.4.chip_ref, bf16[4,2,40,1536]{3,2,1,0:T(8,128)(2,1)S(1)} %collective-permute-done.19.refs_0_, bf16[1536,2304]{1,0:T(8,128)(2,1)} %bitcast.177, bf16[1536,2304]{1,0:T(8,128)(2,1)} %collective-permute-done.5.refs_3_.refs_2_.refs_6_.refs_4_, ...), custom_call_target="tpu_custom_call" | custom-call | flops 1000 | bytes 1000 | tf_op jit(solution)/shard_map/project/pallas_call | solution.py:145
  174.1 7.3 %project.12 = (f32[1,72,2304]{2,1,0:T(8,128)S(1)}, f32[1,1,72,2304]{3,2,1,0:T(8,128)S(1)}) custom-call(s32[1]{0:T(128)} %bitcast.4.chip_ref, bf16[4,2,40,1536]{3,2,1,0:T(8,128)(2,1)} %all-to-all-done.3.refs_0_, bf16[1536,2304]{1,0:T(8,128)(2,1)} %bitcast.23.refs_1_.refs_6_, bf16[1536,2304]{1,0:T(8,128)(2,1)} %collective-permute-done.8.refs_2_.refs_7_, ...), custom_call_target="tpu_custom_call" | custom-call | flops 1000 | bytes 1000 | tf_op jit(solution)/shard_map/project/pallas_call | solution.py:145
  181.5 3.5 %collective-permute-done.18.refs_3_ = bf16[2,64,2304]{2,1,0:T(8,128)(2,1)} collective-permute-done((bf16[2,64,2304]{2,1,0:T(8,128)(2,1)}, bf16[2,64,2304]{2,1,0:T(8,128)(2,1)}, u32[]{:S(2)}, u32[]{:S(2)}) %collective-permute-start.18) | collective-permute-done | bytes 589856 | tf_op jit(solution)/shard_map/ppermute | solution.py:34
  185.1 16.2 %project_back.3 = (bf16[4,2,32,1536]{3,2,1,0:T(8,128)(2,1)S(1)}, bf16[4,2,32,1536]{3,2,1,0:T(8,128)(2,1)S(1)}) custom-call(s32[1]{0:T(128)} %bitcast.4.chip_ref, bf16[2,64,2304]{2,1,0:T(8,128)(2,1)S(1)} %copy-done.7, bf16[2,64,2304]{2,1,0:T(8,128)(2,1)} %collective-permute-done.15.refs_1_, bf16[2,64,2304]{2,1,0:T(8,128)(2,1)} %multiply_convert_fusion.5.refs_2_, ...), custom_call_target="tpu_custom_call" | custom-call | flops 1000 | bytes 1000 | tf_op jit(solution)/shard_map/project_back/pallas_call | solution.py:226
  202.1 7.0 %project.13 = (f32[1,72,2304]{2,1,0:T(8,128)S(1)}, f32[1,1,72,2304]{3,2,1,0:T(8,128)S(1)}) custom-call(s32[1]{0:T(128)} %bitcast.4.chip_ref, bf16[4,2,40,1536]{3,2,1,0:T(8,128)(2,1)S(1)} %collective-permute-done.14.refs_0_, bf16[1536,2304]{1,0:T(8,128)(2,1)} %bitcast.23.refs_1_.refs_6_, bf16[1536,2304]{1,0:T(8,128)(2,1)} %collective-permute-done.8.refs_2_.refs_7_, ...), custom_call_target="tpu_custom_call" | custom-call | flops 1000 | bytes 1000 | tf_op jit(solution)/shard_map/project/pallas_call | solution.py:145
  211.4 6.7 %collective-permute-done.22 = f16[1,72,2304]{2,1,0:T(8,128)(2,1)S(1)} collective-permute-done((f16[1,72,2304]{2,1,0:T(8,128)(2,1)S(1)}, f16[1,72,2304]{2,1,0:T(8,128)(2,1)S(1)}, u32[]{:S(2)}, u32[]{:S(2)}) %collective-permute-start.22) | collective-permute-done | bytes 331808 | tf_op jit(solution)/shard_map/ppermute | solution.py:34
  227.5 20.6 %collective-permute-done.24.refs_1_ = bf16[2,72,2304]{2,1,0:T(8,128)(2,1)S(1)} collective-permute-done((bf16[2,72,2304]{2,1,0:T(8,128)(2,1)S(1)}, bf16[2,72,2304]{2,1,0:T(8,128)(2,1)S(1)}, u32[]{:S(2)}, u32[]{:S(2)}) %collective-permute-start.24) | collective-permute-done | bytes 663584 | tf_op jit(solution)/shard_map/ppermute | solution.py:34
  248.0 9.3 %project_back.4 = (bf16[4,1,36,1536]{3,2,1,0:T(8,128)(2,1)S(1)}, bf16[4,1,36,1536]{3,2,1,0:T(8,128)(2,1)}) custom-call(s32[1]{0:T(128)} %bitcast.4.chip_ref, bf16[2,72,2304]{2,1,0:T(8,128)(2,1)S(1)} %multiply_convert_fusion.1.refs_0_, bf16[2,72,2304]{2,1,0:T(8,128)(2,1)S(1)} %collective-permute-done.24.refs_1_, ...), custom_call_target="tpu_custom_call" | custom-call | flops 1000 | bytes 1000 | tf_op jit(solution)/shard_map/project_back/pallas_call | solution.py:226
  260.8 4.8 %all-to-all-start.4 = ((bf16[4,2,32,1536]{3,2,1,0:T(8,128)(2,1)}), bf16[4,2,32,1536]{3,2,1,0:T(8,128)(2,1)S(1)}, u32[]{:S(2)}, u32[]{:S(2)}) async-start(bf16[4,2,32,1536]{3,2,1,0:T(8,128)(2,1)} %add_convert_fusion.refs_7_), calls=%async_computation.4 | async-start | bytes 1572864 | tf_op jit(solution)/shard_map/all_to_all | solution.py:45
  266.6 9.0 %project_back.5 = (bf16[4,1,36,1536]{3,2,1,0:T(8,128)(2,1)S(1)}, bf16[4,1,36,1536]{3,2,1,0:T(8,128)(2,1)}) custom-call(s32[1]{0:T(128)} %bitcast.4.chip_ref, bf16[2,72,2304]{2,1,0:T(8,128)(2,1)S(1)} %multiply_convert_fusion.1.refs_0_, bf16[2,72,2304]{2,1,0:T(8,128)(2,1)S(1)} %collective-permute-done.24.refs_1_, ...), custom_call_target="tpu_custom_call" | custom-call | flops 1000 | bytes 1000 | tf_op jit(solution)/shard_map/project_back/pallas_call | solution.py:226
  279.3 6.6 %collective-permute-done.27 = bf16[4,1,36,1536]{3,2,1,0:T(8,128)(2,1)S(1)} collective-permute-done((bf16[4,1,36,1536]{3,2,1,0:T(8,128)(2,1)}, bf16[4,1,36,1536]{3,2,1,0:T(8,128)(2,1)S(1)}, u32[]{:S(2)}, u32[]{:S(2)}) %collective-permute-start.27) | collective-permute-done | bytes 442400 | tf_op jit(solution)/shard_map/ppermute | solution.py:55
  287.7 4.9 %all-to-all-start.5 = ((bf16[4,2,36,1536]{3,1,2,0:T(2,128)(2,1)}), bf16[4,2,36,1536]{3,1,2,0:T(2,128)(2,1)S(1)}, u32[]{:S(2)}, u32[]{:S(2)}) async-start(bf16[4,2,36,1536]{3,1,2,0:T(2,128)(2,1)} %copy.93), calls=%async_computation.5 | async-start | bytes 1769472 | tf_op jit(solution)/shard_map/all_to_all | solution.py:45
  294.2 2.5 collective-permute-done.29
  296.8 3.8 %collective-permute-start.32 = (f32[4,68]{1,0:T(4,128)S(1)}, f32[4,68]{1,0:T(4,128)S(1)}, u32[]{:S(2)}, u32[]{:S(2)}) collective-permute-start(f32[4,68]{1,0:T(4,128)S(1)} %convert_add_fusion), channel_id=1, source_target_pairs={{0,6},{1,7},{2,0},{3,1},{4,2},{5,3},{6,4},{7,5},{8,14},{9,15},{10,... | collective-permute-start | bytes 3272 | tf_op jit(solution)/shard_map/ppermute | solution.py:49
  302.5 7.6 %collective-permute-done.31 = f32[4,68]{1,0:T(4,128)S(1)} collective-permute-done((f32[4,68]{1,0:T(4,128)S(1)}, f32[4,68]{1,0:T(4,128)S(1)}, u32[]{:S(2)}, u32[]{:S(2)}) %collective-permute-start.31) | collective-permute-done | bytes 1120 | tf_op jit(solution)/shard_map/ppermute | solution.py:49
  317.1 5.2 %collective-permute-done.33 = bf16[64,1536]{1,0:T(8,128)(2,1)S(1)} collective-permute-done((bf16[64,1536]{1,0:T(8,128)(2,1)S(1)}, bf16[64,1536]{1,0:T(8,128)(2,1)S(1)}, u32[]{:S(2)}, u32[]{:S(2)}) %collective-permute-start.33) | collective-permute-done | bytes 196640 | tf_op jit(solution)/shard_map/ppermute | solution.py:34
  (247 shorter events, 78.9 us)
Async XLA Ops:
  0.7 32.0 %collective-permute-start.5 = (bf16[1536,2304]{1,0:T(8,128)(2,1)}, bf16[1536,2304]{1,0:T(8,128)(2,1)}, u32[]{:S(2)}, u32[]{:S(2)}) collective-permute-start(bf16[1536,2304]{1,0:T(8,128)(2,1)} %bitcast.173), channel_id=1, source_target_pairs={{0,8},{8,0},{16,24},{24,16},{1,9},{9,1},{17,25},{25,17},{2,10},{10... | collective-permute-start | bytes 21233672 | tf_op jit(solution)/shard_map/ppermute | solution.py:30
  1.2 31.5 %collective-permute-start.6 = (bf16[1536,2304]{1,0:T(8,128)(2,1)}, bf16[1536,2304]{1,0:T(8,128)(2,1)}, u32[]{:S(2)}, u32[]{:S(2)}) collective-permute-start(bf16[1536,2304]{1,0:T(8,128)(2,1)} %bitcast.180), channel_id=1, source_target_pairs={{0,8},{8,0},{16,24},{24,16},{1,9},{9,1},{17,25},{25,17},{2,10},{10... | collective-permute-start | bytes 21233672 | tf_op jit(solution)/shard_map/ppermute | solution.py:30
  3.7 13.9 %collective-permute-start.2 = (f32[64,8]{0,1:T(8,128)S(1)}, f32[64,8]{0,1:T(8,128)S(1)}, u32[]{:S(2)}, u32[]{:S(2)}) collective-permute-start(f32[64,8]{0,1:T(8,128)S(1)} %get-tuple-element.155), channel_id=1, source_target_pairs={{0,16},{8,24},{16,0},{24,8},{1,17},{9,25},{17,1},{25,9},{2,18},{10... | collective-permute-start | bytes 6152 | tf_op jit(solution)/shard_map/ppermute | solution.py:34
  7.4 10.9 %collective-permute-start.3 = (bf16[2,64,1536]{2,1,0:T(8,128)(2,1)S(1)}, bf16[2,64,1536]{2,1,0:T(8,128)(2,1)S(1)}, u32[]{:S(2)}, u32[]{:S(2)}) collective-permute-start(bf16[2,64,1536]{2,1,0:T(8,128)(2,1)S(1)} %bitcast.172), channel_id=1, source_target_pairs={{0,16},{8,24},{16,0},{24,8},{1,17},{9,25},{17,1},{25,9},{2,18},{10... | collective-permute-start | bytes 1179656 | tf_op jit(solution)/shard_map/ppermute | solution.py:34
  13.7 10.6 %collective-permute-start = (f32[2,2,128,128]{3,2,1,0:T(8,128)S(1)}, f32[2,2,128,128]{3,2,1,0:T(8,128)S(1)}, u32[]{:S(2)}, u32[]{:S(2)}) collective-permute-start(f32[2,2,128,128]{3,2,1,0:T(8,128)S(1)} %key_value_state.1.refs_2_), channel_id=1, source_target_pairs={{0,16},{8,24},{1,17},{9,25},{2,18},{10,26},{3,19},{11,27},{4,20},{... | collective-permute-start | bytes 786440 | tf_op jit(solution)/shard_map/ppermute | solution.py:40
  17.6 13.7 %collective-permute-start.4 = (bf16[2,64,1536]{2,1,0:T(8,128)(2,1)}, bf16[2,64,1536]{2,1,0:T(8,128)(2,1)S(1)}, u32[]{:S(2)}, u32[]{:S(2)}) collective-permute-start(bf16[2,64,1536]{2,1,0:T(8,128)(2,1)} %bitcast.20), channel_id=1, source_target_pairs={{0,16},{8,24},{16,0},{24,8},{1,17},{9,25},{17,1},{25,9},{2,18},{10... | collective-permute-start | bytes 1179656 | tf_op jit(solution)/shard_map/ppermute | solution.py:34
  34.2 60.1 %collective-permute-start.8 = (bf16[1536,2304]{1,0:T(8,128)(2,1)}, bf16[1536,2304]{1,0:T(8,128)(2,1)}, u32[]{:S(2)}, u32[]{:S(2)}) collective-permute-start(bf16[1536,2304]{1,0:T(8,128)(2,1)} %bitcast.23.refs_1_.refs_6_), channel_id=1, source_target_pairs={{0,8},{8,0},{16,24},{24,16},{1,9},{9,1},{17,25},{25,17},{2,10},{10... | collective-permute-start | bytes 21233672 | tf_op jit(solution)/shard_map/ppermute | solution.py:30
  34.2 25.7 %all-to-all-start = ((bf16[4,2,32,1536]{3,2,1,0:T(8,128)(2,1)}), bf16[4,2,32,1536]{3,2,1,0:T(8,128)(2,1)S(1)}, u32[]{:S(2)}, u32[]{:S(2)}) async-start(bf16[4,2,32,1536]{3,2,1,0:T(8,128)(2,1)} %pick_rows.4.refs_2_), calls=%async_computation | async-start | bytes 1572864 | tf_op jit(solution)/shard_map/all_to_all | solution.py:45
  40.8 22.6 %collective-permute-start.1 = (f32[2,2,2,128,128]{4,3,2,1,0:T(8,128)}, f32[2,2,2,128,128]{4,3,2,1,0:T(8,128)S(1)}, u32[]{:S(2)}, u32[]{:S(2)}) collective-permute-start(f32[2,2,2,128,128]{4,3,2,1,0:T(8,128)} %pad_maximum_fusion.1), channel_id=1, source_target_pairs={{0,8},{8,0},{16,24},{24,16},{1,9},{9,1},{17,25},{25,17},{2,10},{10... | collective-permute-start | bytes 1572872 | tf_op jit(solution)/shard_map/ppermute | solution.py:30
  59.9 28.8 %all-to-all-start.1 = ((bf16[4,2,32,1536]{3,2,1,0:T(8,128)(2,1)}), bf16[4,2,32,1536]{3,2,1,0:T(8,128)(2,1)S(1)}, u32[]{:S(2)}, u32[]{:S(2)}) async-start(bf16[4,2,32,1536]{3,2,1,0:T(8,128)(2,1)} %pick_rows.6.refs_2_), calls=%async_computation.1 | async-start | bytes 1572864 | tf_op jit(solution)/shard_map/all_to_all | solution.py:45
  63.9 47.5 %collective-permute-start.7 = (bf16[4,2,32,1536]{3,2,1,0:T(8,128)(2,1)S(1)}, bf16[4,2,32,1536]{3,2,1,0:T(8,128)(2,1)}, u32[]{:S(2)}, u32[]{:S(2)}) collective-permute-start(bf16[4,2,32,1536]{3,2,1,0:T(8,128)(2,1)S(1)} %all-to-all-done.refs_0_), channel_id=1, source_target_pairs={{0,1},{1,0},{2,3},{3,2},{4,5},{5,4},{6,7},{7,6},{8,9},{9,8},{10,11... | collective-permute-start | bytes 2359304 | tf_op jit(solution)/shard_map/ppermute | solution.py:55
  77.4 24.0 %collective-permute-start.10 = (f16[2,64,2304]{2,1,0:T(8,128)(2,1)}, f16[2,64,2304]{2,1,0:T(8,128)(2,1)}, u32[]{:S(2)}, u32[]{:S(2)}) collective-permute-start(f16[2,64,2304]{2,1,0:T(8,128)(2,1)} %fusion.8), channel_id=1, source_target_pairs={{0,16},{8,24},{16,0},{24,8},{1,17},{9,25},{17,1},{25,9},{2,18},{10... | collective-permute-start | bytes 1769480 | tf_op jit(solution)/shard_map/ppermute | solution.py:34
  88.6 44.2 %all-to-all-start.2 = ((bf16[4,2,40,1536]{3,2,1,0:T(8,128)(2,1)}), bf16[4,2,40,1536]{3,2,1,0:T(8,128)(2,1)}, u32[]{:S(2)}, u32[]{:S(2)}) async-start(bf16[4,2,40,1536]{3,2,1,0:T(8,128)(2,1)} %pick_rows.5.refs_2_), calls=%async_computation.2 | async-start | bytes 1966080 | tf_op jit(solution)/shard_map/all_to_all | solution.py:45
  93.8 17.6 %collective-permute-start.11 = (bf16[4,2,32,1536]{3,2,1,0:T(8,128)(2,1)S(1)}, bf16[4,2,32,1536]{3,2,1,0:T(8,128)(2,1)S(1)}, u32[]{:S(2)}, u32[]{:S(2)}) collective-permute-start(bf16[4,2,32,1536]{3,2,1,0:T(8,128)(2,1)S(1)} %all-to-all-done.1.refs_0_), channel_id=1, source_target_pairs={{0,1},{1,0},{2,3},{3,2},{4,5},{5,4},{6,7},{7,6},{8,9},{9,8},{10,11... | collective-permute-start | bytes 2359304 | tf_op jit(solution)/shard_map/ppermute | solution.py:55
  108.5 32.5 %collective-permute-start.15 = (bf16[2,64,2304]{2,1,0:T(8,128)(2,1)S(1)}, bf16[2,64,2304]{2,1,0:T(8,128)(2,1)}, u32[]{:S(2)}, u32[]{:S(2)}) collective-permute-start(bf16[2,64,2304]{2,1,0:T(8,128)(2,1)S(1)} %multiply_convert_fusion.6.refs_0_), channel_id=1, source_target_pairs={{0,16},{8,24},{16,0},{24,8},{1,17},{9,25},{17,1},{25,9},{2,18},{10... | collective-permute-start | bytes 1769480 | tf_op jit(solution)/shard_map/ppermute | solution.py:34
  127.7 11.3 %collective-permute-start.12 = (f32[2,2,128,128]{3,2,1,0:T(8,128)}, f32[2,2,128,128]{3,2,1,0:T(8,128)S(1)}, u32[]{:S(2)}, u32[]{:S(2)}) collective-permute-start(f32[2,2,128,128]{3,2,1,0:T(8,128)} %get-tuple-element.78), channel_id=1, source_target_pairs={{16,0},{24,8},{17,1},{25,9},{18,2},{26,10},{19,3},{27,11},{20,4},{... | collective-permute-start | bytes 786440 | tf_op jit(solution)/shard_map/ppermute | solution.py:40
  130.2 24.1 %collective-permute-start.17 = (f16[3,64,2304]{2,1,0:T(8,128)(2,1)}, f16[3,64,2304]{2,1,0:T(8,128)(2,1)}, u32[]{:S(2)}, u32[]{:S(2)}) collective-permute-start(f16[3,64,2304]{2,1,0:T(8,128)(2,1)} %fusion.1), channel_id=1, source_target_pairs={{0,16},{8,24},{16,0},{24,8},{1,17},{9,25},{17,1},{25,9},{2,18},{10... | collective-permute-start | bytes 2654216 | tf_op jit(solution)/shard_map/ppermute | solution.py:34
  132.9 39.0 %all-to-all-start.3 = ((bf16[4,2,40,1536]{3,2,1,0:T(8,128)(2,1)}), bf16[4,2,40,1536]{3,2,1,0:T(8,128)(2,1)}, u32[]{:S(2)}, u32[]{:S(2)}) async-start(bf16[4,2,40,1536]{3,2,1,0:T(8,128)(2,1)} %pick_rows.7.refs_5_), calls=%async_computation.3 | async-start | bytes 1966080 | tf_op jit(solution)/shard_map/all_to_all | solution.py:45
  137.7 21.5 %collective-permute-start.19 = (bf16[4,2,40,1536]{3,2,1,0:T(8,128)(2,1)}, bf16[4,2,40,1536]{3,2,1,0:T(8,128)(2,1)S(1)}, u32[]{:S(2)}, u32[]{:S(2)}) collective-permute-start(bf16[4,2,40,1536]{3,2,1,0:T(8,128)(2,1)} %all-to-all-done.2.refs_0_), channel_id=1, source_target_pairs={{0,1},{1,0},{2,3},{3,2},{4,5},{5,4},{6,7},{7,6},{8,9},{9,8},{10,11... | collective-permute-start | bytes 2949128 | tf_op jit(solution)/shard_map/ppermute | solution.py:55
  141.0 81.9 %collective-permute-start.13 = (f32[2,2,2,128,128]{4,3,2,1,0:T(8,128)}, f32[2,2,2,128,128]{4,3,2,1,0:T(8,128)}, u32[]{:S(2)}, u32[]{:S(2)}) collective-permute-start(f32[2,2,2,128,128]{4,3,2,1,0:T(8,128)} %pad_maximum_fusion.2), channel_id=1, source_target_pairs={{0,8},{8,0},{16,24},{24,16},{1,9},{9,1},{17,25},{25,17},{2,10},{10... | collective-permute-start | bytes 1572872 | tf_op jit(solution)/shard_map/ppermute | solution.py:30
  154.3 47.0 %collective-permute-start.16 = (f16[2,72,2304]{2,1,0:T(8,128)(2,1)}, f16[2,72,2304]{2,1,0:T(8,128)(2,1)}, u32[]{:S(2)}, u32[]{:S(2)}) collective-permute-start(f16[2,72,2304]{2,1,0:T(8,128)(2,1)} %fusion.2), channel_id=1, source_target_pairs={{0,16},{8,24},{16,0},{24,8},{1,17},{9,25},{17,1},{25,9},{2,18},{10... | collective-permute-start | bytes 1990664 | tf_op jit(solution)/shard_map/ppermute | solution.py:34
  157.2 27.8 %collective-permute-start.18 = (bf16[2,64,2304]{2,1,0:T(8,128)(2,1)}, bf16[2,64,2304]{2,1,0:T(8,128)(2,1)}, u32[]{:S(2)}, u32[]{:S(2)}) collective-permute-start(bf16[2,64,2304]{2,1,0:T(8,128)(2,1)} %multiply_convert_fusion.5.refs_2_), channel_id=1, source_target_pairs={{0,16},{8,24},{16,0},{24,8},{1,17},{9,25},{17,1},{25,9},{2,18},{10... | collective-permute-start | bytes 1769480 | tf_op jit(solution)/shard_map/ppermute | solution.py:34
  171.9 30.2 %collective-permute-start.14 = (bf16[4,2,40,1536]{3,2,1,0:T(8,128)(2,1)}, bf16[4,2,40,1536]{3,2,1,0:T(8,128)(2,1)S(1)}, u32[]{:S(2)}, u32[]{:S(2)}) collective-permute-start(bf16[4,2,40,1536]{3,2,1,0:T(8,128)(2,1)} %all-to-all-done.3.refs_0_), channel_id=1, source_target_pairs={{0,1},{1,0},{2,3},{3,2},{4,5},{5,4},{6,7},{7,6},{8,9},{9,8},{10,11... | collective-permute-start | bytes 2949128 | tf_op jit(solution)/shard_map/ppermute | solution.py:55
  174.0 37.2 %collective-permute-start.23 = (f16[2,72,2304]{2,1,0:T(8,128)(2,1)S(1)}, f16[2,72,2304]{2,1,0:T(8,128)(2,1)S(1)}, u32[]{:S(2)}, u32[]{:S(2)}) collective-permute-start(f16[2,72,2304]{2,1,0:T(8,128)(2,1)S(1)} %fusion.3), channel_id=1, source_target_pairs={{0,16},{8,24},{16,0},{24,8},{1,17},{9,25},{17,1},{25,9},{2,18},{10... | collective-permute-start | bytes 1990664 | tf_op jit(solution)/shard_map/ppermute | solution.py:34
  185.0 36.6 %collective-permute-start.21 = (f16[1,72,2304]{2,1,0:T(8,128)(2,1)S(1)}, f16[1,72,2304]{2,1,0:T(8,128)(2,1)S(1)}, u32[]{:S(2)}, u32[]{:S(2)}) collective-permute-start(f16[1,72,2304]{2,1,0:T(8,128)(2,1)S(1)} %fusion.12), channel_id=1, source_target_pairs={{0,16},{8,24},{16,0},{24,8},{1,17},{9,25},{17,1},{25,9},{2,18},{10... | collective-permute-start | bytes 995336 | tf_op jit(solution)/shard_map/ppermute | solution.py:34
  201.4 25.0 %collective-permute-start.20 = (bf16[4,2,32,1536]{3,2,1,0:T(8,128)(2,1)S(1)}, bf16[4,2,32,1536]{3,2,1,0:T(8,128)(2,1)S(1)}, u32[]{:S(2)}, u32[]{:S(2)}) collective-permute-start(bf16[4,2,32,1536]{3,2,1,0:T(8,128)(2,1)S(1)} %get-tuple-element.94), channel_id=1, source_target_pairs={{0,1},{1,0},{2,3},{3,2},{4,5},{5,4},{6,7},{7,6},{8,9},{9,8},{10,11... | collective-permute-start | bytes 2359304 | tf_op jit(solution)/shard_map/ppermute | solution.py:55
  218.7 29.3 %collective-permute-start.25 = (bf16[2,72,2304]{2,1,0:T(8,128)(2,1)S(1)}, bf16[2,72,2304]{2,1,0:T(8,128)(2,1)S(1)}, u32[]{:S(2)}, u32[]{:S(2)}) collective-permute-start(bf16[2,72,2304]{2,1,0:T(8,128)(2,1)S(1)} %multiply_convert_fusion.2.refs_2_), channel_id=1, source_target_pairs={{0,16},{8,24},{16,0},{24,8},{1,17},{9,25},{17,1},{25,9},{2,18},{10... | collective-permute-start | bytes 1990664 | tf_op jit(solution)/shard_map/ppermute | solution.py:34
  222.4 25.7 %collective-permute-start.24 = (bf16[2,72,2304]{2,1,0:T(8,128)(2,1)S(1)}, bf16[2,72,2304]{2,1,0:T(8,128)(2,1)S(1)}, u32[]{:S(2)}, u32[]{:S(2)}) collective-permute-start(bf16[2,72,2304]{2,1,0:T(8,128)(2,1)S(1)} %multiply_convert_fusion.1.refs_0_), channel_id=1, source_target_pairs={{0,16},{8,24},{16,0},{24,8},{1,17},{9,25},{17,1},{25,9},{2,18},{10... | collective-permute-start | bytes 1990664 | tf_op jit(solution)/shard_map/ppermute | solution.py:34
  258.1 19.9 %collective-permute-start.26 = (bf16[4,1,36,1536]{3,2,1,0:T(8,128)(2,1)}, bf16[4,1,36,1536]{3,2,1,0:T(8,128)(2,1)}, u32[]{:S(2)}, u32[]{:S(2)}) collective-permute-start(bf16[4,1,36,1536]{3,2,1,0:T(8,128)(2,1)} %get-tuple-element.102), channel_id=1, source_target_pairs={{0,1},{1,0},{2,3},{3,2},{4,5},{5,4},{6,7},{7,6},{8,9},{9,8},{10,11... | collective-permute-start | bytes 1327112 | tf_op jit(solution)/shard_map/ppermute | solution.py:55
  259.6 17.8 %collective-permute-start.28 = (bf16[272]{0:T(512)(128)(2,1)S(1)}, bf16[272]{0:T(512)(128)(2,1)S(1)}, u32[]{:S(2)}, u32[]{:S(2)}) collective-permute-start(bf16[272]{0:T(512)(128)(2,1)S(1)} %pad_maximum_fusion.6), channel_id=1, source_target_pairs={{0,16},{8,24},{16,0},{24,8},{1,17},{9,25},{17,1},{25,9},{2,18},{10... | collective-permute-start | bytes 1640 | tf_op jit(solution)/shard_map/ppermute | solution.py:34
  260.8 25.3 %all-to-all-start.4 = ((bf16[4,2,32,1536]{3,2,1,0:T(8,128)(2,1)}), bf16[4,2,32,1536]{3,2,1,0:T(8,128)(2,1)S(1)}, u32[]{:S(2)}, u32[]{:S(2)}) async-start(bf16[4,2,32,1536]{3,2,1,0:T(8,128)(2,1)} %add_convert_fusion.refs_7_), calls=%async_computation.4 | async-start | bytes 1572864 | tf_op jit(solution)/shard_map/all_to_all | solution.py:45
  287.7 23.1 %all-to-all-start.5 = ((bf16[4,2,36,1536]{3,1,2,0:T(2,128)(2,1)}), bf16[4,2,36,1536]{3,1,2,0:T(2,128)(2,1)S(1)}, u32[]{:S(2)}, u32[]{:S(2)}) async-start(bf16[4,2,36,1536]{3,1,2,0:T(2,128)(2,1)} %copy.93), calls=%async_computation.5 | async-start | bytes 1769472 | tf_op jit(solution)/shard_map/all_to_all | solution.py:45
  (53 other events, 320.4 us)

commit v4 on v3

--- a/solution.py
+++ b/solution.py
@@ -448,13 +448,16 @@
     )(decay_rate, key_rows, value_rows, grad_k, grad_v, state, *after)
 
 
-def carried(place, summary, decay_rate, block_size, direction, hold=None):
+def outside_states(place, summary, direction):
+    return [place.later_chip(summary, direction * p) for p in range(1, place.chips)]
+
+
+def carried(place, summary, decay_rate, block_size, direction, found=None):
     def block_decay(blocks):
         return jnp.exp(-decay_rate * (block_size * blocks)).reshape(1, -1, 1, 1)
 
-    found = [place.later_chip(summary, direction * p) for p in range(1, place.chips)]
-    if hold is not None:
-        hold.extend(found)
+    if found is None:
+        found = outside_states(place, summary, direction)
     mine = jnp.stack([summary, *found])
     partner = place.swap_core(mine)
     first = (place.core == 0) if direction > 0 else (place.core == 1)
@@ -641,16 +644,17 @@
         return keep, [behind(v, kernel_result) for v in arrived], scale
 
     summary = ordered(key_value_state, key_rows, value_rows, decay_rate)
-    early = []
-    state_before = carried(place, summary, decay_rate, block, 1, early)
+    early = outside_states(place, summary, 1)
     picked_hidden_a = dispatch(hidden_groups, first_a, count_a)
+    picked_grads_a = dispatch(grad_groups, first_a, count_a)
     picked_hidden_b = dispatch(hidden_groups, first_b, count_b)
-    picked_grads_a = dispatch(grad_groups, first_a, count_a, early)
     hidden_a = place.between_experts(behind(picked_hidden_a, picked_grads_a))
     picked_grads_b = dispatch(grad_groups, first_b, count_b, [pairs[0][1], pairs[1][1]])
     far_hidden_a = relay(hidden_a)
     pairs.append((own_mats[2], place.swap_core(behind(own_mats[2], picked_grads_b))))
-    inner_own_a = partial([([hidden_a], pairs[:2], in_scale)], count_a)
+    inner_own_a = partial([([hidden_a], pairs[:2], in_scale)], count_a, early)
+    early = [behind(v, inner_own_a[0]) for v in early]
+    state_before = carried(place, summary, decay_rate, block, 1, early)
     grad_queries, local_k, local_v, summary = ordered(
         local_grads,
         queries,
@@ -660,7 +664,7 @@
         norm_gain.reshape(1, -1),
         coeff.T,
         decay_rate,
-        behind(state_before, inner_own_a[0]),
+        state_before,
     )
     grads_a = place.between_experts(behind(picked_grads_a, hidden_a))
     far_grads_a = relay(behind(grads_a, summary))
@@ -689,16 +693,18 @@
     own_b, score_own_b = middle(held(inner_own_b, far_b[0]), held(outer_own_b, far_b[0]))
     from_far_a = to_slices(dx_far_a)
     total_a = dx_own_a.astype(f32) + sum(
-        behind(v, grad_keys).astype(f32) for v in from_far_a
+        behind(v, own_b[0], grad_keys).astype(f32) for v in from_far_a
     )
     total_a = total_a.astype(bf16)
     home_a = place.between_experts(total_a)
-    total_b = []
-    for h in range(2):
-        dx_own_b, dx_far_b = back([own_b, far_b], (h,), count_b, [total_a])
-        found = sum(v.astype(f32) for v in to_slices(dx_far_b))
-        total_b.append((dx_own_b.astype(f32) + found).astype(bf16))
-    total_b = behind(jnp.concatenate(total_b, axis=1), home_a)
+    from_far_b = [
+        to_slices(back([far_b], (h,), count_b, [total_a])[0]) for h in range(2)
+    ]
+    (dx_own_b,) = back([own_b], (0, 1), count_b)
+    total_b = dx_own_b.astype(f32) + sum(
+        jnp.concatenate(halves, axis=1).astype(f32) for halves in zip(*from_far_b)
+    )
+    total_b = behind(total_b.astype(bf16), home_a)
     home_b = place.between_experts(total_b)
 
     kinds = [score_own_a, score_far_a, score_own_b, score_far_b]

time: 324 us -> 316 us (0.975)
  waiting for transfers between devices: 89.2 us -> 68.9 us
  Pallas kernels: 129 us -> 146 us
    pallas_call x3 -> x4, Pallas kernels: 34.6 us -> 50.7 us  [project_back(): pl.pallas_call(body, grid=(halves * steps,), in_specs=[pl.BlockSpec(memor...]
    ppermute x17, waiting for transfers between devices: 48.5 us -> 36.8 us  [turn_chip(): lax.ppermute(v, 'seq', [(i, (i // 2 + p) % n * 2 + i % 2) for i in range(...]
    ppermute x8, waiting for transfers between devices: 11.3 us -> 2.9 us  [turn_slice(): lax.ppermute(v, 'expert', [(i, i // m * m + (i % m + k) % m) for i in ran...]
    unnamed x92 -> x72, local copies, waits for them, and re-layouts: 9.09 us -> 7.94 us
  transfers between devices with their start and end apart: 41 -> 41, of which waited for: 14 -> 14; matrix products, arithmetic and copies ran while one was open for 9% -> 8% of each run, Pallas kernels for 36% -> 45%
where the time goes in v4:
time: 316 us; the launch traced here: 315 us
  Pallas kernels  146 us (46%)
  waiting for transfers between devices  68.9 us (22%)
  starting transfers between devices  64.8 us (21%)
  other arithmetic  18.7 us (6%)
  local copies, waits for them, and re-layouts  12.2 us (4%)
    pallas_call x7, Pallas kernels, project(): pl.pallas_call(body, grid=(units // tile,), in_specs=[pl.BlockSpec(memory...  72.6 us
    pallas_call x4, Pallas kernels, project_back(): pl.pallas_call(body, grid=(halves * steps,), in_specs=[pl.BlockSpec(memor...  50.7 us
    ppermute x17, waiting for transfers between devices, turn_chip(): lax.ppermute(v, 'seq', [(i, (i // 2 + p) % n * 2 + i % 2) for i in range(...  36.8 us
    all_to_all x6, starting transfers between devices, between_experts(): lax.all_to_all(v, 'expert', 0, 0, axis_index_groups=groups, tiled=True)  29.1 us
    ppermute x17, starting transfers between devices, turn_chip(): lax.ppermute(v, 'seq', [(i, (i // 2 + p) % n * 2 + i % 2) for i in range(...  18.9 us
    all_to_all x6, waiting for transfers between devices, between_experts(): lax.all_to_all(v, 'expert', 0, 0, axis_index_groups=groups, tiled=True)  17.4 us
    unnamed x72, local copies, waits for them, and re-layouts  7.94 us
    ppermute x8, starting transfers between devices, turn_slice(): lax.ppermute(v, 'expert', [(i, i // m * m + (i % m + k) % m) for i in ran...  7.46 us
  transfers between devices with their start and end apart: 41, of which 14 were waited for; matrix products, arithmetic and copies ran while one was open for 8% of the time, Pallas kernels for 45%

profile of v4, /device:TPU:0, one launch (start us, length us, event | category | flops | bytes accessed | tf_op | source)
XLA Modules:
  0.0 314.7 jit_solution(12680507358963443281)
XLA Ops:
  3.7 3.0 collective-permute-start.1
  15.6 3.9 %collective-permute-done.2.refs_1_ = bf16[2,64,1536]{2,1,0:T(8,128)(2,1)S(1)} collective-permute-done((bf16[2,64,1536]{2,1,0:T(8,128)(2,1)S(1)}, bf16[2,64,1536]{2,1,0:T(8,128)(2,1)S(1)}, u32[]{:S(2)}, u32[]{:S(2)}) %collective-permute-start.2) | collective-permute-done | bytes 393248 | tf_op jit(solution)/shard_map/ppermute | solution.py:34
  20.9 5.8 %collective-permute-done.3.refs_1_ = bf16[2,64,1536]{2,1,0:T(8,128)(2,1)S(1)} collective-permute-done((bf16[2,64,1536]{2,1,0:T(8,128)(2,1)}, bf16[2,64,1536]{2,1,0:T(8,128)(2,1)S(1)}, u32[]{:S(2)}, u32[]{:S(2)}) %collective-permute-start.3) | collective-permute-done | bytes 393248 | tf_op jit(solution)/shard_map/ppermute | solution.py:34
  31.3 5.0 %all-to-all-start = ((bf16[4,2,32,1536]{3,2,1,0:T(8,128)(2,1)}), bf16[4,2,32,1536]{3,2,1,0:T(8,128)(2,1)S(1)}, u32[]{:S(2)}, u32[]{:S(2)}) async-start(bf16[4,2,32,1536]{3,2,1,0:T(8,128)(2,1)} %pick_rows.4.refs_2_), calls=%async_computation | async-start | bytes 1572864 | tf_op jit(solution)/shard_map/all_to_all | solution.py:45
  36.3 2.4 collective-permute-start
  39.5 17.4 %all-to-all-done.refs_0_ = bf16[4,2,32,1536]{3,2,1,0:T(8,128)(2,1)S(1)} async-done(((bf16[4,2,32,1536]{3,2,1,0:T(8,128)(2,1)}), bf16[4,2,32,1536]{3,2,1,0:T(8,128)(2,1)S(1)}, u32[]{:S(2)}, u32[]{:S(2)}) %all-to-all-start) | async-done | bytes 786464 | tf_op jit(solution)/shard_map/all_to_all | solution.py:45
  56.9 3.5 %all-to-all-start.1 = ((bf16[4,2,32,1536]{3,2,1,0:T(8,128)(2,1)}), bf16[4,2,32,1536]{3,2,1,0:T(8,128)(2,1)S(1)}, u32[]{:S(2)}, u32[]{:S(2)}) async-start(bf16[4,2,32,1536]{3,2,1,0:T(8,128)(2,1)} %pick_rows.5.refs_2_), calls=%async_computation.1 | async-start | bytes 1572864 | tf_op jit(solution)/shard_map/all_to_all | solution.py:45
  62.7 11.1 %project.7 = (f32[2,64,2304]{2,1,0:T(8,128)S(1)}, f32[1,2,64,2304]{3,2,1,0:T(8,128)S(1)}) custom-call(s32[1]{0:T(128)} %bitcast.4.chip_ref, bf16[4,2,32,1536]{3,2,1,0:T(8,128)(2,1)S(1)} %all-to-all-done.refs_0_, bf16[1536,2304]{1,0:T(8,128)(2,1)} %bitcast.174, bf16[1536,2304]{1,0:T(8,128)(2,1)} %collective-permute-done.4.refs_3_.refs_2_.refs_6_.refs_4_, ...), custom_call_target="tpu_custom_call" | custom-call | flops 1000 | bytes 1000 | tf_op jit(solution)/shard_map/project/pallas_call | solution.py:145
  76.0 6.9 %local_grads.1 = (bf16[2,256,256]{2,1,0:T(8,128)(2,1)}, f32[2,256,256]{2,1,0:T(8,128)S(1)}, f32[2,256,256]{2,1,0:T(8,128)S(1)}, f32[2,2,128,128]{3,2,1,0:T(8,128)S(1)}) custom-call(f32[2]{0:T(128)S(1)} %copy-done.20, bf16[2,256,256]{2,1,0:T(8,128)(2,1)S(1)} %copy-done.18, bf16[2,256,256]{2,1,0:T(8,128)(2,1)S(1)} %copy-done, ...), custom_call_target="tpu_custom_call" | custom-call | flops 1000 | bytes 1000 | tf_op jit(solution)/shard_map/local_grads/pallas_call | solution.py:394
  85.2 5.2 %all-to-all-start.2 = ((bf16[4,2,40,1536]{3,2,1,0:T(8,128)(2,1)}), bf16[4,2,40,1536]{3,2,1,0:T(8,128)(2,1)}, u32[]{:S(2)}, u32[]{:S(2)}) async-start(bf16[4,2,40,1536]{3,2,1,0:T(8,128)(2,1)} %pick_rows.6.refs_2_), calls=%async_computation.2 | async-start | bytes 1966080 | tf_op jit(solution)/shard_map/all_to_all | solution.py:45
  90.9 6.7 %project.8 = (f32[1,64,2304]{2,1,0:T(8,128)S(1)}, f32[1,1,64,2304]{3,2,1,0:T(8,128)S(1)}) custom-call(s32[1]{0:T(128)} %bitcast.4.chip_ref, bf16[4,2,32,1536]{3,2,1,0:T(8,128)(2,1)S(1)} %all-to-all-done.1.refs_0_, bf16[1536,2304]{1,0:T(8,128)(2,1)} %bitcast.23.refs_1_.refs_6_, bf16[1536,2304]{1,0:T(8,128)(2,1)} %collective-permute-done.8.refs_2_.refs_7_, ...), custom_call_target="tpu_custom_call" | custom-call | flops 1000 | bytes 1000 | tf_op jit(solution)/shard_map/project/pallas_call | solution.py:145
  100.0 6.2 %collective-permute-done.9 = f16[1,64,2304]{2,1,0:T(8,128)(2,1)S(1)} collective-permute-done((f16[1,64,2304]{2,1,0:T(8,128)(2,1)S(1)}, f16[1,64,2304]{2,1,0:T(8,128)(2,1)S(1)}, u32[]{:S(2)}, u32[]{:S(2)}) %collective-permute-start.9) | collective-permute-done | bytes 294944 | tf_op jit(solution)/shard_map/ppermute | solution.py:34
  109.6 16.4 %project.9 = (f32[3,64,2304]{2,1,0:T(8,128)S(1)}, f32[1,3,64,2304]{3,2,1,0:T(8,128)S(1)}) custom-call(s32[1]{0:T(128)} %bitcast.4.chip_ref, bf16[4,2,32,1536]{3,2,1,0:T(8,128)(2,1)} %collective-permute-done.7.refs_0_, bf16[4,2,32,1536]{3,2,1,0:T(8,128)(2,1)S(1)} %collective-permute-done.11.refs_1_, bf16[1536,2304]{1,0:T(8,128)(2,1)} %bitcast.175, ...), custom_call_target="tpu_custom_call" | custom-call | flops 1000 | bytes 1000 | tf_op jit(solution)/shard_map/project/pallas_call | solution.py:145
  127.3 4.9 %all-to-all-start.3 = ((bf16[4,2,40,1536]{3,2,1,0:T(8,128)(2,1)}), bf16[4,2,40,1536]{3,2,1,0:T(8,128)(2,1)}, u32[]{:S(2)}, u32[]{:S(2)}) async-start(bf16[4,2,40,1536]{3,2,1,0:T(8,128)(2,1)} %pick_rows.7.refs_5_), calls=%async_computation.3 | async-start | bytes 1966080 | tf_op jit(solution)/shard_map/all_to_all | solution.py:45
  135.3 2.7 collective-permute-start.17
  138.6 4.8 %collective-permute-done.12 = f32[2,2,128,128]{3,2,1,0:T(8,128)S(1)} collective-permute-done((f32[2,2,128,128]{3,2,1,0:T(8,128)S(1)}, f32[2,2,128,128]{3,2,1,0:T(8,128)S(1)}, u32[]{:S(2)}, u32[]{:S(2)}) %collective-permute-start.12) | collective-permute-done | bytes 262176 | tf_op jit(solution)/shard_map/ppermute | solution.py:40
  143.6 12.4 %project.10 = (f32[2,72,2304]{2,1,0:T(8,128)S(1)}, f32[1,2,72,2304]{3,2,1,0:T(8,128)S(1)}) custom-call(s32[1]{0:T(128)} %bitcast.4.chip_ref, bf16[4,2,40,1536]{3,2,1,0:T(8,128)(2,1)} %all-to-all-done.2.refs_0_, bf16[1536,2304]{1,0:T(8,128)(2,1)} %bitcast.176, bf16[1536,2304]{1,0:T(8,128)(2,1)} %collective-permute-done.4.refs_3_.refs_2_.refs_6_.refs_4_, ...), custom_call_target="tpu_custom_call" | custom-call | flops 1000 | bytes 1000 | tf_op jit(solution)/shard_map/project/pallas_call | solution.py:145
  161.6 11.7 %project.11 = (f32[2,72,2304]{2,1,0:T(8,128)S(1)}, f32[1,2,72,2304]{3,2,1,0:T(8,128)S(1)}) custom-call(s32[1]{0:T(128)} %bitcast.4.chip_ref, bf16[4,2,40,1536]{3,2,1,0:T(8,128)(2,1)S(1)} %collective-permute-done.19.refs_0_, bf16[1536,2304]{1,0:T(8,128)(2,1)} %bitcast.177, bf16[1536,2304]{1,0:T(8,128)(2,1)} %collective-permute-done.4.refs_3_.refs_2_.refs_6_.refs_4_, ...), custom_call_target="tpu_custom_call" | custom-call | flops 1000 | bytes 1000 | tf_op jit(solution)/shard_map/project/pallas_call | solution.py:145
  178.5 7.3 %project.12 = (f32[1,72,2304]{2,1,0:T(8,128)S(1)}, f32[1,1,72,2304]{3,2,1,0:T(8,128)S(1)}) custom-call(s32[1]{0:T(128)} %bitcast.4.chip_ref, bf16[4,2,40,1536]{3,2,1,0:T(8,128)(2,1)} %all-to-all-done.3.refs_0_, bf16[1536,2304]{1,0:T(8,128)(2,1)} %bitcast.23.refs_1_.refs_6_, bf16[1536,2304]{1,0:T(8,128)(2,1)} %collective-permute-done.8.refs_2_.refs_7_, ...), custom_call_target="tpu_custom_call" | custom-call | flops 1000 | bytes 1000 | tf_op jit(solution)/shard_map/project/pallas_call | solution.py:145
  187.6 16.3 %project_back.4 = (bf16[4,2,32,1536]{3,2,1,0:T(8,128)(2,1)S(1)}, bf16[4,2,32,1536]{3,2,1,0:T(8,128)(2,1)S(1)}) custom-call(s32[1]{0:T(128)} %bitcast.4.chip_ref, bf16[2,64,2304]{2,1,0:T(8,128)(2,1)} %multiply_convert_fusion.6.refs_0_, bf16[2,64,2304]{2,1,0:T(8,128)(2,1)} %collective-permute-done.15.refs_1_, ...), custom_call_target="tpu_custom_call" | custom-call | flops 1000 | bytes 1000 | tf_op jit(solution)/shard_map/project_back/pallas_call | solution.py:226
  204.6 7.0 %project.13 = (f32[1,72,2304]{2,1,0:T(8,128)S(1)}, f32[1,1,72,2304]{3,2,1,0:T(8,128)S(1)}) custom-call(s32[1]{0:T(128)} %bitcast.4.chip_ref, bf16[4,2,40,1536]{3,2,1,0:T(8,128)(2,1)S(1)} %collective-permute-done.14.refs_0_, bf16[1536,2304]{1,0:T(8,128)(2,1)} %bitcast.23.refs_1_.refs_6_, bf16[1536,2304]{1,0:T(8,128)(2,1)} %collective-permute-done.8.refs_2_.refs_7_, ...), custom_call_target="tpu_custom_call" | custom-call | flops 1000 | bytes 1000 | tf_op jit(solution)/shard_map/project/pallas_call | solution.py:145
  213.3 2.1 later_grads.1
  215.4 5.1 %collective-permute-done.22 = f16[1,72,2304]{2,1,0:T(8,128)(2,1)S(1)} collective-permute-done((f16[1,72,2304]{2,1,0:T(8,128)(2,1)S(1)}, f16[1,72,2304]{2,1,0:T(8,128)(2,1)S(1)}, u32[]{:S(2)}, u32[]{:S(2)}) %collective-permute-start.22) | collective-permute-done | bytes 331808 | tf_op jit(solution)/shard_map/ppermute | solution.py:34
  226.4 5.2 %all-to-all-start.4 = ((bf16[4,2,32,1536]{3,2,1,0:T(8,128)(2,1)}), bf16[4,2,32,1536]{3,2,1,0:T(8,128)(2,1)S(1)}, u32[]{:S(2)}, u32[]{:S(2)}) async-start(bf16[4,2,32,1536]{3,2,1,0:T(8,128)(2,1)} %add_convert_fusion.1.refs_5_), calls=%async_computation.4 | async-start | bytes 1572864 | tf_op jit(solution)/shard_map/all_to_all | solution.py:45
  231.6 7.6 %collective-permute-done.25.refs_1_ = bf16[2,72,2304]{2,1,0:T(8,128)(2,1)} collective-permute-done((bf16[2,72,2304]{2,1,0:T(8,128)(2,1)S(1)}, bf16[2,72,2304]{2,1,0:T(8,128)(2,1)}, u32[]{:S(2)}, u32[]{:S(2)}) %collective-permute-start.25) | collective-permute-done | bytes 663584 | tf_op jit(solution)/shard_map/ppermute | solution.py:34
  239.2 8.2 %project_back.5.refs_4_ = bf16[4,1,36,1536]{3,2,1,0:T(8,128)(2,1)S(1)} custom-call(s32[1]{0:T(128)} %bitcast.4.chip_ref, bf16[2,72,2304]{2,1,0:T(8,128)(2,1)S(1)} %multiply_convert_fusion.2.refs_0_, bf16[2,72,2304]{2,1,0:T(8,128)(2,1)} %collective-permute-done.25.refs_1_, bf16[1536,2304]{1,0:T(8,128)(2,1)} %bitcast.179, bf16[1536,2304]{1,0:T(8,128)(2,1)} %bitcast.187, ...), custom_call_target="tpu_custom_call" | custom-call | flops 1000 | bytes 1000 | tf_op jit(solution)/shard_map/project_back/pallas_call | solution.py:226
  248.9 8.2 %project_back.6.refs_6_ = bf16[4,1,36,1536]{3,2,1,0:T(8,128)(2,1)S(1)} custom-call(s32[1]{0:T(128)} %bitcast.4.chip_ref, bf16[2,72,2304]{2,1,0:T(8,128)(2,1)S(1)} %multiply_convert_fusion.2.refs_0_, bf16[2,72,2304]{2,1,0:T(8,128)(2,1)} %collective-permute-done.25.refs_1_, bf16[1536,2304]{1,0:T(8,128)(2,1)} %collective-permute-done.4.refs_3_.refs_2_.refs_6_.refs_4_, ...), custom_call_target="tpu_custom_call" | custom-call | flops 1000 | bytes 1000 | tf_op jit(solution)/shard_map/project_back/pallas_call | solution.py:226
  259.0 17.9 %project_back.7 = bf16[4,2,36,1536]{3,2,1,0:T(8,128)(2,1)S(1)} custom-call(s32[1]{0:T(128)} %bitcast.4.chip_ref, bf16[2,72,2304]{2,1,0:T(8,128)(2,1)S(1)} %multiply_convert_fusion.1.refs_0_, bf16[2,72,2304]{2,1,0:T(8,128)(2,1)} %collective-permute-done.24.refs_1_, bf16[1536,2304]{1,0:T(8,128)(2,1)} %bitcast.180, bf16[1536,2304]{1,0:T(8,128)(2,1)} %bitcast.188, ...), custom_call_target="tpu_custom_call" | custom-call | flops 1000 | bytes 1000 | tf_op jit(solution)/shard_map/project_back/pallas_call | solution.py:226
  280.6 5.2 %all-to-all-start.5 = ((bf16[4,2,36,1536]{3,1,2,0:T(2,128)(2,1)}), bf16[4,2,36,1536]{3,1,2,0:T(2,128)(2,1)S(1)}, u32[]{:S(2)}, u32[]{:S(2)}) async-start(bf16[4,2,36,1536]{3,1,2,0:T(2,128)(2,1)} %copy.93), calls=%async_computation.5 | async-start | bytes 1769472 | tf_op jit(solution)/shard_map/all_to_all | solution.py:45
  290.0 3.8 %collective-permute-start.32 = (f32[4,68]{1,0:T(4,128)S(1)}, f32[4,68]{1,0:T(4,128)S(1)}, u32[]{:S(2)}, u32[]{:S(2)}) collective-permute-start(f32[4,68]{1,0:T(4,128)S(1)} %convert_add_fusion), channel_id=1, source_target_pairs={{0,6},{1,7},{2,0},{3,1},{4,2},{5,3},{6,4},{7,5},{8,14},{9,15},{10,... | collective-permute-start | bytes 3272 | tf_op jit(solution)/shard_map/ppermute | solution.py:49
  295.7 6.6 %collective-permute-done.31 = f32[4,68]{1,0:T(4,128)S(1)} collective-permute-done((f32[4,68]{1,0:T(4,128)S(1)}, f32[4,68]{1,0:T(4,128)S(1)}, u32[]{:S(2)}, u32[]{:S(2)}) %collective-permute-start.31) | collective-permute-done | bytes 1120 | tf_op jit(solution)/shard_map/ppermute | solution.py:49
  309.1 4.6 %collective-permute-done.33 = bf16[64,1536]{1,0:T(8,128)(2,1)S(1)} collective-permute-done((bf16[64,1536]{1,0:T(8,128)(2,1)S(1)}, bf16[64,1536]{1,0:T(8,128)(2,1)S(1)}, u32[]{:S(2)}, u32[]{:S(2)}) %collective-permute-start.33) | collective-permute-done | bytes 196640 | tf_op jit(solution)/shard_map/ppermute | solution.py:34
  (226 shorter events, 76.6 us)
Async XLA Ops:
  0.7 29.1 %collective-permute-start.4 = (bf16[1536,2304]{1,0:T(8,128)(2,1)}, bf16[1536,2304]{1,0:T(8,128)(2,1)}, u32[]{:S(2)}, u32[]{:S(2)}) collective-permute-start(bf16[1536,2304]{1,0:T(8,128)(2,1)} %bitcast.173), channel_id=1, source_target_pairs={{0,8},{8,0},{16,24},{24,16},{1,9},{9,1},{17,25},{25,17},{2,10},{10... | collective-permute-start | bytes 21233672 | tf_op jit(solution)/shard_map/ppermute | solution.py:30
  1.2 28.6 %collective-permute-start.5 = (bf16[1536,2304]{1,0:T(8,128)(2,1)}, bf16[1536,2304]{1,0:T(8,128)(2,1)}, u32[]{:S(2)}, u32[]{:S(2)}) collective-permute-start(bf16[1536,2304]{1,0:T(8,128)(2,1)} %bitcast.181), channel_id=1, source_target_pairs={{0,8},{8,0},{16,24},{24,16},{1,9},{9,1},{17,25},{25,17},{2,10},{10... | collective-permute-start | bytes 21233672 | tf_op jit(solution)/shard_map/ppermute | solution.py:30
  3.7 11.3 %collective-permute-start.1 = (f32[64,8]{0,1:T(8,128)S(1)}, f32[64,8]{0,1:T(8,128)S(1)}, u32[]{:S(2)}, u32[]{:S(2)}) collective-permute-start(f32[64,8]{0,1:T(8,128)S(1)} %get-tuple-element.149), channel_id=1, source_target_pairs={{0,16},{8,24},{16,0},{24,8},{1,17},{9,25},{17,1},{25,9},{2,18},{10... | collective-permute-start | bytes 6152 | tf_op jit(solution)/shard_map/ppermute | solution.py:34
  7.4 12.1 %collective-permute-start.2 = (bf16[2,64,1536]{2,1,0:T(8,128)(2,1)S(1)}, bf16[2,64,1536]{2,1,0:T(8,128)(2,1)S(1)}, u32[]{:S(2)}, u32[]{:S(2)}) collective-permute-start(bf16[2,64,1536]{2,1,0:T(8,128)(2,1)S(1)} %bitcast.172), channel_id=1, source_target_pairs={{0,16},{8,24},{16,0},{24,8},{1,17},{9,25},{17,1},{25,9},{2,18},{10... | collective-permute-start | bytes 1179656 | tf_op jit(solution)/shard_map/ppermute | solution.py:34
  11.7 15.0 %collective-permute-start.3 = (bf16[2,64,1536]{2,1,0:T(8,128)(2,1)}, bf16[2,64,1536]{2,1,0:T(8,128)(2,1)S(1)}, u32[]{:S(2)}, u32[]{:S(2)}) collective-permute-start(bf16[2,64,1536]{2,1,0:T(8,128)(2,1)} %bitcast.17), channel_id=1, source_target_pairs={{0,16},{8,24},{16,0},{24,8},{1,17},{9,25},{17,1},{25,9},{2,18},{10... | collective-permute-start | bytes 1179656 | tf_op jit(solution)/shard_map/ppermute | solution.py:34
  31.3 59.6 %collective-permute-start.8 = (bf16[1536,2304]{1,0:T(8,128)(2,1)}, bf16[1536,2304]{1,0:T(8,128)(2,1)}, u32[]{:S(2)}, u32[]{:S(2)}) collective-permute-start(bf16[1536,2304]{1,0:T(8,128)(2,1)} %bitcast.23.refs_1_.refs_6_), channel_id=1, source_target_pairs={{0,8},{8,0},{16,24},{24,16},{1,9},{9,1},{17,25},{25,17},{2,10},{10... | collective-permute-start | bytes 21233672 | tf_op jit(solution)/shard_map/ppermute | solution.py:30
  31.3 25.7 %all-to-all-start = ((bf16[4,2,32,1536]{3,2,1,0:T(8,128)(2,1)}), bf16[4,2,32,1536]{3,2,1,0:T(8,128)(2,1)S(1)}, u32[]{:S(2)}, u32[]{:S(2)}) async-start(bf16[4,2,32,1536]{3,2,1,0:T(8,128)(2,1)} %pick_rows.4.refs_2_), calls=%async_computation | async-start | bytes 1572864 | tf_op jit(solution)/shard_map/all_to_all | solution.py:45
  36.3 24.1 %collective-permute-start = (f32[2,2,128,128]{3,2,1,0:T(8,128)S(1)}, f32[2,2,128,128]{3,2,1,0:T(8,128)S(1)}, u32[]{:S(2)}, u32[]{:S(2)}) collective-permute-start(f32[2,2,128,128]{3,2,1,0:T(8,128)S(1)} %key_value_state.1.refs_2_), channel_id=1, source_target_pairs={{0,16},{8,24},{1,17},{9,25},{2,18},{10,26},{3,19},{11,27},{4,20},{... | collective-permute-start | bytes 786440 | tf_op jit(solution)/shard_map/ppermute | solution.py:40
  56.9 28.2 %all-to-all-start.1 = ((bf16[4,2,32,1536]{3,2,1,0:T(8,128)(2,1)}), bf16[4,2,32,1536]{3,2,1,0:T(8,128)(2,1)S(1)}, u32[]{:S(2)}, u32[]{:S(2)}) async-start(bf16[4,2,32,1536]{3,2,1,0:T(8,128)(2,1)} %pick_rows.5.refs_2_), calls=%async_computation.1 | async-start | bytes 1572864 | tf_op jit(solution)/shard_map/all_to_all | solution.py:45
  61.2 48.5 %collective-permute-start.7 = (bf16[4,2,32,1536]{3,2,1,0:T(8,128)(2,1)S(1)}, bf16[4,2,32,1536]{3,2,1,0:T(8,128)(2,1)}, u32[]{:S(2)}, u32[]{:S(2)}) collective-permute-start(bf16[4,2,32,1536]{3,2,1,0:T(8,128)(2,1)S(1)} %all-to-all-done.refs_0_), channel_id=1, source_target_pairs={{0,1},{1,0},{2,3},{3,2},{4,5},{5,4},{6,7},{7,6},{8,9},{9,8},{10,11... | collective-permute-start | bytes 2359304 | tf_op jit(solution)/shard_map/ppermute | solution.py:55
  74.9 23.9 %collective-permute-start.10 = (f16[2,64,2304]{2,1,0:T(8,128)(2,1)}, f16[2,64,2304]{2,1,0:T(8,128)(2,1)}, u32[]{:S(2)}, u32[]{:S(2)}) collective-permute-start(f16[2,64,2304]{2,1,0:T(8,128)(2,1)} %fusion.8), channel_id=1, source_target_pairs={{0,16},{8,24},{16,0},{24,8},{1,17},{9,25},{17,1},{25,9},{2,18},{10... | collective-permute-start | bytes 1769480 | tf_op jit(solution)/shard_map/ppermute | solution.py:34
  85.2 42.2 %all-to-all-start.2 = ((bf16[4,2,40,1536]{3,2,1,0:T(8,128)(2,1)}), bf16[4,2,40,1536]{3,2,1,0:T(8,128)(2,1)}, u32[]{:S(2)}, u32[]{:S(2)}) async-start(bf16[4,2,40,1536]{3,2,1,0:T(8,128)(2,1)} %pick_rows.6.refs_2_), calls=%async_computation.2 | async-start | bytes 1966080 | tf_op jit(solution)/shard_map/all_to_all | solution.py:45
  90.3 19.3 %collective-permute-start.11 = (bf16[4,2,32,1536]{3,2,1,0:T(8,128)(2,1)S(1)}, bf16[4,2,32,1536]{3,2,1,0:T(8,128)(2,1)S(1)}, u32[]{:S(2)}, u32[]{:S(2)}) collective-permute-start(bf16[4,2,32,1536]{3,2,1,0:T(8,128)(2,1)S(1)} %all-to-all-done.1.refs_0_), channel_id=1, source_target_pairs={{0,1},{1,0},{2,3},{3,2},{4,5},{5,4},{6,7},{7,6},{8,9},{9,8},{10,11... | collective-permute-start | bytes 2359304 | tf_op jit(solution)/shard_map/ppermute | solution.py:55
  107.6 35.9 %collective-permute-start.15 = (bf16[2,64,2304]{2,1,0:T(8,128)(2,1)}, bf16[2,64,2304]{2,1,0:T(8,128)(2,1)}, u32[]{:S(2)}, u32[]{:S(2)}) collective-permute-start(bf16[2,64,2304]{2,1,0:T(8,128)(2,1)} %multiply_convert_fusion.6.refs_0_), channel_id=1, source_target_pairs={{0,16},{8,24},{16,0},{24,8},{1,17},{9,25},{17,1},{25,9},{2,18},{10... | collective-permute-start | bytes 1769480 | tf_op jit(solution)/shard_map/ppermute | solution.py:34
  127.3 47.1 %all-to-all-start.3 = ((bf16[4,2,40,1536]{3,2,1,0:T(8,128)(2,1)}), bf16[4,2,40,1536]{3,2,1,0:T(8,128)(2,1)}, u32[]{:S(2)}, u32[]{:S(2)}) async-start(bf16[4,2,40,1536]{3,2,1,0:T(8,128)(2,1)} %pick_rows.7.refs_5_), calls=%async_computation.3 | async-start | bytes 1966080 | tf_op jit(solution)/shard_map/all_to_all | solution.py:45
  132.3 11.1 %collective-permute-start.12 = (f32[2,2,128,128]{3,2,1,0:T(8,128)S(1)}, f32[2,2,128,128]{3,2,1,0:T(8,128)S(1)}, u32[]{:S(2)}, u32[]{:S(2)}) collective-permute-start(f32[2,2,128,128]{3,2,1,0:T(8,128)S(1)} %copy-done.7), channel_id=1, source_target_pairs={{16,0},{24,8},{17,1},{25,9},{18,2},{26,10},{19,3},{27,11},{20,4},{... | collective-permute-start | bytes 786440 | tf_op jit(solution)/shard_map/ppermute | solution.py:40
  135.3 24.6 %collective-permute-start.17 = (f16[3,64,2304]{2,1,0:T(8,128)(2,1)S(1)}, f16[3,64,2304]{2,1,0:T(8,128)(2,1)S(1)}, u32[]{:S(2)}, u32[]{:S(2)}) collective-permute-start(f16[3,64,2304]{2,1,0:T(8,128)(2,1)S(1)} %fusion.1), channel_id=1, source_target_pairs={{0,16},{8,24},{16,0},{24,8},{1,17},{9,25},{17,1},{25,9},{2,18},{10... | collective-permute-start | bytes 2654216 | tf_op jit(solution)/shard_map/ppermute | solution.py:34
  138.0 23.6 %collective-permute-start.19 = (bf16[4,2,40,1536]{3,2,1,0:T(8,128)(2,1)}, bf16[4,2,40,1536]{3,2,1,0:T(8,128)(2,1)S(1)}, u32[]{:S(2)}, u32[]{:S(2)}) collective-permute-start(bf16[4,2,40,1536]{3,2,1,0:T(8,128)(2,1)} %all-to-all-done.2.refs_0_), channel_id=1, source_target_pairs={{0,1},{1,0},{2,3},{3,2},{4,5},{5,4},{6,7},{7,6},{8,9},{9,8},{10,11... | collective-permute-start | bytes 2949128 | tf_op jit(solution)/shard_map/ppermute | solution.py:55
  143.5 13.5 %collective-permute-start.13 = (f32[2,2,2,128,128]{4,3,2,1,0:T(8,128)S(1)}, f32[2,2,2,128,128]{4,3,2,1,0:T(8,128)S(1)}, u32[]{:S(2)}, u32[]{:S(2)}) collective-permute-start(f32[2,2,2,128,128]{4,3,2,1,0:T(8,128)S(1)} %pad_maximum_fusion.1), channel_id=1, source_target_pairs={{0,8},{8,0},{16,24},{24,16},{1,9},{9,1},{17,25},{25,17},{2,10},{10... | collective-permute-start | bytes 1572872 | tf_op jit(solution)/shard_map/ppermute | solution.py:30
  156.9 47.6 %collective-permute-start.16 = (f16[2,72,2304]{2,1,0:T(8,128)(2,1)}, f16[2,72,2304]{2,1,0:T(8,128)(2,1)}, u32[]{:S(2)}, u32[]{:S(2)}) collective-permute-start(f16[2,72,2304]{2,1,0:T(8,128)(2,1)} %fusion.2), channel_id=1, source_target_pairs={{0,16},{8,24},{16,0},{24,8},{1,17},{9,25},{17,1},{25,9},{2,18},{10... | collective-permute-start | bytes 1990664 | tf_op jit(solution)/shard_map/ppermute | solution.py:34
  161.6 26.0 %collective-permute-start.18 = (bf16[2,64,2304]{2,1,0:T(8,128)(2,1)}, bf16[2,64,2304]{2,1,0:T(8,128)(2,1)}, u32[]{:S(2)}, u32[]{:S(2)}) collective-permute-start(bf16[2,64,2304]{2,1,0:T(8,128)(2,1)} %multiply_convert_fusion.5.refs_2_), channel_id=1, source_target_pairs={{0,16},{8,24},{16,0},{24,8},{1,17},{9,25},{17,1},{25,9},{2,18},{10... | collective-permute-start | bytes 1769480 | tf_op jit(solution)/shard_map/ppermute | solution.py:34
  174.4 30.1 %collective-permute-start.14 = (bf16[4,2,40,1536]{3,2,1,0:T(8,128)(2,1)}, bf16[4,2,40,1536]{3,2,1,0:T(8,128)(2,1)S(1)}, u32[]{:S(2)}, u32[]{:S(2)}) collective-permute-start(bf16[4,2,40,1536]{3,2,1,0:T(8,128)(2,1)} %all-to-all-done.3.refs_0_), channel_id=1, source_target_pairs={{0,1},{1,0},{2,3},{3,2},{4,5},{5,4},{6,7},{7,6},{8,9},{9,8},{10,11... | collective-permute-start | bytes 2949128 | tf_op jit(solution)/shard_map/ppermute | solution.py:55
  176.4 36.6 %collective-permute-start.23 = (f16[2,72,2304]{2,1,0:T(8,128)(2,1)S(1)}, f16[2,72,2304]{2,1,0:T(8,128)(2,1)S(1)}, u32[]{:S(2)}, u32[]{:S(2)}) collective-permute-start(f16[2,72,2304]{2,1,0:T(8,128)(2,1)S(1)} %fusion.3), channel_id=1, source_target_pairs={{0,16},{8,24},{16,0},{24,8},{1,17},{9,25},{17,1},{25,9},{2,18},{10... | collective-permute-start | bytes 1990664 | tf_op jit(solution)/shard_map/ppermute | solution.py:34
  185.9 37.1 %collective-permute-start.21 = (f16[1,72,2304]{2,1,0:T(8,128)(2,1)S(1)}, f16[1,72,2304]{2,1,0:T(8,128)(2,1)S(1)}, u32[]{:S(2)}, u32[]{:S(2)}) collective-permute-start(f16[1,72,2304]{2,1,0:T(8,128)(2,1)S(1)} %fusion.12), channel_id=1, source_target_pairs={{0,16},{8,24},{16,0},{24,8},{1,17},{9,25},{17,1},{25,9},{2,18},{10... | collective-permute-start | bytes 995336 | tf_op jit(solution)/shard_map/ppermute | solution.py:34
  203.9 21.4 %collective-permute-start.20 = (bf16[4,2,32,1536]{3,2,1,0:T(8,128)(2,1)S(1)}, bf16[4,2,32,1536]{3,2,1,0:T(8,128)(2,1)S(1)}, u32[]{:S(2)}, u32[]{:S(2)}) collective-permute-start(bf16[4,2,32,1536]{3,2,1,0:T(8,128)(2,1)S(1)} %get-tuple-element.92), channel_id=1, source_target_pairs={{0,1},{1,0},{2,3},{3,2},{4,5},{5,4},{6,7},{7,6},{8,9},{9,8},{10,11... | collective-permute-start | bytes 2359304 | tf_op jit(solution)/shard_map/ppermute | solution.py:55
  221.2 18.0 %collective-permute-start.25 = (bf16[2,72,2304]{2,1,0:T(8,128)(2,1)S(1)}, bf16[2,72,2304]{2,1,0:T(8,128)(2,1)}, u32[]{:S(2)}, u32[]{:S(2)}) collective-permute-start(bf16[2,72,2304]{2,1,0:T(8,128)(2,1)S(1)} %multiply_convert_fusion.2.refs_0_), channel_id=1, source_target_pairs={{0,16},{8,24},{16,0},{24,8},{1,17},{9,25},{17,1},{25,9},{2,18},{10... | collective-permute-start | bytes 1990664 | tf_op jit(solution)/shard_map/ppermute | solution.py:34
  223.7 35.3 %collective-permute-start.24 = (bf16[2,72,2304]{2,1,0:T(8,128)(2,1)S(1)}, bf16[2,72,2304]{2,1,0:T(8,128)(2,1)}, u32[]{:S(2)}, u32[]{:S(2)}) collective-permute-start(bf16[2,72,2304]{2,1,0:T(8,128)(2,1)S(1)} %multiply_convert_fusion.1.refs_0_), channel_id=1, source_target_pairs={{0,16},{8,24},{16,0},{24,8},{1,17},{9,25},{17,1},{25,9},{2,18},{10... | collective-permute-start | bytes 1990664 | tf_op jit(solution)/shard_map/ppermute | solution.py:34
  226.4 52.6 %all-to-all-start.4 = ((bf16[4,2,32,1536]{3,2,1,0:T(8,128)(2,1)}), bf16[4,2,32,1536]{3,2,1,0:T(8,128)(2,1)S(1)}, u32[]{:S(2)}, u32[]{:S(2)}) async-start(bf16[4,2,32,1536]{3,2,1,0:T(8,128)(2,1)} %add_convert_fusion.1.refs_5_), calls=%async_computation.4 | async-start | bytes 1572864 | tf_op jit(solution)/shard_map/all_to_all | solution.py:45
  247.5 30.1 %collective-permute-start.26 = (bf16[4,1,36,1536]{3,2,1,0:T(8,128)(2,1)S(1)}, bf16[4,1,36,1536]{3,2,1,0:T(8,128)(2,1)}, u32[]{:S(2)}, u32[]{:S(2)}) collective-permute-start(bf16[4,1,36,1536]{3,2,1,0:T(8,128)(2,1)S(1)} %project_back.5.refs_4_), channel_id=1, source_target_pairs={{0,1},{1,0},{2,3},{3,2},{4,5},{5,4},{6,7},{7,6},{8,9},{9,8},{10,11... | collective-permute-start | bytes 1327112 | tf_op jit(solution)/shard_map/ppermute | solution.py:55
  257.2 20.4 %collective-permute-start.27 = (bf16[4,1,36,1536]{3,2,1,0:T(8,128)(2,1)S(1)}, bf16[4,1,36,1536]{3,2,1,0:T(8,128)(2,1)}, u32[]{:S(2)}, u32[]{:S(2)}) collective-permute-start(bf16[4,1,36,1536]{3,2,1,0:T(8,128)(2,1)S(1)} %project_back.6.refs_6_), channel_id=1, source_target_pairs={{0,1},{1,0},{2,3},{3,2},{4,5},{5,4},{6,7},{7,6},{8,9},{9,8},{10,11... | collective-permute-start | bytes 1327112 | tf_op jit(solution)/shard_map/ppermute | solution.py:55
  258.5 18.5 %collective-permute-start.28 = (bf16[272]{0:T(512)(128)(2,1)S(1)}, bf16[272]{0:T(512)(128)(2,1)S(1)}, u32[]{:S(2)}, u32[]{:S(2)}) collective-permute-start(bf16[272]{0:T(512)(128)(2,1)S(1)} %pad_maximum_fusion.5), channel_id=1, source_target_pairs={{0,16},{8,24},{16,0},{24,8},{1,17},{9,25},{17,1},{25,9},{2,18},{10... | collective-permute-start | bytes 1640 | tf_op jit(solution)/shard_map/ppermute | solution.py:34
  280.6 22.3 %all-to-all-start.5 = ((bf16[4,2,36,1536]{3,1,2,0:T(2,128)(2,1)}), bf16[4,2,36,1536]{3,1,2,0:T(2,128)(2,1)S(1)}, u32[]{:S(2)}, u32[]{:S(2)}) async-start(bf16[4,2,36,1536]{3,1,2,0:T(2,128)(2,1)} %copy.93), calls=%async_computation.5 | async-start | bytes 1769472 | tf_op jit(solution)/shard_map/all_to_all | solution.py:45
  (43 other events, 216.9 us)

commit v5 on v4

--- a/solution.py
+++ b/solution.py
@@ -676,8 +676,8 @@
         count_a,
         own_a[:1],
     )
-    far_hidden_b = relay(behind(hidden_b, whole_far_a[0]))
-    grads_b = place.between_experts(behind(picked_grads_b, hidden_b, whole_far_a[0]))
+    far_hidden_b = relay(behind(hidden_b, own_a[0]))
+    grads_b = place.between_experts(behind(picked_grads_b, hidden_b, own_a[0]))
     inner_own_b = partial([([hidden_b], pairs[:2], in_scale)], count_b, own_a[1:])
     far_grads_b = relay(grads_b)
     far_a, score_far_a = middle(whole_far_a)

time: 316 us -> 312 us (0.987)
  waiting for transfers between devices: 68.9 us -> 61.7 us
  starting transfers between devices: 64.8 us -> 68.2 us
    ppermute x2, waiting for transfers between devices: 4.8 us -> 0.01 us  [later_chip(): return lax.ppermute(v, 'seq', pairs)]
    unnamed x72 -> x70, local copies, waits for them, and re-layouts: 7.94 us -> 7.25 us
  transfers between devices with their start and end apart: 41 -> 41, of which waited for: 14 -> 15; matrix products, arithmetic and copies ran while one was open for 8% -> 8% of each run, Pallas kernels for 45% -> 46%
where the time goes in v5:
time: 312 us; the launch traced here: 311 us
  Pallas kernels  146 us (47%)
  starting transfers between devices  68.2 us (22%)
  waiting for transfers between devices  61.7 us (20%)
  other arithmetic  19.7 us (6%)
  local copies, waits for them, and re-layouts  11.5 us (4%)
    pallas_call x7, Pallas kernels, project(): pl.pallas_call(body, grid=(units // tile,), in_specs=[pl.BlockSpec(memory...  72.6 us
    pallas_call x4, Pallas kernels, project_back(): pl.pallas_call(body, grid=(halves * steps,), in_specs=[pl.BlockSpec(memor...  50.7 us
    ppermute x17, waiting for transfers between devices, turn_chip(): lax.ppermute(v, 'seq', [(i, (i // 2 + p) % n * 2 + i % 2) for i in range(...  36.2 us
    all_to_all x6, starting transfers between devices, between_experts(): lax.all_to_all(v, 'expert', 0, 0, axis_index_groups=groups, tiled=True)  28.8 us
    ppermute x17, starting transfers between devices, turn_chip(): lax.ppermute(v, 'seq', [(i, (i // 2 + p) % n * 2 + i % 2) for i in range(...  20.4 us
    all_to_all x6, waiting for transfers between devices, between_experts(): lax.all_to_all(v, 'expert', 0, 0, axis_index_groups=groups, tiled=True)  17.4 us
    ppermute x8, starting transfers between devices, turn_slice(): lax.ppermute(v, 'expert', [(i, i // m * m + (i % m + k) % m) for i in ran...  9.47 us
    unnamed x70, local copies, waits for them, and re-layouts  7.25 us
  transfers between devices with their start and end apart: 41, of which 15 were waited for; matrix products, arithmetic and copies ran while one was open for 8% of the time, Pallas kernels for 46%

profile of v5, /device:TPU:0, one launch (start us, length us, event | category | flops | bytes accessed | tf_op | source)
XLA Modules:
  0.0 311.3 jit_solution(16494330164021447873)
XLA Ops:
  3.7 3.0 collective-permute-start.1
  15.6 3.9 %collective-permute-done.2.refs_1_ = bf16[2,64,1536]{2,1,0:T(8,128)(2,1)S(1)} collective-permute-done((bf16[2,64,1536]{2,1,0:T(8,128)(2,1)S(1)}, bf16[2,64,1536]{2,1,0:T(8,128)(2,1)S(1)}, u32[]{:S(2)}, u32[]{:S(2)}) %collective-permute-start.2) | collective-permute-done | bytes 393248 | tf_op jit(solution)/shard_map/ppermute | solution.py:34
  20.9 5.8 %collective-permute-done.3.refs_1_ = bf16[2,64,1536]{2,1,0:T(8,128)(2,1)S(1)} collective-permute-done((bf16[2,64,1536]{2,1,0:T(8,128)(2,1)}, bf16[2,64,1536]{2,1,0:T(8,128)(2,1)S(1)}, u32[]{:S(2)}, u32[]{:S(2)}) %collective-permute-start.3) | collective-permute-done | bytes 393248 | tf_op jit(solution)/shard_map/ppermute | solution.py:34
  31.3 5.0 %all-to-all-start = ((bf16[4,2,32,1536]{3,2,1,0:T(8,128)(2,1)}), bf16[4,2,32,1536]{3,2,1,0:T(8,128)(2,1)S(1)}, u32[]{:S(2)}, u32[]{:S(2)}) async-start(bf16[4,2,32,1536]{3,2,1,0:T(8,128)(2,1)} %pick_rows.4.refs_2_), calls=%async_computation | async-start | bytes 1572864 | tf_op jit(solution)/shard_map/all_to_all | solution.py:45
  36.3 2.4 collective-permute-start
  39.5 17.4 %all-to-all-done.refs_0_ = bf16[4,2,32,1536]{3,2,1,0:T(8,128)(2,1)S(1)} async-done(((bf16[4,2,32,1536]{3,2,1,0:T(8,128)(2,1)}), bf16[4,2,32,1536]{3,2,1,0:T(8,128)(2,1)S(1)}, u32[]{:S(2)}, u32[]{:S(2)}) %all-to-all-start) | async-done | bytes 786464 | tf_op jit(solution)/shard_map/all_to_all | solution.py:45
  56.9 3.5 %all-to-all-start.1 = ((bf16[4,2,32,1536]{3,2,1,0:T(8,128)(2,1)}), bf16[4,2,32,1536]{3,2,1,0:T(8,128)(2,1)S(1)}, u32[]{:S(2)}, u32[]{:S(2)}) async-start(bf16[4,2,32,1536]{3,2,1,0:T(8,128)(2,1)} %pick_rows.5.refs_2_), calls=%async_computation.1 | async-start | bytes 1572864 | tf_op jit(solution)/shard_map/all_to_all | solution.py:45
  62.7 11.1 %project.7 = (f32[2,64,2304]{2,1,0:T(8,128)S(1)}, f32[1,2,64,2304]{3,2,1,0:T(8,128)S(1)}) custom-call(s32[1]{0:T(128)} %bitcast.4.chip_ref, bf16[4,2,32,1536]{3,2,1,0:T(8,128)(2,1)S(1)} %all-to-all-done.refs_0_, bf16[1536,2304]{1,0:T(8,128)(2,1)} %bitcast.172, bf16[1536,2304]{1,0:T(8,128)(2,1)} %collective-permute-done.4.refs_3_.refs_2_.refs_6_.refs_4_, ...), custom_call_target="tpu_custom_call" | custom-call | flops 1000 | bytes 1000 | tf_op jit(solution)/shard_map/project/pallas_call | solution.py:145
  76.0 7.2 %local_grads.1 = (bf16[2,256,256]{2,1,0:T(8,128)(2,1)}, f32[2,256,256]{2,1,0:T(8,128)S(1)}, f32[2,256,256]{2,1,0:T(8,128)S(1)}, f32[2,2,128,128]{3,2,1,0:T(8,128)}) custom-call(f32[2]{0:T(128)S(1)} %copy-done.17, bf16[2,256,256]{2,1,0:T(8,128)(2,1)S(1)} %copy-done.15, bf16[2,256,256]{2,1,0:T(8,128)(2,1)S(1)} %copy-done, bf16[2,256,256]{2,1,0:T(8,128)(2,1)S(1)} %copy-done.2, ...), custom_call_target="tpu_custom_call" | custom-call | flops 1000 | bytes 1000 | tf_op jit(solution)/shard_map/local_grads/pallas_call | solution.py:394
  85.3 5.0 %all-to-all-start.2 = ((bf16[4,2,40,1536]{3,2,1,0:T(8,128)(2,1)}), bf16[4,2,40,1536]{3,2,1,0:T(8,128)(2,1)}, u32[]{:S(2)}, u32[]{:S(2)}) async-start(bf16[4,2,40,1536]{3,2,1,0:T(8,128)(2,1)} %pick_rows.6.refs_2_), calls=%async_computation.2 | async-start | bytes 1966080 | tf_op jit(solution)/shard_map/all_to_all | solution.py:45
  90.3 6.7 %project.8 = (f32[1,64,2304]{2,1,0:T(8,128)S(1)}, f32[1,1,64,2304]{3,2,1,0:T(8,128)S(1)}) custom-call(s32[1]{0:T(128)} %bitcast.4.chip_ref, bf16[4,2,32,1536]{3,2,1,0:T(8,128)(2,1)S(1)} %all-to-all-done.1.refs_0_, bf16[1536,2304]{1,0:T(8,128)(2,1)} %bitcast.23.refs_1_.refs_6_, bf16[1536,2304]{1,0:T(8,128)(2,1)} %collective-permute-done.8.refs_2_.refs_7_, ...), custom_call_target="tpu_custom_call" | custom-call | flops 1000 | bytes 1000 | tf_op jit(solution)/shard_map/project/pallas_call | solution.py:145
  99.4 6.2 %collective-permute-done.9 = f16[1,64,2304]{2,1,0:T(8,128)(2,1)S(1)} collective-permute-done((f16[1,64,2304]{2,1,0:T(8,128)(2,1)S(1)}, f16[1,64,2304]{2,1,0:T(8,128)(2,1)S(1)}, u32[]{:S(2)}, u32[]{:S(2)}) %collective-permute-start.9) | collective-permute-done | bytes 294944 | tf_op jit(solution)/shard_map/ppermute | solution.py:34
  108.2 16.6 %project.9 = (f32[3,64,2304]{2,1,0:T(8,128)S(1)}, f32[1,3,64,2304]{3,2,1,0:T(8,128)S(1)}) custom-call(s32[1]{0:T(128)} %bitcast.4.chip_ref, bf16[4,2,32,1536]{3,2,1,0:T(8,128)(2,1)} %collective-permute-done.7.refs_0_, bf16[4,2,32,1536]{3,2,1,0:T(8,128)(2,1)} %collective-permute-done.11.refs_1_, bf16[1536,2304]{1,0:T(8,128)(2,1)} %bitcast.173, ...), custom_call_target="tpu_custom_call" | custom-call | flops 1000 | bytes 1000 | tf_op jit(solution)/shard_map/project/pallas_call | solution.py:145
  127.6 4.8 %all-to-all-start.3 = ((bf16[4,2,40,1536]{3,2,1,0:T(8,128)(2,1)}), bf16[4,2,40,1536]{3,2,1,0:T(8,128)(2,1)}, u32[]{:S(2)}, u32[]{:S(2)}) async-start(bf16[4,2,40,1536]{3,2,1,0:T(8,128)(2,1)} %pick_rows.7.refs_5_), calls=%async_computation.3 | async-start | bytes 1966080 | tf_op jit(solution)/shard_map/all_to_all | solution.py:45
  134.1 2.7 collective-permute-start.17
  139.5 12.3 %project.10 = (f32[2,72,2304]{2,1,0:T(8,128)S(1)}, f32[1,2,72,2304]{3,2,1,0:T(8,128)S(1)}) custom-call(s32[1]{0:T(128)} %bitcast.4.chip_ref, bf16[4,2,40,1536]{3,2,1,0:T(8,128)(2,1)} %all-to-all-done.2.refs_0_, bf16[1536,2304]{1,0:T(8,128)(2,1)} %bitcast.174, bf16[1536,2304]{1,0:T(8,128)(2,1)} %collective-permute-done.4.refs_3_.refs_2_.refs_6_.refs_4_, ...), custom_call_target="tpu_custom_call" | custom-call | flops 1000 | bytes 1000 | tf_op jit(solution)/shard_map/project/pallas_call | solution.py:145
  158.1 11.6 %project.11 = (f32[2,72,2304]{2,1,0:T(8,128)S(1)}, f32[1,2,72,2304]{3,2,1,0:T(8,128)S(1)}) custom-call(s32[1]{0:T(128)} %bitcast.4.chip_ref, bf16[4,2,40,1536]{3,2,1,0:T(8,128)(2,1)S(1)} %collective-permute-done.19.refs_0_, bf16[1536,2304]{1,0:T(8,128)(2,1)} %bitcast.175, bf16[1536,2304]{1,0:T(8,128)(2,1)} %collective-permute-done.4.refs_3_.refs_2_.refs_6_.refs_4_, ...), custom_call_target="tpu_custom_call" | custom-call | flops 1000 | bytes 1000 | tf_op jit(solution)/shard_map/project/pallas_call | solution.py:145
  174.0 7.3 %project.12 = (f32[1,72,2304]{2,1,0:T(8,128)S(1)}, f32[1,1,72,2304]{3,2,1,0:T(8,128)S(1)}) custom-call(s32[1]{0:T(128)} %bitcast.4.chip_ref, bf16[4,2,40,1536]{3,2,1,0:T(8,128)(2,1)} %all-to-all-done.3.refs_0_, bf16[1536,2304]{1,0:T(8,128)(2,1)} %bitcast.23.refs_1_.refs_6_, bf16[1536,2304]{1,0:T(8,128)(2,1)} %collective-permute-done.8.refs_2_.refs_7_, ...), custom_call_target="tpu_custom_call" | custom-call | flops 1000 | bytes 1000 | tf_op jit(solution)/shard_map/project/pallas_call | solution.py:145
  181.3 2.2 collective-permute-done.18.refs_3_
  183.5 16.3 %project_back.4 = (bf16[4,2,32,1536]{3,2,1,0:T(8,128)(2,1)S(1)}, bf16[4,2,32,1536]{3,2,1,0:T(8,128)(2,1)S(1)}) custom-call(s32[1]{0:T(128)} %bitcast.4.chip_ref, bf16[2,64,2304]{2,1,0:T(8,128)(2,1)} %multiply_convert_fusion.6.refs_0_, bf16[2,64,2304]{2,1,0:T(8,128)(2,1)} %collective-permute-done.15.refs_1_, ...), custom_call_target="tpu_custom_call" | custom-call | flops 1000 | bytes 1000 | tf_op jit(solution)/shard_map/project_back/pallas_call | solution.py:226
  201.4 7.0 %project.13 = (f32[1,72,2304]{2,1,0:T(8,128)S(1)}, f32[1,1,72,2304]{3,2,1,0:T(8,128)S(1)}) custom-call(s32[1]{0:T(128)} %bitcast.4.chip_ref, bf16[4,2,40,1536]{3,2,1,0:T(8,128)(2,1)S(1)} %collective-permute-done.14.refs_0_, bf16[1536,2304]{1,0:T(8,128)(2,1)} %bitcast.23.refs_1_.refs_6_, bf16[1536,2304]{1,0:T(8,128)(2,1)} %collective-permute-done.8.refs_2_.refs_7_, ...), custom_call_target="tpu_custom_call" | custom-call | flops 1000 | bytes 1000 | tf_op jit(solution)/shard_map/project/pallas_call | solution.py:145
  209.9 2.1 later_grads.1
  212.1 4.8 %collective-permute-done.22 = f16[1,72,2304]{2,1,0:T(8,128)(2,1)S(1)} collective-permute-done((f16[1,72,2304]{2,1,0:T(8,128)(2,1)S(1)}, f16[1,72,2304]{2,1,0:T(8,128)(2,1)S(1)}, u32[]{:S(2)}, u32[]{:S(2)}) %collective-permute-start.22) | collective-permute-done | bytes 331808 | tf_op jit(solution)/shard_map/ppermute | solution.py:34
  222.7 5.2 %all-to-all-start.4 = ((bf16[4,2,32,1536]{3,2,1,0:T(8,128)(2,1)}), bf16[4,2,32,1536]{3,2,1,0:T(8,128)(2,1)S(1)}, u32[]{:S(2)}, u32[]{:S(2)}) async-start(bf16[4,2,32,1536]{3,2,1,0:T(8,128)(2,1)} %add_convert_fusion.1.refs_5_), calls=%async_computation.4 | async-start | bytes 1572864 | tf_op jit(solution)/shard_map/all_to_all | solution.py:45
  228.0 7.6 %collective-permute-done.25.refs_1_ = bf16[2,72,2304]{2,1,0:T(8,128)(2,1)} collective-permute-done((bf16[2,72,2304]{2,1,0:T(8,128)(2,1)S(1)}, bf16[2,72,2304]{2,1,0:T(8,128)(2,1)}, u32[]{:S(2)}, u32[]{:S(2)}) %collective-permute-start.25) | collective-permute-done | bytes 663584 | tf_op jit(solution)/shard_map/ppermute | solution.py:34
  235.5 8.2 %project_back.5.refs_4_ = bf16[4,1,36,1536]{3,2,1,0:T(8,128)(2,1)S(1)} custom-call(s32[1]{0:T(128)} %bitcast.4.chip_ref, bf16[2,72,2304]{2,1,0:T(8,128)(2,1)S(1)} %multiply_convert_fusion.2.refs_0_, bf16[2,72,2304]{2,1,0:T(8,128)(2,1)} %collective-permute-done.25.refs_1_, bf16[1536,2304]{1,0:T(8,128)(2,1)} %bitcast.177, bf16[1536,2304]{1,0:T(8,128)(2,1)} %bitcast.185, ...), custom_call_target="tpu_custom_call" | custom-call | flops 1000 | bytes 1000 | tf_op jit(solution)/shard_map/project_back/pallas_call | solution.py:226
  245.0 8.2 %project_back.6.refs_6_ = bf16[4,1,36,1536]{3,2,1,0:T(8,128)(2,1)S(1)} custom-call(s32[1]{0:T(128)} %bitcast.4.chip_ref, bf16[2,72,2304]{2,1,0:T(8,128)(2,1)S(1)} %multiply_convert_fusion.2.refs_0_, bf16[2,72,2304]{2,1,0:T(8,128)(2,1)} %collective-permute-done.25.refs_1_, bf16[1536,2304]{1,0:T(8,128)(2,1)} %collective-permute-done.4.refs_3_.refs_2_.refs_6_.refs_4_, ...), custom_call_target="tpu_custom_call" | custom-call | flops 1000 | bytes 1000 | tf_op jit(solution)/shard_map/project_back/pallas_call | solution.py:226
  256.1 17.9 %project_back.7 = bf16[4,2,36,1536]{3,2,1,0:T(8,128)(2,1)S(1)} custom-call(s32[1]{0:T(128)} %bitcast.4.chip_ref, bf16[2,72,2304]{2,1,0:T(8,128)(2,1)S(1)} %multiply_convert_fusion.1.refs_0_, bf16[2,72,2304]{2,1,0:T(8,128)(2,1)} %collective-permute-done.24.refs_1_, bf16[1536,2304]{1,0:T(8,128)(2,1)} %bitcast.178, bf16[1536,2304]{1,0:T(8,128)(2,1)} %bitcast.186, ...), custom_call_target="tpu_custom_call" | custom-call | flops 1000 | bytes 1000 | tf_op jit(solution)/shard_map/project_back/pallas_call | solution.py:226
  277.7 5.2 %all-to-all-start.5 = ((bf16[4,2,36,1536]{3,1,2,0:T(2,128)(2,1)}), bf16[4,2,36,1536]{3,1,2,0:T(2,128)(2,1)S(1)}, u32[]{:S(2)}, u32[]{:S(2)}) async-start(bf16[4,2,36,1536]{3,1,2,0:T(2,128)(2,1)} %copy.93), calls=%async_computation.5 | async-start | bytes 1769472 | tf_op jit(solution)/shard_map/all_to_all | solution.py:45
  287.1 3.8 %collective-permute-start.32 = (f32[4,68]{1,0:T(4,128)S(1)}, f32[4,68]{1,0:T(4,128)S(1)}, u32[]{:S(2)}, u32[]{:S(2)}) collective-permute-start(f32[4,68]{1,0:T(4,128)S(1)} %convert_add_fusion), channel_id=1, source_target_pairs={{0,6},{1,7},{2,0},{3,1},{4,2},{5,3},{6,4},{7,5},{8,14},{9,15},{10,... | collective-permute-start | bytes 3272 | tf_op jit(solution)/shard_map/ppermute | solution.py:49
  292.9 5.4 %collective-permute-done.31 = f32[4,68]{1,0:T(4,128)S(1)} collective-permute-done((f32[4,68]{1,0:T(4,128)S(1)}, f32[4,68]{1,0:T(4,128)S(1)}, u32[]{:S(2)}, u32[]{:S(2)}) %collective-permute-start.31) | collective-permute-done | bytes 1120 | tf_op jit(solution)/shard_map/ppermute | solution.py:49
  306.7 3.7 %collective-permute-done.34 = bf16[64,1536]{1,0:T(8,128)(2,1)S(1)} collective-permute-done((bf16[64,1536]{1,0:T(8,128)(2,1)S(1)}, bf16[64,1536]{1,0:T(8,128)(2,1)S(1)}, u32[]{:S(2)}, u32[]{:S(2)}) %collective-permute-start.34) | collective-permute-done | bytes 196640 | tf_op jit(solution)/shard_map/ppermute | solution.py:34
  (224 shorter events, 78.3 us)
Async XLA Ops:
  0.7 29.1 %collective-permute-start.4 = (bf16[1536,2304]{1,0:T(8,128)(2,1)}, bf16[1536,2304]{1,0:T(8,128)(2,1)}, u32[]{:S(2)}, u32[]{:S(2)}) collective-permute-start(bf16[1536,2304]{1,0:T(8,128)(2,1)} %bitcast.171), channel_id=1, source_target_pairs={{0,8},{8,0},{16,24},{24,16},{1,9},{9,1},{17,25},{25,17},{2,10},{10... | collective-permute-start | bytes 21233672 | tf_op jit(solution)/shard_map/ppermute | solution.py:30
  1.2 28.6 %collective-permute-start.5 = (bf16[1536,2304]{1,0:T(8,128)(2,1)}, bf16[1536,2304]{1,0:T(8,128)(2,1)}, u32[]{:S(2)}, u32[]{:S(2)}) collective-permute-start(bf16[1536,2304]{1,0:T(8,128)(2,1)} %bitcast.179), channel_id=1, source_target_pairs={{0,8},{8,0},{16,24},{24,16},{1,9},{9,1},{17,25},{25,17},{2,10},{10... | collective-permute-start | bytes 21233672 | tf_op jit(solution)/shard_map/ppermute | solution.py:30
  3.7 11.3 %collective-permute-start.1 = (f32[64,8]{0,1:T(8,128)S(1)}, f32[64,8]{0,1:T(8,128)S(1)}, u32[]{:S(2)}, u32[]{:S(2)}) collective-permute-start(f32[64,8]{0,1:T(8,128)S(1)} %get-tuple-element.149), channel_id=1, source_target_pairs={{0,16},{8,24},{16,0},{24,8},{1,17},{9,25},{17,1},{25,9},{2,18},{10... | collective-permute-start | bytes 6152 | tf_op jit(solution)/shard_map/ppermute | solution.py:34
  7.4 12.1 %collective-permute-start.2 = (bf16[2,64,1536]{2,1,0:T(8,128)(2,1)S(1)}, bf16[2,64,1536]{2,1,0:T(8,128)(2,1)S(1)}, u32[]{:S(2)}, u32[]{:S(2)}) collective-permute-start(bf16[2,64,1536]{2,1,0:T(8,128)(2,1)S(1)} %bitcast.170), channel_id=1, source_target_pairs={{0,16},{8,24},{16,0},{24,8},{1,17},{9,25},{17,1},{25,9},{2,18},{10... | collective-permute-start | bytes 1179656 | tf_op jit(solution)/shard_map/ppermute | solution.py:34
  11.6 15.1 %collective-permute-start.3 = (bf16[2,64,1536]{2,1,0:T(8,128)(2,1)}, bf16[2,64,1536]{2,1,0:T(8,128)(2,1)S(1)}, u32[]{:S(2)}, u32[]{:S(2)}) collective-permute-start(bf16[2,64,1536]{2,1,0:T(8,128)(2,1)} %bitcast.17), channel_id=1, source_target_pairs={{0,16},{8,24},{16,0},{24,8},{1,17},{9,25},{17,1},{25,9},{2,18},{10... | collective-permute-start | bytes 1179656 | tf_op jit(solution)/shard_map/ppermute | solution.py:34
  31.3 59.0 %collective-permute-start.8 = (bf16[1536,2304]{1,0:T(8,128)(2,1)}, bf16[1536,2304]{1,0:T(8,128)(2,1)}, u32[]{:S(2)}, u32[]{:S(2)}) collective-permute-start(bf16[1536,2304]{1,0:T(8,128)(2,1)} %bitcast.23.refs_1_.refs_6_), channel_id=1, source_target_pairs={{0,8},{8,0},{16,24},{24,16},{1,9},{9,1},{17,25},{25,17},{2,10},{10... | collective-permute-start | bytes 21233672 | tf_op jit(solution)/shard_map/ppermute | solution.py:30
  31.3 25.7 %all-to-all-start = ((bf16[4,2,32,1536]{3,2,1,0:T(8,128)(2,1)}), bf16[4,2,32,1536]{3,2,1,0:T(8,128)(2,1)S(1)}, u32[]{:S(2)}, u32[]{:S(2)}) async-start(bf16[4,2,32,1536]{3,2,1,0:T(8,128)(2,1)} %pick_rows.4.refs_2_), calls=%async_computation | async-start | bytes 1572864 | tf_op jit(solution)/shard_map/all_to_all | solution.py:45
  36.3 24.1 %collective-permute-start = (f32[2,2,128,128]{3,2,1,0:T(8,128)S(1)}, f32[2,2,128,128]{3,2,1,0:T(8,128)S(1)}, u32[]{:S(2)}, u32[]{:S(2)}) collective-permute-start(f32[2,2,128,128]{3,2,1,0:T(8,128)S(1)} %key_value_state.1.refs_2_), channel_id=1, source_target_pairs={{0,16},{8,24},{1,17},{9,25},{2,18},{10,26},{3,19},{11,27},{4,20},{... | collective-permute-start | bytes 786440 | tf_op jit(solution)/shard_map/ppermute | solution.py:40
  56.9 27.8 %all-to-all-start.1 = ((bf16[4,2,32,1536]{3,2,1,0:T(8,128)(2,1)}), bf16[4,2,32,1536]{3,2,1,0:T(8,128)(2,1)S(1)}, u32[]{:S(2)}, u32[]{:S(2)}) async-start(bf16[4,2,32,1536]{3,2,1,0:T(8,128)(2,1)} %pick_rows.5.refs_2_), calls=%async_computation.1 | async-start | bytes 1572864 | tf_op jit(solution)/shard_map/all_to_all | solution.py:45
  61.2 47.1 %collective-permute-start.7 = (bf16[4,2,32,1536]{3,2,1,0:T(8,128)(2,1)S(1)}, bf16[4,2,32,1536]{3,2,1,0:T(8,128)(2,1)}, u32[]{:S(2)}, u32[]{:S(2)}) collective-permute-start(bf16[4,2,32,1536]{3,2,1,0:T(8,128)(2,1)S(1)} %all-to-all-done.refs_0_), channel_id=1, source_target_pairs={{0,1},{1,0},{2,3},{3,2},{4,5},{5,4},{6,7},{7,6},{8,9},{9,8},{10,11... | collective-permute-start | bytes 2359304 | tf_op jit(solution)/shard_map/ppermute | solution.py:55
  74.9 23.4 %collective-permute-start.10 = (f16[2,64,2304]{2,1,0:T(8,128)(2,1)}, f16[2,64,2304]{2,1,0:T(8,128)(2,1)}, u32[]{:S(2)}, u32[]{:S(2)}) collective-permute-start(f16[2,64,2304]{2,1,0:T(8,128)(2,1)} %fusion.8), channel_id=1, source_target_pairs={{0,16},{8,24},{16,0},{24,8},{1,17},{9,25},{17,1},{25,9},{2,18},{10... | collective-permute-start | bytes 1769480 | tf_op jit(solution)/shard_map/ppermute | solution.py:34
  84.8 23.5 %collective-permute-start.11 = (bf16[4,2,32,1536]{3,2,1,0:T(8,128)(2,1)S(1)}, bf16[4,2,32,1536]{3,2,1,0:T(8,128)(2,1)}, u32[]{:S(2)}, u32[]{:S(2)}) collective-permute-start(bf16[4,2,32,1536]{3,2,1,0:T(8,128)(2,1)S(1)} %all-to-all-done.1.refs_0_), channel_id=1, source_target_pairs={{0,1},{1,0},{2,3},{3,2},{4,5},{5,4},{6,7},{7,6},{8,9},{9,8},{10,11... | collective-permute-start | bytes 2359304 | tf_op jit(solution)/shard_map/ppermute | solution.py:55
  85.3 42.3 %all-to-all-start.2 = ((bf16[4,2,40,1536]{3,2,1,0:T(8,128)(2,1)}), bf16[4,2,40,1536]{3,2,1,0:T(8,128)(2,1)}, u32[]{:S(2)}, u32[]{:S(2)}) async-start(bf16[4,2,40,1536]{3,2,1,0:T(8,128)(2,1)} %pick_rows.6.refs_2_), calls=%async_computation.2 | async-start | bytes 1966080 | tf_op jit(solution)/shard_map/all_to_all | solution.py:45
  107.1 32.4 %collective-permute-start.15 = (bf16[2,64,2304]{2,1,0:T(8,128)(2,1)}, bf16[2,64,2304]{2,1,0:T(8,128)(2,1)}, u32[]{:S(2)}, u32[]{:S(2)}) collective-permute-start(bf16[2,64,2304]{2,1,0:T(8,128)(2,1)} %multiply_convert_fusion.6.refs_0_), channel_id=1, source_target_pairs={{0,16},{8,24},{16,0},{24,8},{1,17},{9,25},{17,1},{25,9},{2,18},{10... | collective-permute-start | bytes 1769480 | tf_op jit(solution)/shard_map/ppermute | solution.py:34
  126.1 12.2 %collective-permute-start.12 = (f32[2,2,128,128]{3,2,1,0:T(8,128)}, f32[2,2,128,128]{3,2,1,0:T(8,128)S(1)}, u32[]{:S(2)}, u32[]{:S(2)}) collective-permute-start(f32[2,2,128,128]{3,2,1,0:T(8,128)} %get-tuple-element.76), channel_id=1, source_target_pairs={{16,0},{24,8},{17,1},{25,9},{18,2},{26,10},{19,3},{27,11},{20,4},{... | collective-permute-start | bytes 786440 | tf_op jit(solution)/shard_map/ppermute | solution.py:40
  127.6 43.2 %all-to-all-start.3 = ((bf16[4,2,40,1536]{3,2,1,0:T(8,128)(2,1)}), bf16[4,2,40,1536]{3,2,1,0:T(8,128)(2,1)}, u32[]{:S(2)}, u32[]{:S(2)}) async-start(bf16[4,2,40,1536]{3,2,1,0:T(8,128)(2,1)} %pick_rows.7.refs_5_), calls=%async_computation.3 | async-start | bytes 1966080 | tf_op jit(solution)/shard_map/all_to_all | solution.py:45
  134.1 20.2 %collective-permute-start.17 = (f16[3,64,2304]{2,1,0:T(8,128)(2,1)S(1)}, f16[3,64,2304]{2,1,0:T(8,128)(2,1)S(1)}, u32[]{:S(2)}, u32[]{:S(2)}) collective-permute-start(f16[3,64,2304]{2,1,0:T(8,128)(2,1)S(1)} %fusion.1), channel_id=1, source_target_pairs={{0,16},{8,24},{16,0},{24,8},{1,17},{9,25},{17,1},{25,9},{2,18},{10... | collective-permute-start | bytes 2654216 | tf_op jit(solution)/shard_map/ppermute | solution.py:34
  136.8 21.3 %collective-permute-start.19 = (bf16[4,2,40,1536]{3,2,1,0:T(8,128)(2,1)}, bf16[4,2,40,1536]{3,2,1,0:T(8,128)(2,1)S(1)}, u32[]{:S(2)}, u32[]{:S(2)}) collective-permute-start(bf16[4,2,40,1536]{3,2,1,0:T(8,128)(2,1)} %all-to-all-done.2.refs_0_), channel_id=1, source_target_pairs={{0,1},{1,0},{2,3},{3,2},{4,5},{5,4},{6,7},{7,6},{8,9},{9,8},{10,11... | collective-permute-start | bytes 2949128 | tf_op jit(solution)/shard_map/ppermute | solution.py:55
  139.4 13.5 %collective-permute-start.13 = (f32[2,2,2,128,128]{4,3,2,1,0:T(8,128)S(1)}, f32[2,2,2,128,128]{4,3,2,1,0:T(8,128)S(1)}, u32[]{:S(2)}, u32[]{:S(2)}) collective-permute-start(f32[2,2,2,128,128]{4,3,2,1,0:T(8,128)S(1)} %pad_maximum_fusion.1), channel_id=1, source_target_pairs={{0,8},{8,0},{16,24},{24,16},{1,9},{9,1},{17,25},{25,17},{2,10},{10... | collective-permute-start | bytes 1572872 | tf_op jit(solution)/shard_map/ppermute | solution.py:30
  152.8 48.6 %collective-permute-start.16 = (f16[2,72,2304]{2,1,0:T(8,128)(2,1)}, f16[2,72,2304]{2,1,0:T(8,128)(2,1)}, u32[]{:S(2)}, u32[]{:S(2)}) collective-permute-start(f16[2,72,2304]{2,1,0:T(8,128)(2,1)} %fusion.2), channel_id=1, source_target_pairs={{0,16},{8,24},{16,0},{24,8},{1,17},{9,25},{17,1},{25,9},{2,18},{10... | collective-permute-start | bytes 1990664 | tf_op jit(solution)/shard_map/ppermute | solution.py:34
  156.1 27.4 %collective-permute-start.18 = (bf16[2,64,2304]{2,1,0:T(8,128)(2,1)}, bf16[2,64,2304]{2,1,0:T(8,128)(2,1)}, u32[]{:S(2)}, u32[]{:S(2)}) collective-permute-start(bf16[2,64,2304]{2,1,0:T(8,128)(2,1)} %multiply_convert_fusion.5.refs_2_), channel_id=1, source_target_pairs={{0,16},{8,24},{16,0},{24,8},{1,17},{9,25},{17,1},{25,9},{2,18},{10... | collective-permute-start | bytes 1769480 | tf_op jit(solution)/shard_map/ppermute | solution.py:34
  170.7 30.7 %collective-permute-start.14 = (bf16[4,2,40,1536]{3,2,1,0:T(8,128)(2,1)}, bf16[4,2,40,1536]{3,2,1,0:T(8,128)(2,1)S(1)}, u32[]{:S(2)}, u32[]{:S(2)}) collective-permute-start(bf16[4,2,40,1536]{3,2,1,0:T(8,128)(2,1)} %all-to-all-done.3.refs_0_), channel_id=1, source_target_pairs={{0,1},{1,0},{2,3},{3,2},{4,5},{5,4},{6,7},{7,6},{8,9},{9,8},{10,11... | collective-permute-start | bytes 2949128 | tf_op jit(solution)/shard_map/ppermute | solution.py:55
  173.8 35.9 %collective-permute-start.23 = (f16[2,72,2304]{2,1,0:T(8,128)(2,1)S(1)}, f16[2,72,2304]{2,1,0:T(8,128)(2,1)S(1)}, u32[]{:S(2)}, u32[]{:S(2)}) collective-permute-start(f16[2,72,2304]{2,1,0:T(8,128)(2,1)S(1)} %fusion.3), channel_id=1, source_target_pairs={{0,16},{8,24},{16,0},{24,8},{1,17},{9,25},{17,1},{25,9},{2,18},{10... | collective-permute-start | bytes 1990664 | tf_op jit(solution)/shard_map/ppermute | solution.py:34
  199.8 21.9 %collective-permute-start.20 = (bf16[4,2,32,1536]{3,2,1,0:T(8,128)(2,1)S(1)}, bf16[4,2,32,1536]{3,2,1,0:T(8,128)(2,1)S(1)}, u32[]{:S(2)}, u32[]{:S(2)}) collective-permute-start(bf16[4,2,32,1536]{3,2,1,0:T(8,128)(2,1)S(1)} %get-tuple-element.92), channel_id=1, source_target_pairs={{0,1},{1,0},{2,3},{3,2},{4,5},{5,4},{6,7},{7,6},{8,9},{9,8},{10,11... | collective-permute-start | bytes 2359304 | tf_op jit(solution)/shard_map/ppermute | solution.py:55
  200.4 19.7 %collective-permute-start.21 = (f16[1,72,2304]{2,1,0:T(8,128)(2,1)S(1)}, f16[1,72,2304]{2,1,0:T(8,128)(2,1)S(1)}, u32[]{:S(2)}, u32[]{:S(2)}) collective-permute-start(f16[1,72,2304]{2,1,0:T(8,128)(2,1)S(1)} %fusion.12), channel_id=1, source_target_pairs={{0,16},{8,24},{16,0},{24,8},{1,17},{9,25},{17,1},{25,9},{2,18},{10... | collective-permute-start | bytes 995336 | tf_op jit(solution)/shard_map/ppermute | solution.py:34
  217.5 18.0 %collective-permute-start.25 = (bf16[2,72,2304]{2,1,0:T(8,128)(2,1)S(1)}, bf16[2,72,2304]{2,1,0:T(8,128)(2,1)}, u32[]{:S(2)}, u32[]{:S(2)}) collective-permute-start(bf16[2,72,2304]{2,1,0:T(8,128)(2,1)S(1)} %multiply_convert_fusion.2.refs_0_), channel_id=1, source_target_pairs={{0,16},{8,24},{16,0},{24,8},{1,17},{9,25},{17,1},{25,9},{2,18},{10... | collective-permute-start | bytes 1990664 | tf_op jit(solution)/shard_map/ppermute | solution.py:34
  220.8 35.3 %collective-permute-start.24 = (bf16[2,72,2304]{2,1,0:T(8,128)(2,1)S(1)}, bf16[2,72,2304]{2,1,0:T(8,128)(2,1)}, u32[]{:S(2)}, u32[]{:S(2)}) collective-permute-start(bf16[2,72,2304]{2,1,0:T(8,128)(2,1)S(1)} %multiply_convert_fusion.1.refs_0_), channel_id=1, source_target_pairs={{0,16},{8,24},{16,0},{24,8},{1,17},{9,25},{17,1},{25,9},{2,18},{10... | collective-permute-start | bytes 1990664 | tf_op jit(solution)/shard_map/ppermute | solution.py:34
  222.7 53.4 %all-to-all-start.4 = ((bf16[4,2,32,1536]{3,2,1,0:T(8,128)(2,1)}), bf16[4,2,32,1536]{3,2,1,0:T(8,128)(2,1)S(1)}, u32[]{:S(2)}, u32[]{:S(2)}) async-start(bf16[4,2,32,1536]{3,2,1,0:T(8,128)(2,1)} %add_convert_fusion.1.refs_5_), calls=%async_computation.4 | async-start | bytes 1572864 | tf_op jit(solution)/shard_map/all_to_all | solution.py:45
  243.8 30.8 %collective-permute-start.26 = (bf16[4,1,36,1536]{3,2,1,0:T(8,128)(2,1)S(1)}, bf16[4,1,36,1536]{3,2,1,0:T(8,128)(2,1)}, u32[]{:S(2)}, u32[]{:S(2)}) collective-permute-start(bf16[4,1,36,1536]{3,2,1,0:T(8,128)(2,1)S(1)} %project_back.5.refs_4_), channel_id=1, source_target_pairs={{0,1},{1,0},{2,3},{3,2},{4,5},{5,4},{6,7},{7,6},{8,9},{9,8},{10,11... | collective-permute-start | bytes 1327112 | tf_op jit(solution)/shard_map/ppermute | solution.py:55
  253.2 21.4 %collective-permute-start.27 = (bf16[4,1,36,1536]{3,2,1,0:T(8,128)(2,1)S(1)}, bf16[4,1,36,1536]{3,2,1,0:T(8,128)(2,1)}, u32[]{:S(2)}, u32[]{:S(2)}) collective-permute-start(bf16[4,1,36,1536]{3,2,1,0:T(8,128)(2,1)S(1)} %project_back.6.refs_6_), channel_id=1, source_target_pairs={{0,1},{1,0},{2,3},{3,2},{4,5},{5,4},{6,7},{7,6},{8,9},{9,8},{10,11... | collective-permute-start | bytes 1327112 | tf_op jit(solution)/shard_map/ppermute | solution.py:55
  254.8 19.2 %collective-permute-start.28 = (bf16[272]{0:T(512)(128)(2,1)S(1)}, bf16[272]{0:T(512)(128)(2,1)S(1)}, u32[]{:S(2)}, u32[]{:S(2)}) collective-permute-start(bf16[272]{0:T(512)(128)(2,1)S(1)} %pad_maximum_fusion.5), channel_id=1, source_target_pairs={{0,16},{8,24},{16,0},{24,8},{1,17},{9,25},{17,1},{25,9},{2,18},{10... | collective-permute-start | bytes 1640 | tf_op jit(solution)/shard_map/ppermute | solution.py:34
  277.7 21.2 %all-to-all-start.5 = ((bf16[4,2,36,1536]{3,1,2,0:T(2,128)(2,1)}), bf16[4,2,36,1536]{3,1,2,0:T(2,128)(2,1)S(1)}, u32[]{:S(2)}, u32[]{:S(2)}) async-start(bf16[4,2,36,1536]{3,1,2,0:T(2,128)(2,1)} %copy.93), calls=%async_computation.5 | async-start | bytes 1769472 | tf_op jit(solution)/shard_map/all_to_all | solution.py:45
  (42 other events, 201.0 us)

commit v6 on v5

--- a/solution.py
+++ b/solution.py
@@ -169,7 +169,7 @@
     units = groups[0][0].shape[2]
     width = mats[0][0].shape[0]
     halves = len(mats)
-    tile = tile_of(width)
+    tile = 512 if width % 512 == 0 else tile_of(width)
     steps = width // tile
     parts = [v for group in groups for v in group]
     sizes = [group[0].shape[1] for group in groups]

time: 312 us -> 312 us (level)
  no operation moved by 1% of the time
where the time goes in v6:
time: 312 us; the launch traced here: 311 us
  Pallas kernels  145 us (46%)
  starting transfers between devices  68.2 us (22%)
  waiting for transfers between devices  61.7 us (20%)
  other arithmetic  19.7 us (6%)
  local copies, waits for them, and re-layouts  11.5 us (4%)
    pallas_call x7, Pallas kernels, project(): pl.pallas_call(body, grid=(units // tile,), in_specs=[pl.BlockSpec(memory...  72.6 us
    pallas_call x4, Pallas kernels, project_back(): pl.pallas_call(body, grid=(halves * steps,), in_specs=[pl.BlockSpec(memor...  50.3 us
    ppermute x17, waiting for transfers between devices, turn_chip(): lax.ppermute(v, 'seq', [(i, (i // 2 + p) % n * 2 + i % 2) for i in range(...  36.2 us
    all_to_all x6, starting transfers between devices, between_experts(): lax.all_to_all(v, 'expert', 0, 0, axis_index_groups=groups, tiled=True)  28.8 us
    ppermute x17, starting transfers between devices, turn_chip(): lax.ppermute(v, 'seq', [(i, (i // 2 + p) % n * 2 + i % 2) for i in range(...  20.4 us
    all_to_all x6, waiting for transfers between devices, between_experts(): lax.all_to_all(v, 'expert', 0, 0, axis_index_groups=groups, tiled=True)  17.4 us
    ppermute x8, starting transfers between devices, turn_slice(): lax.ppermute(v, 'expert', [(i, i // m * m + (i % m + k) % m) for i in ran...  9.47 us
    unnamed x70, local copies, waits for them, and re-layouts  7.25 us
  transfers between devices with their start and end apart: 41, of which 15 were waited for; matrix products, arithmetic and copies ran while one was open for 8% of the time, Pallas kernels for 46%

profile of v6, /device:TPU:0, one launch (start us, length us, event | category | flops | bytes accessed | tf_op | source)
XLA Modules:
  0.0 310.9 jit_solution(3095854715981055552)
XLA Ops:
  3.7 3.0 collective-permute-start.1
  15.6 3.9 %collective-permute-done.2.refs_1_ = bf16[2,64,1536]{2,1,0:T(8,128)(2,1)S(1)} collective-permute-done((bf16[2,64,1536]{2,1,0:T(8,128)(2,1)S(1)}, bf16[2,64,1536]{2,1,0:T(8,128)(2,1)S(1)}, u32[]{:S(2)}, u32[]{:S(2)}) %collective-permute-start.2) | collective-permute-done | bytes 393248 | tf_op jit(solution)/shard_map/ppermute | solution.py:34
  20.9 5.8 %collective-permute-done.3.refs_1_ = bf16[2,64,1536]{2,1,0:T(8,128)(2,1)S(1)} collective-permute-done((bf16[2,64,1536]{2,1,0:T(8,128)(2,1)}, bf16[2,64,1536]{2,1,0:T(8,128)(2,1)S(1)}, u32[]{:S(2)}, u32[]{:S(2)}) %collective-permute-start.3) | collective-permute-done | bytes 393248 | tf_op jit(solution)/shard_map/ppermute | solution.py:34
  31.3 5.0 %all-to-all-start = ((bf16[4,2,32,1536]{3,2,1,0:T(8,128)(2,1)}), bf16[4,2,32,1536]{3,2,1,0:T(8,128)(2,1)S(1)}, u32[]{:S(2)}, u32[]{:S(2)}) async-start(bf16[4,2,32,1536]{3,2,1,0:T(8,128)(2,1)} %pick_rows.4.refs_2_), calls=%async_computation | async-start | bytes 1572864 | tf_op jit(solution)/shard_map/all_to_all | solution.py:45
  36.3 2.4 collective-permute-start
  39.5 17.4 %all-to-all-done.refs_0_ = bf16[4,2,32,1536]{3,2,1,0:T(8,128)(2,1)S(1)} async-done(((bf16[4,2,32,1536]{3,2,1,0:T(8,128)(2,1)}), bf16[4,2,32,1536]{3,2,1,0:T(8,128)(2,1)S(1)}, u32[]{:S(2)}, u32[]{:S(2)}) %all-to-all-start) | async-done | bytes 786464 | tf_op jit(solution)/shard_map/all_to_all | solution.py:45
  56.9 3.5 %all-to-all-start.1 = ((bf16[4,2,32,1536]{3,2,1,0:T(8,128)(2,1)}), bf16[4,2,32,1536]{3,2,1,0:T(8,128)(2,1)S(1)}, u32[]{:S(2)}, u32[]{:S(2)}) async-start(bf16[4,2,32,1536]{3,2,1,0:T(8,128)(2,1)} %pick_rows.5.refs_2_), calls=%async_computation.1 | async-start | bytes 1572864 | tf_op jit(solution)/shard_map/all_to_all | solution.py:45
  62.7 11.1 %project.7 = (f32[2,64,2304]{2,1,0:T(8,128)S(1)}, f32[1,2,64,2304]{3,2,1,0:T(8,128)S(1)}) custom-call(s32[1]{0:T(128)} %bitcast.4.chip_ref, bf16[4,2,32,1536]{3,2,1,0:T(8,128)(2,1)S(1)} %all-to-all-done.refs_0_, bf16[1536,2304]{1,0:T(8,128)(2,1)} %bitcast.172, bf16[1536,2304]{1,0:T(8,128)(2,1)} %collective-permute-done.4.refs_3_.refs_2_.refs_6_.refs_4_, ...), custom_call_target="tpu_custom_call" | custom-call | flops 1000 | bytes 1000 | tf_op jit(solution)/shard_map/project/pallas_call | solution.py:145
  76.0 7.2 %local_grads.1 = (bf16[2,256,256]{2,1,0:T(8,128)(2,1)}, f32[2,256,256]{2,1,0:T(8,128)S(1)}, f32[2,256,256]{2,1,0:T(8,128)S(1)}, f32[2,2,128,128]{3,2,1,0:T(8,128)}) custom-call(f32[2]{0:T(128)S(1)} %copy-done.17, bf16[2,256,256]{2,1,0:T(8,128)(2,1)S(1)} %copy-done.15, bf16[2,256,256]{2,1,0:T(8,128)(2,1)S(1)} %copy-done, bf16[2,256,256]{2,1,0:T(8,128)(2,1)S(1)} %copy-done.2, ...), custom_call_target="tpu_custom_call" | custom-call | flops 1000 | bytes 1000 | tf_op jit(solution)/shard_map/local_grads/pallas_call | solution.py:394
  85.3 5.0 %all-to-all-start.2 = ((bf16[4,2,40,1536]{3,2,1,0:T(8,128)(2,1)}), bf16[4,2,40,1536]{3,2,1,0:T(8,128)(2,1)}, u32[]{:S(2)}, u32[]{:S(2)}) async-start(bf16[4,2,40,1536]{3,2,1,0:T(8,128)(2,1)} %pick_rows.6.refs_2_), calls=%async_computation.2 | async-start | bytes 1966080 | tf_op jit(solution)/shard_map/all_to_all | solution.py:45
  90.3 6.7 %project.8 = (f32[1,64,2304]{2,1,0:T(8,128)S(1)}, f32[1,1,64,2304]{3,2,1,0:T(8,128)S(1)}) custom-call(s32[1]{0:T(128)} %bitcast.4.chip_ref, bf16[4,2,32,1536]{3,2,1,0:T(8,128)(2,1)S(1)} %all-to-all-done.1.refs_0_, bf16[1536,2304]{1,0:T(8,128)(2,1)} %bitcast.23.refs_1_.refs_6_, bf16[1536,2304]{1,0:T(8,128)(2,1)} %collective-permute-done.8.refs_2_.refs_7_, ...), custom_call_target="tpu_custom_call" | custom-call | flops 1000 | bytes 1000 | tf_op jit(solution)/shard_map/project/pallas_call | solution.py:145
  99.4 6.2 %collective-permute-done.9 = f16[1,64,2304]{2,1,0:T(8,128)(2,1)S(1)} collective-permute-done((f16[1,64,2304]{2,1,0:T(8,128)(2,1)S(1)}, f16[1,64,2304]{2,1,0:T(8,128)(2,1)S(1)}, u32[]{:S(2)}, u32[]{:S(2)}) %collective-permute-start.9) | collective-permute-done | bytes 294944 | tf_op jit(solution)/shard_map/ppermute | solution.py:34
  108.2 16.6 %project.9 = (f32[3,64,2304]{2,1,0:T(8,128)S(1)}, f32[1,3,64,2304]{3,2,1,0:T(8,128)S(1)}) custom-call(s32[1]{0:T(128)} %bitcast.4.chip_ref, bf16[4,2,32,1536]{3,2,1,0:T(8,128)(2,1)} %collective-permute-done.7.refs_0_, bf16[4,2,32,1536]{3,2,1,0:T(8,128)(2,1)} %collective-permute-done.11.refs_1_, bf16[1536,2304]{1,0:T(8,128)(2,1)} %bitcast.173, ...), custom_call_target="tpu_custom_call" | custom-call | flops 1000 | bytes 1000 | tf_op jit(solution)/shard_map/project/pallas_call | solution.py:145
  127.6 4.8 %all-to-all-start.3 = ((bf16[4,2,40,1536]{3,2,1,0:T(8,128)(2,1)}), bf16[4,2,40,1536]{3,2,1,0:T(8,128)(2,1)}, u32[]{:S(2)}, u32[]{:S(2)}) async-start(bf16[4,2,40,1536]{3,2,1,0:T(8,128)(2,1)} %pick_rows.7.refs_5_), calls=%async_computation.3 | async-start | bytes 1966080 | tf_op jit(solution)/shard_map/all_to_all | solution.py:45
  134.1 2.7 collective-permute-start.17
  139.5 12.3 %project.10 = (f32[2,72,2304]{2,1,0:T(8,128)S(1)}, f32[1,2,72,2304]{3,2,1,0:T(8,128)S(1)}) custom-call(s32[1]{0:T(128)} %bitcast.4.chip_ref, bf16[4,2,40,1536]{3,2,1,0:T(8,128)(2,1)} %all-to-all-done.2.refs_0_, bf16[1536,2304]{1,0:T(8,128)(2,1)} %bitcast.174, bf16[1536,2304]{1,0:T(8,128)(2,1)} %collective-permute-done.4.refs_3_.refs_2_.refs_6_.refs_4_, ...), custom_call_target="tpu_custom_call" | custom-call | flops 1000 | bytes 1000 | tf_op jit(solution)/shard_map/project/pallas_call | solution.py:145
  158.1 11.6 %project.11 = (f32[2,72,2304]{2,1,0:T(8,128)S(1)}, f32[1,2,72,2304]{3,2,1,0:T(8,128)S(1)}) custom-call(s32[1]{0:T(128)} %bitcast.4.chip_ref, bf16[4,2,40,1536]{3,2,1,0:T(8,128)(2,1)S(1)} %collective-permute-done.19.refs_0_, bf16[1536,2304]{1,0:T(8,128)(2,1)} %bitcast.175, bf16[1536,2304]{1,0:T(8,128)(2,1)} %collective-permute-done.4.refs_3_.refs_2_.refs_6_.refs_4_, ...), custom_call_target="tpu_custom_call" | custom-call | flops 1000 | bytes 1000 | tf_op jit(solution)/shard_map/project/pallas_call | solution.py:145
  174.0 7.3 %project.12 = (f32[1,72,2304]{2,1,0:T(8,128)S(1)}, f32[1,1,72,2304]{3,2,1,0:T(8,128)S(1)}) custom-call(s32[1]{0:T(128)} %bitcast.4.chip_ref, bf16[4,2,40,1536]{3,2,1,0:T(8,128)(2,1)} %all-to-all-done.3.refs_0_, bf16[1536,2304]{1,0:T(8,128)(2,1)} %bitcast.23.refs_1_.refs_6_, bf16[1536,2304]{1,0:T(8,128)(2,1)} %collective-permute-done.8.refs_2_.refs_7_, ...), custom_call_target="tpu_custom_call" | custom-call | flops 1000 | bytes 1000 | tf_op jit(solution)/shard_map/project/pallas_call | solution.py:145
  181.3 2.2 collective-permute-done.18.refs_3_
  183.5 16.1 %project_back.4 = (bf16[4,2,32,1536]{3,2,1,0:T(8,128)(2,1)S(1)}, bf16[4,2,32,1536]{3,2,1,0:T(8,128)(2,1)S(1)}) custom-call(s32[1]{0:T(128)} %bitcast.4.chip_ref, bf16[2,64,2304]{2,1,0:T(8,128)(2,1)} %multiply_convert_fusion.6.refs_0_, bf16[2,64,2304]{2,1,0:T(8,128)(2,1)} %collective-permute-done.15.refs_1_, ...), custom_call_target="tpu_custom_call" | custom-call | flops 1000 | bytes 1000 | tf_op jit(solution)/shard_map/project_back/pallas_call | solution.py:226
  201.3 7.0 %project.13 = (f32[1,72,2304]{2,1,0:T(8,128)S(1)}, f32[1,1,72,2304]{3,2,1,0:T(8,128)S(1)}) custom-call(s32[1]{0:T(128)} %bitcast.4.chip_ref, bf16[4,2,40,1536]{3,2,1,0:T(8,128)(2,1)S(1)} %collective-permute-done.14.refs_0_, bf16[1536,2304]{1,0:T(8,128)(2,1)} %bitcast.23.refs_1_.refs_6_, bf16[1536,2304]{1,0:T(8,128)(2,1)} %collective-permute-done.8.refs_2_.refs_7_, ...), custom_call_target="tpu_custom_call" | custom-call | flops 1000 | bytes 1000 | tf_op jit(solution)/shard_map/project/pallas_call | solution.py:145
  209.8 2.1 later_grads.1
  211.9 4.8 %collective-permute-done.22 = f16[1,72,2304]{2,1,0:T(8,128)(2,1)S(1)} collective-permute-done((f16[1,72,2304]{2,1,0:T(8,128)(2,1)S(1)}, f16[1,72,2304]{2,1,0:T(8,128)(2,1)S(1)}, u32[]{:S(2)}, u32[]{:S(2)}) %collective-permute-start.22) | collective-permute-done | bytes 331808 | tf_op jit(solution)/shard_map/ppermute | solution.py:34
  222.6 5.2 %all-to-all-start.4 = ((bf16[4,2,32,1536]{3,2,1,0:T(8,128)(2,1)}), bf16[4,2,32,1536]{3,2,1,0:T(8,128)(2,1)S(1)}, u32[]{:S(2)}, u32[]{:S(2)}) async-start(bf16[4,2,32,1536]{3,2,1,0:T(8,128)(2,1)} %add_convert_fusion.1.refs_5_), calls=%async_computation.4 | async-start | bytes 1572864 | tf_op jit(solution)/shard_map/all_to_all | solution.py:45
  227.8 7.6 %collective-permute-done.25.refs_1_ = bf16[2,72,2304]{2,1,0:T(8,128)(2,1)} collective-permute-done((bf16[2,72,2304]{2,1,0:T(8,128)(2,1)S(1)}, bf16[2,72,2304]{2,1,0:T(8,128)(2,1)}, u32[]{:S(2)}, u32[]{:S(2)}) %collective-permute-start.25) | collective-permute-done | bytes 663584 | tf_op jit(solution)/shard_map/ppermute | solution.py:34
  235.4 8.4 %project_back.5.refs_4_ = bf16[4,1,36,1536]{3,2,1,0:T(8,128)(2,1)S(1)} custom-call(s32[1]{0:T(128)} %bitcast.4.chip_ref, bf16[2,72,2304]{2,1,0:T(8,128)(2,1)S(1)} %multiply_convert_fusion.2.refs_0_, bf16[2,72,2304]{2,1,0:T(8,128)(2,1)} %collective-permute-done.25.refs_1_, bf16[1536,2304]{1,0:T(8,128)(2,1)} %bitcast.177, bf16[1536,2304]{1,0:T(8,128)(2,1)} %bitcast.185, ...), custom_call_target="tpu_custom_call" | custom-call | flops 1000 | bytes 1000 | tf_op jit(solution)/shard_map/project_back/pallas_call | solution.py:226
  245.0 8.4 %project_back.6.refs_6_ = bf16[4,1,36,1536]{3,2,1,0:T(8,128)(2,1)S(1)} custom-call(s32[1]{0:T(128)} %bitcast.4.chip_ref, bf16[2,72,2304]{2,1,0:T(8,128)(2,1)S(1)} %multiply_convert_fusion.2.refs_0_, bf16[2,72,2304]{2,1,0:T(8,128)(2,1)} %collective-permute-done.25.refs_1_, bf16[1536,2304]{1,0:T(8,128)(2,1)} %collective-permute-done.4.refs_3_.refs_2_.refs_6_.refs_4_, ...), custom_call_target="tpu_custom_call" | custom-call | flops 1000 | bytes 1000 | tf_op jit(solution)/shard_map/project_back/pallas_call | solution.py:226
  256.4 17.3 %project_back.7 = bf16[4,2,36,1536]{3,2,1,0:T(8,128)(2,1)S(1)} custom-call(s32[1]{0:T(128)} %bitcast.4.chip_ref, bf16[2,72,2304]{2,1,0:T(8,128)(2,1)S(1)} %multiply_convert_fusion.1.refs_0_, bf16[2,72,2304]{2,1,0:T(8,128)(2,1)} %collective-permute-done.24.refs_1_, bf16[1536,2304]{1,0:T(8,128)(2,1)} %bitcast.178, bf16[1536,2304]{1,0:T(8,128)(2,1)} %bitcast.186, ...), custom_call_target="tpu_custom_call" | custom-call | flops 1000 | bytes 1000 | tf_op jit(solution)/shard_map/project_back/pallas_call | solution.py:226
  277.4 5.2 %all-to-all-start.5 = ((bf16[4,2,36,1536]{3,1,2,0:T(2,128)(2,1)}), bf16[4,2,36,1536]{3,1,2,0:T(2,128)(2,1)S(1)}, u32[]{:S(2)}, u32[]{:S(2)}) async-start(bf16[4,2,36,1536]{3,1,2,0:T(2,128)(2,1)} %copy.93), calls=%async_computation.5 | async-start | bytes 1769472 | tf_op jit(solution)/shard_map/all_to_all | solution.py:45
  286.7 3.8 %collective-permute-start.32 = (f32[4,68]{1,0:T(4,128)S(1)}, f32[4,68]{1,0:T(4,128)S(1)}, u32[]{:S(2)}, u32[]{:S(2)}) collective-permute-start(f32[4,68]{1,0:T(4,128)S(1)} %convert_add_fusion), channel_id=1, source_target_pairs={{0,6},{1,7},{2,0},{3,1},{4,2},{5,3},{6,4},{7,5},{8,14},{9,15},{10,... | collective-permute-start | bytes 3272 | tf_op jit(solution)/shard_map/ppermute | solution.py:49
  292.5 5.4 %collective-permute-done.31 = f32[4,68]{1,0:T(4,128)S(1)} collective-permute-done((f32[4,68]{1,0:T(4,128)S(1)}, f32[4,68]{1,0:T(4,128)S(1)}, u32[]{:S(2)}, u32[]{:S(2)}) %collective-permute-start.31) | collective-permute-done | bytes 1120 | tf_op jit(solution)/shard_map/ppermute | solution.py:49
  306.3 3.6 %collective-permute-done.34 = bf16[64,1536]{1,0:T(8,128)(2,1)S(1)} collective-permute-done((bf16[64,1536]{1,0:T(8,128)(2,1)S(1)}, bf16[64,1536]{1,0:T(8,128)(2,1)S(1)}, u32[]{:S(2)}, u32[]{:S(2)}) %collective-permute-start.34) | collective-permute-done | bytes 196640 | tf_op jit(solution)/shard_map/ppermute | solution.py:34
  (224 shorter events, 78.3 us)
Async XLA Ops:
  0.7 29.1 %collective-permute-start.4 = (bf16[1536,2304]{1,0:T(8,128)(2,1)}, bf16[1536,2304]{1,0:T(8,128)(2,1)}, u32[]{:S(2)}, u32[]{:S(2)}) collective-permute-start(bf16[1536,2304]{1,0:T(8,128)(2,1)} %bitcast.171), channel_id=1, source_target_pairs={{0,8},{8,0},{16,24},{24,16},{1,9},{9,1},{17,25},{25,17},{2,10},{10... | collective-permute-start | bytes 21233672 | tf_op jit(solution)/shard_map/ppermute | solution.py:30
  1.2 28.6 %collective-permute-start.5 = (bf16[1536,2304]{1,0:T(8,128)(2,1)}, bf16[1536,2304]{1,0:T(8,128)(2,1)}, u32[]{:S(2)}, u32[]{:S(2)}) collective-permute-start(bf16[1536,2304]{1,0:T(8,128)(2,1)} %bitcast.179), channel_id=1, source_target_pairs={{0,8},{8,0},{16,24},{24,16},{1,9},{9,1},{17,25},{25,17},{2,10},{10... | collective-permute-start | bytes 21233672 | tf_op jit(solution)/shard_map/ppermute | solution.py:30
  3.7 11.3 %collective-permute-start.1 = (f32[64,8]{0,1:T(8,128)S(1)}, f32[64,8]{0,1:T(8,128)S(1)}, u32[]{:S(2)}, u32[]{:S(2)}) collective-permute-start(f32[64,8]{0,1:T(8,128)S(1)} %get-tuple-element.149), channel_id=1, source_target_pairs={{0,16},{8,24},{16,0},{24,8},{1,17},{9,25},{17,1},{25,9},{2,18},{10... | collective-permute-start | bytes 6152 | tf_op jit(solution)/shard_map/ppermute | solution.py:34
  7.4 12.1 %collective-permute-start.2 = (bf16[2,64,1536]{2,1,0:T(8,128)(2,1)S(1)}, bf16[2,64,1536]{2,1,0:T(8,128)(2,1)S(1)}, u32[]{:S(2)}, u32[]{:S(2)}) collective-permute-start(bf16[2,64,1536]{2,1,0:T(8,128)(2,1)S(1)} %bitcast.170), channel_id=1, source_target_pairs={{0,16},{8,24},{16,0},{24,8},{1,17},{9,25},{17,1},{25,9},{2,18},{10... | collective-permute-start | bytes 1179656 | tf_op jit(solution)/shard_map/ppermute | solution.py:34
  11.6 15.1 %collective-permute-start.3 = (bf16[2,64,1536]{2,1,0:T(8,128)(2,1)}, bf16[2,64,1536]{2,1,0:T(8,128)(2,1)S(1)}, u32[]{:S(2)}, u32[]{:S(2)}) collective-permute-start(bf16[2,64,1536]{2,1,0:T(8,128)(2,1)} %bitcast.17), channel_id=1, source_target_pairs={{0,16},{8,24},{16,0},{24,8},{1,17},{9,25},{17,1},{25,9},{2,18},{10... | collective-permute-start | bytes 1179656 | tf_op jit(solution)/shard_map/ppermute | solution.py:34
  31.3 59.0 %collective-permute-start.8 = (bf16[1536,2304]{1,0:T(8,128)(2,1)}, bf16[1536,2304]{1,0:T(8,128)(2,1)}, u32[]{:S(2)}, u32[]{:S(2)}) collective-permute-start(bf16[1536,2304]{1,0:T(8,128)(2,1)} %bitcast.23.refs_1_.refs_6_), channel_id=1, source_target_pairs={{0,8},{8,0},{16,24},{24,16},{1,9},{9,1},{17,25},{25,17},{2,10},{10... | collective-permute-start | bytes 21233672 | tf_op jit(solution)/shard_map/ppermute | solution.py:30
  31.3 25.7 %all-to-all-start = ((bf16[4,2,32,1536]{3,2,1,0:T(8,128)(2,1)}), bf16[4,2,32,1536]{3,2,1,0:T(8,128)(2,1)S(1)}, u32[]{:S(2)}, u32[]{:S(2)}) async-start(bf16[4,2,32,1536]{3,2,1,0:T(8,128)(2,1)} %pick_rows.4.refs_2_), calls=%async_computation | async-start | bytes 1572864 | tf_op jit(solution)/shard_map/all_to_all | solution.py:45
  36.3 24.1 %collective-permute-start = (f32[2,2,128,128]{3,2,1,0:T(8,128)S(1)}, f32[2,2,128,128]{3,2,1,0:T(8,128)S(1)}, u32[]{:S(2)}, u32[]{:S(2)}) collective-permute-start(f32[2,2,128,128]{3,2,1,0:T(8,128)S(1)} %key_value_state.1.refs_2_), channel_id=1, source_target_pairs={{0,16},{8,24},{1,17},{9,25},{2,18},{10,26},{3,19},{11,27},{4,20},{... | collective-permute-start | bytes 786440 | tf_op jit(solution)/shard_map/ppermute | solution.py:40
  56.9 27.8 %all-to-all-start.1 = ((bf16[4,2,32,1536]{3,2,1,0:T(8,128)(2,1)}), bf16[4,2,32,1536]{3,2,1,0:T(8,128)(2,1)S(1)}, u32[]{:S(2)}, u32[]{:S(2)}) async-start(bf16[4,2,32,1536]{3,2,1,0:T(8,128)(2,1)} %pick_rows.5.refs_2_), calls=%async_computation.1 | async-start | bytes 1572864 | tf_op jit(solution)/shard_map/all_to_all | solution.py:45
  61.2 47.1 %collective-permute-start.7 = (bf16[4,2,32,1536]{3,2,1,0:T(8,128)(2,1)S(1)}, bf16[4,2,32,1536]{3,2,1,0:T(8,128)(2,1)}, u32[]{:S(2)}, u32[]{:S(2)}) collective-permute-start(bf16[4,2,32,1536]{3,2,1,0:T(8,128)(2,1)S(1)} %all-to-all-done.refs_0_), channel_id=1, source_target_pairs={{0,1},{1,0},{2,3},{3,2},{4,5},{5,4},{6,7},{7,6},{8,9},{9,8},{10,11... | collective-permute-start | bytes 2359304 | tf_op jit(solution)/shard_map/ppermute | solution.py:55
  74.9 23.4 %collective-permute-start.10 = (f16[2,64,2304]{2,1,0:T(8,128)(2,1)}, f16[2,64,2304]{2,1,0:T(8,128)(2,1)}, u32[]{:S(2)}, u32[]{:S(2)}) collective-permute-start(f16[2,64,2304]{2,1,0:T(8,128)(2,1)} %fusion.8), channel_id=1, source_target_pairs={{0,16},{8,24},{16,0},{24,8},{1,17},{9,25},{17,1},{25,9},{2,18},{10... | collective-permute-start | bytes 1769480 | tf_op jit(solution)/shard_map/ppermute | solution.py:34
  84.8 23.5 %collective-permute-start.11 = (bf16[4,2,32,1536]{3,2,1,0:T(8,128)(2,1)S(1)}, bf16[4,2,32,1536]{3,2,1,0:T(8,128)(2,1)}, u32[]{:S(2)}, u32[]{:S(2)}) collective-permute-start(bf16[4,2,32,1536]{3,2,1,0:T(8,128)(2,1)S(1)} %all-to-all-done.1.refs_0_), channel_id=1, source_target_pairs={{0,1},{1,0},{2,3},{3,2},{4,5},{5,4},{6,7},{7,6},{8,9},{9,8},{10,11... | collective-permute-start | bytes 2359304 | tf_op jit(solution)/shard_map/ppermute | solution.py:55
  85.3 42.3 %all-to-all-start.2 = ((bf16[4,2,40,1536]{3,2,1,0:T(8,128)(2,1)}), bf16[4,2,40,1536]{3,2,1,0:T(8,128)(2,1)}, u32[]{:S(2)}, u32[]{:S(2)}) async-start(bf16[4,2,40,1536]{3,2,1,0:T(8,128)(2,1)} %pick_rows.6.refs_2_), calls=%async_computation.2 | async-start | bytes 1966080 | tf_op jit(solution)/shard_map/all_to_all | solution.py:45
  107.1 32.4 %collective-permute-start.15 = (bf16[2,64,2304]{2,1,0:T(8,128)(2,1)}, bf16[2,64,2304]{2,1,0:T(8,128)(2,1)}, u32[]{:S(2)}, u32[]{:S(2)}) collective-permute-start(bf16[2,64,2304]{2,1,0:T(8,128)(2,1)} %multiply_convert_fusion.6.refs_0_), channel_id=1, source_target_pairs={{0,16},{8,24},{16,0},{24,8},{1,17},{9,25},{17,1},{25,9},{2,18},{10... | collective-permute-start | bytes 1769480 | tf_op jit(solution)/shard_map/ppermute | solution.py:34
  126.1 12.2 %collective-permute-start.12 = (f32[2,2,128,128]{3,2,1,0:T(8,128)}, f32[2,2,128,128]{3,2,1,0:T(8,128)S(1)}, u32[]{:S(2)}, u32[]{:S(2)}) collective-permute-start(f32[2,2,128,128]{3,2,1,0:T(8,128)} %get-tuple-element.76), channel_id=1, source_target_pairs={{16,0},{24,8},{17,1},{25,9},{18,2},{26,10},{19,3},{27,11},{20,4},{... | collective-permute-start | bytes 786440 | tf_op jit(solution)/shard_map/ppermute | solution.py:40
  127.6 43.2 %all-to-all-start.3 = ((bf16[4,2,40,1536]{3,2,1,0:T(8,128)(2,1)}), bf16[4,2,40,1536]{3,2,1,0:T(8,128)(2,1)}, u32[]{:S(2)}, u32[]{:S(2)}) async-start(bf16[4,2,40,1536]{3,2,1,0:T(8,128)(2,1)} %pick_rows.7.refs_5_), calls=%async_computation.3 | async-start | bytes 1966080 | tf_op jit(solution)/shard_map/all_to_all | solution.py:45
  134.1 20.2 %collective-permute-start.17 = (f16[3,64,2304]{2,1,0:T(8,128)(2,1)S(1)}, f16[3,64,2304]{2,1,0:T(8,128)(2,1)S(1)}, u32[]{:S(2)}, u32[]{:S(2)}) collective-permute-start(f16[3,64,2304]{2,1,0:T(8,128)(2,1)S(1)} %fusion.1), channel_id=1, source_target_pairs={{0,16},{8,24},{16,0},{24,8},{1,17},{9,25},{17,1},{25,9},{2,18},{10... | collective-permute-start | bytes 2654216 | tf_op jit(solution)/shard_map/ppermute | solution.py:34
  136.8 21.3 %collective-permute-start.19 = (bf16[4,2,40,1536]{3,2,1,0:T(8,128)(2,1)}, bf16[4,2,40,1536]{3,2,1,0:T(8,128)(2,1)S(1)}, u32[]{:S(2)}, u32[]{:S(2)}) collective-permute-start(bf16[4,2,40,1536]{3,2,1,0:T(8,128)(2,1)} %all-to-all-done.2.refs_0_), channel_id=1, source_target_pairs={{0,1},{1,0},{2,3},{3,2},{4,5},{5,4},{6,7},{7,6},{8,9},{9,8},{10,11... | collective-permute-start | bytes 2949128 | tf_op jit(solution)/shard_map/ppermute | solution.py:55
  139.4 13.5 %collective-permute-start.13 = (f32[2,2,2,128,128]{4,3,2,1,0:T(8,128)S(1)}, f32[2,2,2,128,128]{4,3,2,1,0:T(8,128)S(1)}, u32[]{:S(2)}, u32[]{:S(2)}) collective-permute-start(f32[2,2,2,128,128]{4,3,2,1,0:T(8,128)S(1)} %pad_maximum_fusion.1), channel_id=1, source_target_pairs={{0,8},{8,0},{16,24},{24,16},{1,9},{9,1},{17,25},{25,17},{2,10},{10... | collective-permute-start | bytes 1572872 | tf_op jit(solution)/shard_map/ppermute | solution.py:30
  152.8 48.5 %collective-permute-start.16 = (f16[2,72,2304]{2,1,0:T(8,128)(2,1)}, f16[2,72,2304]{2,1,0:T(8,128)(2,1)}, u32[]{:S(2)}, u32[]{:S(2)}) collective-permute-start(f16[2,72,2304]{2,1,0:T(8,128)(2,1)} %fusion.2), channel_id=1, source_target_pairs={{0,16},{8,24},{16,0},{24,8},{1,17},{9,25},{17,1},{25,9},{2,18},{10... | collective-permute-start | bytes 1990664 | tf_op jit(solution)/shard_map/ppermute | solution.py:34
  156.1 27.4 %collective-permute-start.18 = (bf16[2,64,2304]{2,1,0:T(8,128)(2,1)}, bf16[2,64,2304]{2,1,0:T(8,128)(2,1)}, u32[]{:S(2)}, u32[]{:S(2)}) collective-permute-start(bf16[2,64,2304]{2,1,0:T(8,128)(2,1)} %multiply_convert_fusion.5.refs_2_), channel_id=1, source_target_pairs={{0,16},{8,24},{16,0},{24,8},{1,17},{9,25},{17,1},{25,9},{2,18},{10... | collective-permute-start | bytes 1769480 | tf_op jit(solution)/shard_map/ppermute | solution.py:34
  170.7 30.6 %collective-permute-start.14 = (bf16[4,2,40,1536]{3,2,1,0:T(8,128)(2,1)}, bf16[4,2,40,1536]{3,2,1,0:T(8,128)(2,1)S(1)}, u32[]{:S(2)}, u32[]{:S(2)}) collective-permute-start(bf16[4,2,40,1536]{3,2,1,0:T(8,128)(2,1)} %all-to-all-done.3.refs_0_), channel_id=1, source_target_pairs={{0,1},{1,0},{2,3},{3,2},{4,5},{5,4},{6,7},{7,6},{8,9},{9,8},{10,11... | collective-permute-start | bytes 2949128 | tf_op jit(solution)/shard_map/ppermute | solution.py:55
  173.8 35.8 %collective-permute-start.23 = (f16[2,72,2304]{2,1,0:T(8,128)(2,1)S(1)}, f16[2,72,2304]{2,1,0:T(8,128)(2,1)S(1)}, u32[]{:S(2)}, u32[]{:S(2)}) collective-permute-start(f16[2,72,2304]{2,1,0:T(8,128)(2,1)S(1)} %fusion.3), channel_id=1, source_target_pairs={{0,16},{8,24},{16,0},{24,8},{1,17},{9,25},{17,1},{25,9},{2,18},{10... | collective-permute-start | bytes 1990664 | tf_op jit(solution)/shard_map/ppermute | solution.py:34
  199.6 21.9 %collective-permute-start.20 = (bf16[4,2,32,1536]{3,2,1,0:T(8,128)(2,1)S(1)}, bf16[4,2,32,1536]{3,2,1,0:T(8,128)(2,1)S(1)}, u32[]{:S(2)}, u32[]{:S(2)}) collective-permute-start(bf16[4,2,32,1536]{3,2,1,0:T(8,128)(2,1)S(1)} %get-tuple-element.92), channel_id=1, source_target_pairs={{0,1},{1,0},{2,3},{3,2},{4,5},{5,4},{6,7},{7,6},{8,9},{9,8},{10,11... | collective-permute-start | bytes 2359304 | tf_op jit(solution)/shard_map/ppermute | solution.py:55
  200.3 19.7 %collective-permute-start.21 = (f16[1,72,2304]{2,1,0:T(8,128)(2,1)S(1)}, f16[1,72,2304]{2,1,0:T(8,128)(2,1)S(1)}, u32[]{:S(2)}, u32[]{:S(2)}) collective-permute-start(f16[1,72,2304]{2,1,0:T(8,128)(2,1)S(1)} %fusion.12), channel_id=1, source_target_pairs={{0,16},{8,24},{16,0},{24,8},{1,17},{9,25},{17,1},{25,9},{2,18},{10... | collective-permute-start | bytes 995336 | tf_op jit(solution)/shard_map/ppermute | solution.py:34
  217.4 18.0 %collective-permute-start.25 = (bf16[2,72,2304]{2,1,0:T(8,128)(2,1)S(1)}, bf16[2,72,2304]{2,1,0:T(8,128)(2,1)}, u32[]{:S(2)}, u32[]{:S(2)}) collective-permute-start(bf16[2,72,2304]{2,1,0:T(8,128)(2,1)S(1)} %multiply_convert_fusion.2.refs_0_), channel_id=1, source_target_pairs={{0,16},{8,24},{16,0},{24,8},{1,17},{9,25},{17,1},{25,9},{2,18},{10... | collective-permute-start | bytes 1990664 | tf_op jit(solution)/shard_map/ppermute | solution.py:34
  220.7 35.7 %collective-permute-start.24 = (bf16[2,72,2304]{2,1,0:T(8,128)(2,1)S(1)}, bf16[2,72,2304]{2,1,0:T(8,128)(2,1)}, u32[]{:S(2)}, u32[]{:S(2)}) collective-permute-start(bf16[2,72,2304]{2,1,0:T(8,128)(2,1)S(1)} %multiply_convert_fusion.1.refs_0_), channel_id=1, source_target_pairs={{0,16},{8,24},{16,0},{24,8},{1,17},{9,25},{17,1},{25,9},{2,18},{10... | collective-permute-start | bytes 1990664 | tf_op jit(solution)/shard_map/ppermute | solution.py:34
  222.6 53.2 %all-to-all-start.4 = ((bf16[4,2,32,1536]{3,2,1,0:T(8,128)(2,1)}), bf16[4,2,32,1536]{3,2,1,0:T(8,128)(2,1)S(1)}, u32[]{:S(2)}, u32[]{:S(2)}) async-start(bf16[4,2,32,1536]{3,2,1,0:T(8,128)(2,1)} %add_convert_fusion.1.refs_5_), calls=%async_computation.4 | async-start | bytes 1572864 | tf_op jit(solution)/shard_map/all_to_all | solution.py:45
  243.8 30.4 %collective-permute-start.26 = (bf16[4,1,36,1536]{3,2,1,0:T(8,128)(2,1)S(1)}, bf16[4,1,36,1536]{3,2,1,0:T(8,128)(2,1)}, u32[]{:S(2)}, u32[]{:S(2)}) collective-permute-start(bf16[4,1,36,1536]{3,2,1,0:T(8,128)(2,1)S(1)} %project_back.5.refs_4_), channel_id=1, source_target_pairs={{0,1},{1,0},{2,3},{3,2},{4,5},{5,4},{6,7},{7,6},{8,9},{9,8},{10,11... | collective-permute-start | bytes 1327112 | tf_op jit(solution)/shard_map/ppermute | solution.py:55
  253.5 20.8 %collective-permute-start.27 = (bf16[4,1,36,1536]{3,2,1,0:T(8,128)(2,1)S(1)}, bf16[4,1,36,1536]{3,2,1,0:T(8,128)(2,1)}, u32[]{:S(2)}, u32[]{:S(2)}) collective-permute-start(bf16[4,1,36,1536]{3,2,1,0:T(8,128)(2,1)S(1)} %project_back.6.refs_6_), channel_id=1, source_target_pairs={{0,1},{1,0},{2,3},{3,2},{4,5},{5,4},{6,7},{7,6},{8,9},{9,8},{10,11... | collective-permute-start | bytes 1327112 | tf_op jit(solution)/shard_map/ppermute | solution.py:55
  255.0 18.6 %collective-permute-start.28 = (bf16[272]{0:T(512)(128)(2,1)S(1)}, bf16[272]{0:T(512)(128)(2,1)S(1)}, u32[]{:S(2)}, u32[]{:S(2)}) collective-permute-start(bf16[272]{0:T(512)(128)(2,1)S(1)} %pad_maximum_fusion.5), channel_id=1, source_target_pairs={{0,16},{8,24},{16,0},{24,8},{1,17},{9,25},{17,1},{25,9},{2,18},{10... | collective-permute-start | bytes 1640 | tf_op jit(solution)/shard_map/ppermute | solution.py:34
  277.4 21.1 %all-to-all-start.5 = ((bf16[4,2,36,1536]{3,1,2,0:T(2,128)(2,1)}), bf16[4,2,36,1536]{3,1,2,0:T(2,128)(2,1)S(1)}, u32[]{:S(2)}, u32[]{:S(2)}) async-start(bf16[4,2,36,1536]{3,1,2,0:T(2,128)(2,1)} %copy.93), calls=%async_computation.5 | async-start | bytes 1769472 | tf_op jit(solution)/shard_map/all_to_all | solution.py:45
  (42 other events, 201.0 us)
